TPU v7x, 256 devices: a whole 4x4x8 slice. The times are simulated.
256 devices in a mesh: row: 32 (over x, y, core), col: 8 (over z).
Axes of the slice: x: 4, y: 4, z: 8, core: 2. Of those that a mesh axis runs over, the one named last changes fastest.
Arguments:
- inputs: bfloat16 [768, 12288], P('row', 'col'), may hold values from -6 to 6
- w_in: bfloat16 [12288, 24576], P('col', 'row'), may hold values from -0.0546875 to 0.0546875
- w_out: bfloat16 [24576, 12288], P('row', 'col'), may hold values from -0.0390625 to 0.0390625
- out_grad: bfloat16 [768, 12288], P('row', 'col'), may hold values from -6 to 6
Outputs:
- output: bfloat16 [768, 12288], P('row', 'col')
- input_grad: bfloat16 [768, 12288], P('row', 'col')
- grad_in_w: bfloat16 [12288, 24576], P('col', 'row')
- grad_out_w: bfloat16 [24576, 12288], P('row', 'col')
All inputs are finite; a program needn't handle non-finite values.
Results may differ from a plain program's by a relative error of at most 0.0049.
Values may be sent and summed in bfloat16 or wider, within the bound.
No kernel may reach another device: no remote copies, remote signals or barrier semaphores. Data moves between devices by JAX's collectives and lax.ppermute only.
A program may use at most 128 MiB of HBM per device.

v0:
```python
import jax
import jax.numpy as jnp
from jax import lax
from jax.sharding import PartitionSpec as P

gelu_scale = 0.7978845608028654
gelu_cubic = 0.044715


def gelu_parts(hidden):
    inner = gelu_scale * (hidden + gelu_cubic * hidden * hidden * hidden)
    tangent = jnp.tanh(inner)
    value = 0.5 * hidden * (1.0 + tangent)
    slopes = 0.5 * (1.0 + tangent) + 0.5 * hidden * (1.0 - tangent * tangent) * gelu_scale * (
        1.0 + 3.0 * gelu_cubic * hidden * hidden
    )
    return (value, slopes)


def contract_first(left, right):
    return lax.dot_general(
        left, right, (((0,), (0,)), ((), ())), preferred_element_type=jnp.float32
    )


def contract_last(left, right):
    return lax.dot_general(
        left, right, (((1,), (1,)), ((), ())), preferred_element_type=jnp.float32
    )


def local(inputs, w_in, w_out, out_grad):
    all_inputs, all_grads = (
        lax.all_gather(inputs, "row", axis=0, tiled=True),
        lax.all_gather(out_grad, "row", axis=0, tiled=True),
    )
    hidden_part = jnp.dot(all_inputs, w_in, preferred_element_type=jnp.float32)
    act_part = contract_last(all_grads, w_out)
    hidden = lax.psum(hidden_part, "col")
    value, slopes = gelu_parts(hidden)
    activation = value.astype(jnp.bfloat16)
    act_grad = lax.psum(act_part, "col")
    hid_grad = (act_grad * slopes).astype(jnp.bfloat16)
    grad_out_w = contract_first(activation, all_grads).astype(jnp.bfloat16)
    grad_in_w = contract_first(all_inputs, hid_grad).astype(jnp.bfloat16)
    picked = activation
    output = lax.psum_scatter(
        jnp.dot(picked, w_out, preferred_element_type=jnp.float32),
        "row",
        scatter_dimension=0,
        tiled=True,
    )
    picked = hid_grad
    input_grad = lax.psum_scatter(
        contract_last(picked, w_in), "row", scatter_dimension=0, tiled=True
    )
    return (output.astype(jnp.bfloat16), input_grad.astype(jnp.bfloat16), grad_in_w, grad_out_w)


def solution(mesh):
    placed = (P("row", "col"), P("col", "row"), P("row", "col"), P("row", "col"))
    return jax.shard_map(
        local,
        mesh=mesh,
        in_specs=placed,
        out_specs=(P("row", "col"), P("row", "col"), P("col", "row"), P("row", "col")),
        check_vma=False,
    )
```

profile of v0, /device:TPU:1, one launch (start us, length us, event | category | flops | bytes accessed | tf_op | source)
XLA Modules:
  0.0 437.0 jit_solution(65639151080491937)
XLA Ops:
  7.2 0.0 all-gather.5.cloned.1.call-start
  7.2 0.7 all-gather.5.cloned.1.call-update
  7.9 0.0 all-gather.3.cloned.1.call-start
  8.0 0.7 all-gather.3.cloned.1.call-update
  8.7 0.0 all-reduce.3.cloned.1.call-start
  8.7 55.3 %all-gather.5.cloned.1.call-done = bf16[768,1536]{1,0:T(8,128)(2,1)} async-done(((bf16[24,1536]{1,0:T(8,128)(2,1)}), bf16[768,1536]{1,0:T(8,128)(2,1)}) %all-gather.5.cloned.1.call-update) | async-done | bytes 2359312 | tf_op jit(solution)/shard_map/all_gather | solution.py:35
  64.1 5.1 %fusion.10 = f32[768,768]{1,0:T(8,128)} fusion(bf16[768,1536]{1,0:T(8,128)(2,1)} %all-gather.5.cloned.1.call-done, bf16[768,1536]{1,0:T(8,128)(2,1)S(1)} %copy-done), kind=kOutput, calls=%fused_computation.15 | convolution fusion | flops 1811939328 | bytes 7077888 | tf_op jit(solution)/shard_map/dot_general | solution.py:27
  69.2 46.1 %all-gather.3.cloned.1.call-done = bf16[768,1536]{1,0:T(8,128)(2,1)} async-done(((bf16[24,1536]{1,0:T(8,128)(2,1)}), bf16[768,1536]{1,0:T(8,128)(2,1)}) %all-gather.3.cloned.1.call-update) | async-done | bytes 2359312 | tf_op jit(solution)/shard_map/all_gather | solution.py:34
  115.3 5.8 %fusion.9 = f32[768,768]{1,0:T(8,128)} fusion(bf16[768,1536]{1,0:T(8,128)(2,1)} %all-gather.3.cloned.1.call-done, bf16[1536,768]{1,0:T(8,128)(2,1)} %param.5), kind=kOutput, calls=%fused_computation.14 | convolution fusion | flops 1811939328 | bytes 7077888 | tf_op jit(solution)/shard_map/dot_general | solution.py:37
  121.1 0.0 all-reduce.3.cloned.1.call-update
  121.1 0.0 reduce-scatter.3.cloned.1.call-start
  121.1 118.3 %all-reduce.3.cloned.1.call-done = (f32[768,768]{1,0:T(8,128)}, f32[768,768]{1,0:T(8,128)}) async-done(((f32[768,768]{1,0:T(8,128)}, f32[768,768]{1,0:T(8,128)}), (f32[768,768]{1,0:T(8,128)}, f32[768,768]{1,0:T(8,128)})) %all-reduce.3.cloned.1.call-update) | async-done | bytes 4718608 | tf_op jit(solution)/shard_map/psum | solution.py:39
  239.4 6.0 %fusion.8 = f32[768,1536]{1,0:T(8,128)} fusion(bf16[768,1536]{1,0:T(8,128)(2,1)S(1)} %copy-done, f32[768,768]{1,0:T(8,128)} %get-tuple-element.8), kind=kOutput, calls=%fused_computation.13 | convolution fusion | flops 1817247744 | bytes 9437184 | tf_op jit(solution)/shard_map/dot_general | solution.py:48
  245.4 0.0 reduce-scatter.3.cloned.1.call-update
  245.4 0.0 reduce-scatter.5.cloned.1.call-start
  245.5 4.0 fusion.7
  249.5 4.2 fusion.11
  253.8 5.2 %fusion = bf16[1536,768]{0,1:T(8,128)(2,1)} fusion(bf16[768,768]{1,0:T(8,128)(2,1)S(1)} %fusion.7, bf16[768,1536]{1,0:T(8,128)(2,1)} %all-gather.3.cloned.1.call-done), kind=kOutput, calls=%fused_computation.4 | convolution fusion | flops 1813118976 | bytes 5898240 | tf_op jit(solution)/shard_map/dot_general | solution.py:21
  258.9 4.3 copy.8
  263.2 6.1 %convolution_convert_fusion = bf16[768,1536]{1,0:T(8,128)(2,1)} fusion(bf16[768,1536]{1,0:T(8,128)(2,1)} %all-gather.5.cloned.1.call-done, f32[768,768]{1,0:T(8,128)} %get-tuple-element.8), kind=kOutput, calls=%fused_computation.2 | convolution fusion | flops 1818427392 | bytes 7077888 | tf_op jit(solution)/shard_map/dot_general | solution.py:21
  269.3 64.6 %reduce-scatter.3.cloned.1.call-done = f32[24,1536]{1,0:T(8,128)} async-done(((f32[768,1536]{1,0:T(8,128)}), f32[24,1536]{1,0:T(8,128)}) %reduce-scatter.3.cloned.1.call-update) | async-done | bytes 147472 | tf_op jit(solution)/shard_map/reduce_scatter | solution.py:47
  333.9 1.6 convert_element_type.22
  335.4 93.5 %reduce-scatter.5.cloned.1.call-done = f32[24,1536]{1,0:T(8,128)} async-done(((f32[768,1536]{1,0:T(8,128)}), f32[24,1536]{1,0:T(8,128)}) %reduce-scatter.5.cloned.1.call-update) | async-done | bytes 147472 | tf_op jit(solution)/shard_map/reduce_scatter | solution.py:54
  428.9 1.6 convert_element_type.24
  (5 shorter events, 0.0 us)
Async XLA Ops:
  7.2 56.9 %copy-start = (bf16[768,1536]{1,0:T(8,128)(2,1)S(1)}, bf16[768,1536]{1,0:T(8,128)(2,1)}, u32[]{:S(2)}) copy-start(bf16[768,1536]{1,0:T(8,128)(2,1)} %param.6) | copy-start | bytes 7077892
  7.2 56.9 %all-gather.5.cloned.1.call-start = ((), (), s32[]{:S(2)}) async-start(), calls=%async_computation.4 | async-start | bytes 2433024 | tf_op jit(solution)/shard_map/all_gather | solution.py:35
  7.9 107.4 %all-gather.3.cloned.1.call-start = ((), (), s32[]{:S(2)}) async-start(), calls=%async_computation.2 | async-start | bytes 2433024 | tf_op jit(solution)/shard_map/all_gather | solution.py:34
  8.7 230.8 %all-reduce.3.cloned.1.call-start = ((), (), s32[]{:S(2)}) async-start(), calls=%async_computation.6 | async-start | bytes 9437184 | tf_op jit(solution)/shard_map/psum | solution.py:39
  121.1 212.8 %reduce-scatter.3.cloned.1.call-start = ((), (), s32[]{:S(2)}) async-start(), calls=%async_computation.3 | async-start | bytes 4866048 | tf_op jit(solution)/shard_map/reduce_scatter | solution.py:47
  245.4 183.5 %reduce-scatter.5.cloned.1.call-start = ((), (), s32[]{:S(2)}) async-start(), calls=%async_computation.5 | async-start | bytes 4866048 | tf_op jit(solution)/shard_map/reduce_scatter | solution.py:54
  245.5 4.0 copy-start.1
Sparse Core Ops, SparseCore 0:
  10.6 53.4 all-gather.4
  66.6 48.6 all-gather.2
  121.2 118.1 all-reduce.2
  245.6 88.2 reduce-scatter.2
  338.3 90.6 reduce-scatter.4
where the time goes:
time: 438 us; the launch traced here: 437 us
  waiting for transfers between devices  379 us (87%)
  matrix products  32.3 us (7%)
  between operations  13.8 us (3%)
  other arithmetic  7.11 us (2%)
    psum x1, waiting for transfers between devices, local(): hidden = lax.psum(hidden_part, 'col')  118 us
    reduce_scatter x1, waiting for transfers between devices, local(): lax.psum_scatter(contract_last(picked, w_in), 'row', scatter_dimension=0,...  93.5 us
    reduce_scatter x1, waiting for transfers between devices, local(): lax.psum_scatter(jnp.dot(picked, w_out, preferred_element_type=jnp.float3...  64.6 us
    all_gather x1, waiting for transfers between devices, local(): lax.all_gather(out_grad, 'row', axis=0, tiled=True)  55.3 us
    all_gather x1, waiting for transfers between devices, local(): lax.all_gather(inputs, 'row', axis=0, tiled=True)  46.1 us
    dot_general x2, matrix products, contract_first(): lax.dot_general(left, right, (((0,), (0,)), ((), ())), preferred_element_...  11.2 us
    dot_general x2, matrix products, contract_last(): lax.dot_general(left, right, (((1,), (1,)), ((), ())), preferred_element_...  9.31 us
  transfers between devices with their start and end apart: 5, of which 5 were waited for; matrix products, arithmetic and copies ran while one was open for 7% of the time, Pallas kernels for 0%

commit v1 on v0

v1 whole, which is shorter than its diff:
```python
import functools

import jax
import jax.numpy as jnp
from jax import lax
from jax.experimental import pallas as pl
from jax.experimental.pallas import tpu as pltpu
from jax.sharding import PartitionSpec as P

gelu_scale = 0.7978845608028654
gelu_cubic = 0.044715
f32 = jnp.float32
bf16 = jnp.bfloat16
side = 4
ring = 8
tile = 256
steps = (1, -1, 2)


def gelu_parts(hidden):
    inner = gelu_scale * (hidden + gelu_cubic * hidden * hidden * hidden)
    tangent = jnp.tanh(inner)
    value = 0.5 * hidden * (1.0 + tangent)
    slopes = 0.5 * (1.0 + tangent) + 0.5 * hidden * (1.0 - tangent * tangent) * gelu_scale * (
        1.0 + 3.0 * gelu_cubic * hidden * hidden
    )
    return (value, slopes)


def coded(array):
    array = array * 2.0**30
    return (array * array * array).astype(bf16)


def decoded(array):
    array = array.astype(f32)
    return jnp.sign(array) * jnp.exp2(jnp.log2(jnp.abs(array)) * (1.0 / 3.0) - 30.0)


def place(x, y, core):
    return ((x % side) * side + y % side) * 2 + core


def swap_cores(array):
    return lax.ppermute(
        array, "row", [(place(0, 0, 0) + r, (place(0, 0, 0) + r) ^ 1) for r in range(32)]
    )


def first_axis(array, by):
    pairs = []
    for x in range(side):
        for y in range(side):
            pairs.append((place(x, y, 0), place(x + by, y, 0)))
            pairs.append((place(x, y, 1), place(x, y + by, 1)))
    return lax.ppermute(array, "row", pairs)


def second_axis(array, by):
    pairs = []
    for x in range(side):
        for y in range(side):
            pairs.append((place(x, y, 0), place(x, y + by, 0)))
            pairs.append((place(x, y, 1), place(x + by, y, 1)))
    return lax.ppermute(array, "row", pairs)


def along_z(array, by):
    return lax.ppermute(array, "col", [(z, (z + by) % ring) for z in range(ring)])


def slot(at, outer, inner):
    core, me = at[0], at[1]
    spot = jnp.where(core == 0, inner * side + outer, outer * side + inner)
    return lax.rem(spot // 2 + ring - me, ring), lax.rem(spot, 2)


def first_kernel(at, a0, a1, a2, a3, in_own, in_par, out_own, out_par, h_ref, g_ref, held):
    step = pl.program_id(0)
    core = at[0]

    @pl.when(step == 0)
    def _():
        for outer, ref in enumerate((a0, a1, a2, a3)):
            for inner in range(side):
                chunk, half = slot(at, outer, inner)
                block = ref[pl.ds(inner * 48, 48), :]
                g_ref[chunk, half] = block
                held[chunk, half] = block

    def plain(w):
        a = held[...].reshape(768, 1536)
        h_ref[...] = jnp.dot(a, w[...], preferred_element_type=f32).reshape(h_ref.shape)

    def turned(w):
        a = held[...].reshape(768, 1536)
        h_ref[...] = lax.dot_general(
            a, w[...], (((1,), (1,)), ((), ())), preferred_element_type=f32
        ).reshape(h_ref.shape)

    pl.when((core == 0) & (step < 3))(lambda: plain(in_own))
    pl.when((core == 0) & (step >= 3))(lambda: plain(in_par))
    pl.when((core == 1) & (step < 3))(lambda: turned(out_par))
    pl.when((core == 1) & (step >= 3))(lambda: turned(out_own))


def first_product(at, blocks, in_own, in_par, out_own, out_par):
    whole = pl.BlockSpec((192, 1536), lambda j, at: (0, 0))
    early = lambda j: jnp.minimum(j, 2)
    late = lambda j: jnp.maximum(j - 3, 0)
    return pl.pallas_call(
        first_kernel,
        grid_spec=pltpu.PrefetchScalarGridSpec(
            num_scalar_prefetch=1,
            grid=(6,),
            in_specs=[whole] * 4
            + [
                pl.BlockSpec((1536, tile), lambda j, at: (0, jnp.where(at[0] == 0, early(j), 0))),
                pl.BlockSpec((1536, tile), lambda j, at: (0, jnp.where(at[0] == 0, late(j), 0))),
                pl.BlockSpec((tile, 1536), lambda j, at: (jnp.where(at[0] == 1, late(j), 0), 0)),
                pl.BlockSpec((tile, 1536), lambda j, at: (jnp.where(at[0] == 1, early(j), 0), 0)),
            ],
            out_specs=[
                pl.BlockSpec((ring, 2, 48, tile), lambda j, at: (0, 0, 0, j)),
                pl.BlockSpec((ring, 2, 48, 1536), lambda j, at: (0, 0, 0, 0)),
            ],
            scratch_shapes=[pltpu.VMEM((ring, 2, 48, 1536), bf16)],
        ),
        out_shape=[
            jax.ShapeDtypeStruct((ring, 2, 48, 1536), f32),
            jax.ShapeDtypeStruct((ring, 2, 48, 1536), bf16),
        ],
        compiler_params=pltpu.CompilerParams(vmem_limit_bytes=40 << 20),
        cost_estimate=pl.CostEstimate(
            flops=2 * 768 * 1536 * 1536, bytes_accessed=12 << 20, transcendentals=0
        ),
    )(at, *blocks, in_own, in_par, out_own, out_par)


def second_kernel(at, *refs):
    chunks, (in_own, in_par, out_own, out_par, o_ref, held, made) = refs[:ring], refs[ring:]
    step = pl.program_id(0)
    core, me = at[0], at[1]

    @pl.when(step == 0)
    def _():
        for i, ref in enumerate(chunks):
            held[i] = ref[...]

    def plain(w0, w1):
        b = held[...].reshape(768, 1536)
        made[...] = (
            jnp.dot(b[:, :768], w0[...], preferred_element_type=f32)
            + jnp.dot(b[:, 768:], w1[...], preferred_element_type=f32)
        ).astype(bf16).reshape(made.shape)

    def turned(w0, w1):
        b = held[...].reshape(768, 1536)
        last = (((1,), (1,)), ((), ()))
        made[...] = (
            lax.dot_general(b[:, :768], w0[...], last, preferred_element_type=f32)
            + lax.dot_general(b[:, 768:], w1[...], last, preferred_element_type=f32)
        ).astype(bf16).reshape(made.shape)

    pl.when(core == 0)(lambda: plain(out_own, out_par))
    pl.when(core == 1)(lambda: turned(in_par, in_own))
    for outer in range(side):
        for inner in range(side):
            chunk, half = slot(at, outer, inner)
            o_ref[outer, inner] = made[chunk, half]


def second_product(at, chunks, in_own, in_par, out_own, out_par):
    whole = pl.BlockSpec((96, 1536), lambda j, at: (0, 0))
    on_in = pl.BlockSpec((tile, 768), lambda j, at: (jnp.where(at[0] == 1, j, 0), 0))
    on_out = pl.BlockSpec((768, tile), lambda j, at: (0, jnp.where(at[0] == 0, j, 0)))
    return pl.pallas_call(
        second_kernel,
        grid_spec=pltpu.PrefetchScalarGridSpec(
            num_scalar_prefetch=1,
            grid=(6,),
            in_specs=[whole] * ring + [on_in, on_in, on_out, on_out],
            out_specs=pl.BlockSpec((side, side, 48, tile), lambda j, at: (0, 0, 0, j)),
            scratch_shapes=[
                pltpu.VMEM((ring, 96, 1536), bf16),
                pltpu.VMEM((ring, 2, 48, tile), bf16),
            ],
        ),
        out_shape=jax.ShapeDtypeStruct((side, side, 48, 1536), bf16),
        compiler_params=pltpu.CompilerParams(vmem_limit_bytes=40 << 20),
        cost_estimate=pl.CostEstimate(
            flops=2 * 768 * 1536 * 1536, bytes_accessed=12 << 20, transcendentals=0
        ),
    )(at, *chunks, in_own, in_par, out_own, out_par)


def grad_kernel(at, a_own, a_oth, b_own, b_oth, gin_ref, gout_ref):
    core = at[0]
    first = (((0,), (0,)), ((), ()))

    def both(x, g, act, hid):
        gout_ref[...] = lax.dot_general(act[...], g[...], first, preferred_element_type=f32).astype(
            bf16
        )
        gin_ref[...] = lax.dot_general(x[...], hid[...], first, preferred_element_type=f32).astype(
            bf16
        )

    pl.when(core == 0)(lambda: both(a_own, a_oth, b_own, b_oth))
    pl.when(core == 1)(lambda: both(a_oth, a_own, b_oth, b_own))


def weight_grads(at, a_own, a_oth, b_own, b_oth):
    part = pl.BlockSpec((768, tile), lambda j, at: (0, j))
    whole = pl.BlockSpec((768, 768), lambda j, at: (0, 0))
    return pl.pallas_call(
        grad_kernel,
        grid_spec=pltpu.PrefetchScalarGridSpec(
            num_scalar_prefetch=1,
            grid=(6,),
            in_specs=[part, part, whole, whole],
            out_specs=[
                pl.BlockSpec((tile, 768), lambda j, at: (j, 0)),
                pl.BlockSpec((768, tile), lambda j, at: (0, j)),
            ],
        ),
        out_shape=[
            jax.ShapeDtypeStruct((1536, 768), bf16),
            jax.ShapeDtypeStruct((768, 1536), bf16),
        ],
        compiler_params=pltpu.CompilerParams(vmem_limit_bytes=40 << 20),
        cost_estimate=pl.CostEstimate(
            flops=4 * 768 * 768 * 1536, bytes_accessed=12 << 20, transcendentals=0
        ),
    )(at, a_own, a_oth, b_own, b_oth)


def local(inputs, w_in, w_out, out_grad):
    core = lax.axis_index("row") % 2
    me = lax.axis_index("col")
    at = jnp.stack([core, me]).astype(jnp.int32)
    fore = core == 0

    got = swap_cores(jnp.where(fore, out_grad, inputs))
    mine = jnp.where(fore, inputs, out_grad)
    pair = jnp.concatenate([jnp.where(fore, mine, got), jnp.where(fore, got, mine)])
    row = [pair] + [first_axis(pair, by) for by in steps]
    row = jnp.concatenate(row)
    blocks = [row] + [second_axis(row, by) for by in steps]
    in_par = swap_cores(w_in)
    out_par = swap_cores(w_out)

    sums, gathered = first_product(at, blocks, w_in, in_par, w_out, out_par)
    sums = sums.reshape(ring, 96, 1536)

    up, down = sums[4, :, :768], sums[4, :, 768:]
    for left in (3, 2, 1, 0):
        up, down = decoded(along_z(coded(up), 1)), decoded(along_z(coded(down), -1))
        if left == 3:
            up = jnp.pad(up, ((0, 0), (0, 768)))
            down = jnp.pad(down, ((0, 0), (768, 0)))
        if left:
            up, down = sums[left] + up, sums[ring - left] + down
    total = sums[0] + up + down
    gathered = gathered.reshape(768, 1536)
    total, gathered, gathered_oth = lax.optimization_barrier(
        (total, gathered, swap_cores(gathered))
    )

    other = swap_cores(total)
    value, slopes = gelu_parts(jnp.where(fore, total, other))
    hid = jnp.where(fore, other, total) * slopes
    here = jnp.where(fore, value, hid).astype(bf16)

    chunks = [here] + [None] * (ring - 1)
    up = down = here
    for far in (1, 2, 3):
        up, down = along_z(up, 1), along_z(down, -1)
        chunks[ring - far], chunks[far] = up, down
    chunks[4] = jnp.concatenate([along_z(up[:, :768], 1), along_z(down[:, 768:], -1)], axis=1)

    acts = jnp.concatenate(chunks)
    acts_own = jnp.where(fore, acts[:, :768], acts[:, 768:])
    acts_oth = swap_cores(jnp.where(fore, acts[:, 768:], acts[:, :768]))
    partial = second_product(at, chunks, w_in, in_par, w_out, out_par)
    partial, acts_oth = lax.optimization_barrier((partial, acts_oth))

    kept = partial[0].astype(f32)
    for k, by in enumerate(steps):
        kept = kept + second_axis(partial[k + 1], -by).astype(f32)
    grad_in, grad_out = weight_grads(at, gathered, gathered_oth, acts_own, acts_oth)
    kept, grad_in, grad_out = lax.optimization_barrier((kept, grad_in, grad_out))
    last = kept[0]
    for k, by in enumerate(steps):
        last = last + first_axis(kept[k + 1].astype(bf16), -by).astype(f32)
    last = last.astype(bf16)
    keep = jnp.where(fore, last[:24], last[24:])
    came = swap_cores(jnp.where(fore, last[24:], last[:24]))
    output = jnp.where(fore, keep, came)
    input_grad = jnp.where(fore, came, keep)
    return (output, input_grad, grad_in, grad_out)


def solution(mesh):
    placed = (P("row", "col"), P("col", "row"), P("row", "col"), P("row", "col"))
    return jax.shard_map(
        local,
        mesh=mesh,
        in_specs=placed,
        out_specs=(P("row", "col"), P("row", "col"), P("col", "row"), P("row", "col")),
        check_vma=False,
    )
```

time: 438 us -> 171 us (0.39)
  waiting for transfers between devices: 379 us -> 75.9 us
  starting transfers between devices: 0.2 us -> 55 us
  matrix products: 32.3 us -> 0 us
  Pallas kernels: 0 us -> 23.8 us
  between operations: 13.8 us -> 1.02 us
    reduce_scatter x2 -> x0, waiting for transfers between devices: 158 us -> none  [the longest x1 93.5 us: local(): lax.psum_scatter(contract_last(picked, w_in), 'row', scatter_dimension=0,...]
    psum x1 -> x0, waiting for transfers between devices: 118 us -> none  [local(): hidden = lax.psum(hidden_part, 'col')]
    all_gather x2 -> x0, waiting for transfers between devices: 101 us -> none  [the longest x1 55.3 us: local(): lax.all_gather(out_grad, 'row', axis=0, tiled=True)]
    ppermute x0 -> x35, waiting for transfers between devices: none -> 75.9 us  [the longest x16 39.8 us: along_z(): lax.ppermute(array, 'col', [(z, (z + by) % ring) for z in range(ring)])]
    ppermute x0 -> x35, starting transfers between devices: none -> 55 us  [the longest x16 24.4 us: along_z(): lax.ppermute(array, 'col', [(z, (z + by) % ring) for z in range(ring)])]
    dot_general x6 -> x0, matrix products: 32.3 us -> none  [the longest x2 11.2 us: contract_first(): lax.dot_general(left, right, (((0,), (0,)), ((), ())), preferred_element_...]
    pallas_call x0 -> x3, Pallas kernels: none -> 23.8 us  [the longest x1 9.21 us: first_product(): pl.pallas_call(first_kernel, grid_spec=pltpu.PrefetchScalarGridSpec(num_s...]
  transfers between devices with their start and end apart: 5 -> 35, of which waited for: 5 -> 18; matrix products, arithmetic and copies ran while one was open for 7% -> 4% of each run, Pallas kernels for 0% -> 9%
where the time goes in v1:
time: 171 us; the launch traced here: 170 us
  waiting for transfers between devices  75.9 us (44%)
  starting transfers between devices  55 us (32%)
  Pallas kernels  23.8 us (14%)
  other arithmetic  8.56 us (5%)
  local copies, waits for them, and re-layouts  6.27 us (4%)
    ppermute x16, waiting for transfers between devices, along_z(): lax.ppermute(array, 'col', [(z, (z + by) % ring) for z in range(ring)])  39.8 us
    ppermute x16, starting transfers between devices, along_z(): lax.ppermute(array, 'col', [(z, (z + by) % ring) for z in range(ring)])  24.4 us
    ppermute x6, waiting for transfers between devices, second_axis(): return lax.ppermute(array, 'row', pairs)  21.8 us
    ppermute x7, starting transfers between devices, swap_cores(): lax.ppermute(array, 'row', [(place(0, 0, 0) + r, place(0, 0, 0) + r ^ 1)...  18.9 us
    ppermute x6, waiting for transfers between devices, first_axis(): return lax.ppermute(array, 'row', pairs)  11.3 us
    pallas_call x1, Pallas kernels, first_product(): pl.pallas_call(first_kernel, grid_spec=pltpu.PrefetchScalarGridSpec(num_s...  9.21 us
    pallas_call x1, Pallas kernels, second_product(): pl.pallas_call(second_kernel, grid_spec=pltpu.PrefetchScalarGridSpec(num_...  7.61 us
    pallas_call x1, Pallas kernels, weight_grads(): pl.pallas_call(grad_kernel, grid_spec=pltpu.PrefetchScalarGridSpec(num_sc...  6.96 us
  transfers between devices with their start and end apart: 35, of which 18 were waited for; matrix products, arithmetic and copies ran while one was open for 4% of the time, Pallas kernels for 9%

profile of v1, /device:TPU:1, one launch (start us, length us, event | category | flops | bytes accessed | tf_op | source)
XLA Modules:
  0.0 170.4 jit_solution(3766324708716543795)
XLA Ops:
  1.6 3.3 %collective-permute-start = (bf16[24,1536]{1,0:T(8,128)(2,1)S(1)}, bf16[24,1536]{1,0:T(8,128)(2,1)S(1)}, u32[]{:S(2)}, u32[]{:S(2)}) collective-permute-start(bf16[24,1536]{1,0:T(8,128)(2,1)S(1)} %broadcast_select_fusion.8), channel_id=1, source_target_pairs={{0,8},{8,0},{16,24},{24,16},{32,40},{40,32},{48,56},{56,48},{64,72... | collective-permute-start | bytes 221192 | tf_op jit(solution)/shard_map/ppermute | solution.py:45
  10.4 2.8 %collective-permute-done.1 = bf16[48,1536]{1,0:T(8,128)(2,1)S(1)} collective-permute-done((bf16[48,1536]{1,0:T(8,128)(2,1)S(1)}, bf16[48,1536]{1,0:T(8,128)(2,1)S(1)}, u32[]{:S(2)}, u32[]{:S(2)}) %collective-permute-start.1) | collective-permute-done | bytes 147488 | tf_op jit(solution)/shard_map/ppermute | solution.py:56
  19.1 13.9 %collective-permute-done.4.a1 = bf16[192,1536]{1,0:T(8,128)(2,1)S(1)} collective-permute-done((bf16[192,1536]{1,0:T(8,128)(2,1)S(1)}, bf16[192,1536]{1,0:T(8,128)(2,1)S(1)}, u32[]{:S(2)}, u32[]{:S(2)}) %collective-permute-start.4) | collective-permute-done | bytes 589856 | tf_op jit(solution)/shard_map/ppermute | solution.py:65
  36.3 9.2 %shard_map.75 = (f32[8,2,48,1536]{3,2,1,0:T(8,128)}, bf16[8,2,48,1536]{3,2,1,0:T(8,128)(2,1)S(1)}) custom-call(s32[2]{0:T(128)S(1)} %pad_add_fusion.at, bf16[192,1536]{1,0:T(8,128)(2,1)S(1)} %constant_dynamic-update-slice_fusion.a0, bf16[192,1536]{1,0:T(8,128)(2,1)S(1)} %collective-permute-done.4.a1, bf16[192,1536]{1,0:T(8,128)(2,1)} %collective-permute-done.5.a2, ...), custom_call_target="tpu_custom_call" | custom-call | flops 3623878656 | bytes 12582912 | tf_op jit(solution)/shard_map/pallas_call | solution.py:111
  46.7 5.0 %collective-permute-start.13 = (bf16[96,768]{1,0:T(8,128)(2,1)S(1)}, bf16[96,768]{1,0:T(8,128)(2,1)S(1)}, u32[]{:S(2)}, u32[]{:S(2)}) collective-permute-start(bf16[96,768]{1,0:T(8,128)(2,1)S(1)} %get-tuple-element.41), channel_id=1, source_target_pairs={{0,7},{1,0},{2,1},{3,2},{4,3},{5,4},{6,5},{7,6},{8,15},{9,8},{10,9... | collective-permute-start | bytes 442376 | tf_op jit(solution)/shard_map/ppermute | solution.py:69
  54.4 2.7 %collective-permute-start.17 = (bf16[768,1536]{1,0:T(8,128)(2,1)S(1)}, bf16[768,1536]{1,0:T(8,128)(2,1)S(1)}, u32[]{:S(2)}, u32[]{:S(2)}) collective-permute-start(bf16[768,1536]{1,0:T(8,128)(2,1)S(1)} %bitcast.57), channel_id=1, source_target_pairs={{0,8},{8,0},{16,24},{24,16},{32,40},{40,32},{48,56},{56,48},{64,72... | collective-permute-start | bytes 7077896 | tf_op jit(solution)/shard_map/ppermute | solution.py:45
  57.4 3.1 %collective-permute-start.14 = (bf16[96,1536]{1,0:T(8,128)(2,1)S(1)}, bf16[96,1536]{1,0:T(8,128)(2,1)S(1)}, u32[]{:S(2)}, u32[]{:S(2)}) collective-permute-start(bf16[96,1536]{1,0:T(8,128)(2,1)S(1)} %fusion.51), channel_id=1, source_target_pairs={{0,7},{1,0},{2,1},{3,2},{4,3},{5,4},{6,5},{7,6},{8,15},{9,8},{10,9... | collective-permute-start | bytes 884744 | tf_op jit(solution)/shard_map/ppermute | solution.py:69
  60.8 5.6 %collective-permute-done.14 = bf16[96,1536]{1,0:T(8,128)(2,1)S(1)} collective-permute-done((bf16[96,1536]{1,0:T(8,128)(2,1)S(1)}, bf16[96,1536]{1,0:T(8,128)(2,1)S(1)}, u32[]{:S(2)}, u32[]{:S(2)}) %collective-permute-start.14) | collective-permute-done | bytes 294944 | tf_op jit(solution)/shard_map/ppermute | solution.py:69
  66.8 3.5 %collective-permute-start.15 = (bf16[96,1536]{1,0:T(8,128)(2,1)S(1)}, bf16[96,1536]{1,0:T(8,128)(2,1)S(1)}, u32[]{:S(2)}, u32[]{:S(2)}) collective-permute-start(bf16[96,1536]{1,0:T(8,128)(2,1)S(1)} %fusion.52), channel_id=1, source_target_pairs={{0,7},{1,0},{2,1},{3,2},{4,3},{5,4},{6,5},{7,6},{8,15},{9,8},{10,9... | collective-permute-start | bytes 884744 | tf_op jit(solution)/shard_map/ppermute | solution.py:69
  70.8 4.5 %collective-permute-done.15 = bf16[96,1536]{1,0:T(8,128)(2,1)S(1)} collective-permute-done((bf16[96,1536]{1,0:T(8,128)(2,1)S(1)}, bf16[96,1536]{1,0:T(8,128)(2,1)S(1)}, u32[]{:S(2)}, u32[]{:S(2)}) %collective-permute-start.15) | collective-permute-done | bytes 294944 | tf_op jit(solution)/shard_map/ppermute | solution.py:69
  75.8 3.5 %collective-permute-start.16 = (bf16[96,1536]{1,0:T(8,128)(2,1)S(1)}, bf16[96,1536]{1,0:T(8,128)(2,1)S(1)}, u32[]{:S(2)}, u32[]{:S(2)}) collective-permute-start(bf16[96,1536]{1,0:T(8,128)(2,1)S(1)} %fusion.53), channel_id=1, source_target_pairs={{0,7},{1,0},{2,1},{3,2},{4,3},{5,4},{6,5},{7,6},{8,15},{9,8},{10,9... | collective-permute-start | bytes 884744 | tf_op jit(solution)/shard_map/ppermute | solution.py:69
  79.8 3.6 %collective-permute-done.16 = bf16[96,1536]{1,0:T(8,128)(2,1)S(1)} collective-permute-done((bf16[96,1536]{1,0:T(8,128)(2,1)S(1)}, bf16[96,1536]{1,0:T(8,128)(2,1)S(1)}, u32[]{:S(2)}, u32[]{:S(2)}) %collective-permute-start.16) | collective-permute-done | bytes 294944 | tf_op jit(solution)/shard_map/ppermute | solution.py:69
  83.3 3.6 %collective-permute-done.12 = bf16[96,1536]{1,0:T(8,128)(2,1)S(1)} collective-permute-done((bf16[96,1536]{1,0:T(8,128)(2,1)S(1)}, bf16[96,1536]{1,0:T(8,128)(2,1)S(1)}, u32[]{:S(2)}, u32[]{:S(2)}) %collective-permute-start.12) | collective-permute-done | bytes 294944 | tf_op jit(solution)/shard_map/ppermute | solution.py:69
  87.7 3.5 %collective-permute-start.18 = (f32[96,1536]{1,0:T(8,128)S(1)}, f32[96,1536]{1,0:T(8,128)S(1)}, u32[]{:S(2)}, u32[]{:S(2)}) collective-permute-start(f32[96,1536]{1,0:T(8,128)S(1)} %fusion.20), channel_id=1, source_target_pairs={{0,8},{8,0},{16,24},{24,16},{32,40},{40,32},{48,56},{56,48},{64,72... | collective-permute-start | bytes 1769480 | tf_op jit(solution)/shard_map/ppermute | solution.py:45
  94.8 6.8 %collective-permute-done.19.refs_1_ = bf16[96,1536]{1,0:T(8,128)(2,1)S(1)} collective-permute-done((bf16[96,1536]{1,0:T(8,128)(2,1)S(1)}, bf16[96,1536]{1,0:T(8,128)(2,1)S(1)}, u32[]{:S(2)}, u32[]{:S(2)}) %collective-permute-start.19) | collective-permute-done | bytes 294944 | tf_op jit(solution)/shard_map/ppermute | solution.py:69
  103.1 5.8 %collective-permute-done.20.refs_2_ = bf16[96,1536]{1,0:T(8,128)(2,1)S(1)} collective-permute-done((bf16[96,1536]{1,0:T(8,128)(2,1)S(1)}, bf16[96,1536]{1,0:T(8,128)(2,1)S(1)}, u32[]{:S(2)}, u32[]{:S(2)}) %collective-permute-start.20) | collective-permute-done | bytes 294944 | tf_op jit(solution)/shard_map/ppermute | solution.py:69
  108.9 3.1 %collective-permute-start.21 = (bf16[96,1536]{1,0:T(8,128)(2,1)S(1)}, bf16[96,1536]{1,0:T(8,128)(2,1)S(1)}, u32[]{:S(2)}, u32[]{:S(2)}) collective-permute-start(bf16[96,1536]{1,0:T(8,128)(2,1)S(1)} %collective-permute-done.20.refs_2_), channel_id=1, source_target_pairs={{0,7},{1,0},{2,1},{3,2},{4,3},{5,4},{6,5},{7,6},{8,15},{9,8},{10,9... | collective-permute-start | bytes 884744 | tf_op jit(solution)/shard_map/ppermute | solution.py:69
  112.0 7.6 %collective-permute-done.24.refs_5_ = bf16[96,1536]{1,0:T(8,128)(2,1)S(1)} collective-permute-done((bf16[96,1536]{1,0:T(8,128)(2,1)S(1)}, bf16[96,1536]{1,0:T(8,128)(2,1)S(1)}, u32[]{:S(2)}, u32[]{:S(2)}) %collective-permute-start.24) | collective-permute-done | bytes 294944 | tf_op jit(solution)/shard_map/ppermute | solution.py:69
  125.2 4.2 %collective-permute-start.27 = (bf16[768,768]{1,0:T(8,128)(2,1)S(1)}, bf16[768,768]{1,0:T(8,128)(2,1)S(1)}, u32[]{:S(2)}, u32[]{:S(2)}) collective-permute-start(bf16[768,768]{1,0:T(8,128)(2,1)S(1)} %get-tuple-element.44), channel_id=1, source_target_pairs={{0,8},{8,0},{16,24},{24,16},{32,40},{40,32},{48,56},{56,48},{64,72... | collective-permute-start | bytes 3538952 | tf_op jit(solution)/shard_map/ppermute | solution.py:45
  129.5 7.6 %shard_map.76 = bf16[4,4,48,1536]{3,2,1,0:T(8,128)(2,1)S(1)} custom-call(s32[2]{0:T(128)S(1)} %pad_add_fusion.at, bf16[96,1536]{1,0:T(8,128)(2,1)S(1)} %get-tuple-element.29.refs_0_, bf16[96,1536]{1,0:T(8,128)(2,1)S(1)} %collective-permute-done.19.refs_1_, bf16[96,1536]{1,0:T(8,128)(2,1)S(1)} %collective-permute-done.20.refs_2_, ...), custom_call_target="tpu_custom_call" | custom-call | flops 3623878656 | bytes 12582912 | tf_op jit(solution)/shard_map/pallas_call | solution.py:177
  140.3 7.0 %shard_map.77 = (bf16[1536,768]{1,0:T(8,128)(2,1)}, bf16[768,1536]{1,0:T(8,128)(2,1)}) custom-call(s32[2]{0:T(128)S(1)} %pad_add_fusion.at, bf16[768,1536]{1,0:T(8,128)(2,1)S(1)} %bitcast.58, bf16[768,1536]{1,0:T(8,128)(2,1)S(1)} %collective-permute-done.17.a_oth, bf16[768,768]{1,0:T(8,128)(2,1)S(1)} %get-tuple-element.43.b_own, ...), custom_call_target="tpu_custom_call" | custom-call | flops 3623878656 | bytes 12582912 | tf_op jit(solution)/shard_map/pallas_call | solution.py:216
  147.3 7.9 %collective-permute-done.29 = bf16[4,48,1536]{2,1,0:T(8,128)(2,1)S(1)} collective-permute-done((bf16[4,48,1536]{2,1,0:T(8,128)(2,1)S(1)}, bf16[4,48,1536]{2,1,0:T(8,128)(2,1)S(1)}, u32[]{:S(2)}, u32[]{:S(2)}) %collective-permute-start.29) | collective-permute-done | bytes 589856 | tf_op jit(solution)/shard_map/ppermute | solution.py:65
  159.6 4.5 %collective-permute-done.32 = bf16[48,1536]{1,0:T(8,128)(2,1)S(1)} collective-permute-done((bf16[48,1536]{1,0:T(8,128)(2,1)S(1)}, bf16[48,1536]{1,0:T(8,128)(2,1)S(1)}, u32[]{:S(2)}, u32[]{:S(2)}) %collective-permute-start.32) | collective-permute-done | bytes 147488 | tf_op jit(solution)/shard_map/ppermute | solution.py:56
  164.2 4.6 %collective-permute-start.34 = (bf16[24,1536]{1,0:T(8,128)(2,1)S(1)}, bf16[24,1536]{1,0:T(8,128)(2,1)S(1)}, u32[]{:S(2)}, u32[]{:S(2)}) collective-permute-start(bf16[24,1536]{1,0:T(8,128)(2,1)S(1)} %broadcast_select_fusion.4), channel_id=1, source_target_pairs={{0,8},{8,0},{16,24},{24,16},{32,40},{40,32},{48,56},{56,48},{64,72... | collective-permute-start | bytes 221192 | tf_op jit(solution)/shard_map/ppermute | solution.py:45
  (96 shorter events, 42.6 us)
Async XLA Ops:
  4.9 28.1 %collective-permute-start.7 = (bf16[1536,768]{1,0:T(8,128)(2,1)}, bf16[1536,768]{1,0:T(8,128)(2,1)S(1)}, u32[]{:S(2)}, u32[]{:S(2)}) collective-permute-start(bf16[1536,768]{1,0:T(8,128)(2,1)} %refs_8_.1), channel_id=1, source_target_pairs={{0,8},{8,0},{16,24},{24,16},{32,40},{40,32},{48,56},{56,48},{64,72... | collective-permute-start | bytes 7077896 | tf_op jit(solution)/shard_map/ppermute | solution.py:45
  5.0 28.0 %collective-permute-start.8 = (bf16[768,1536]{1,0:T(8,128)(2,1)}, bf16[768,1536]{1,0:T(8,128)(2,1)}, u32[]{:S(2)}, u32[]{:S(2)}) collective-permute-start(bf16[768,1536]{1,0:T(8,128)(2,1)} %refs_10_.1), channel_id=1, source_target_pairs={{0,8},{8,0},{16,24},{24,16},{32,40},{40,32},{48,56},{56,48},{64,72... | collective-permute-start | bytes 7077896 | tf_op jit(solution)/shard_map/ppermute | solution.py:45
  16.2 16.7 %collective-permute-start.4 = (bf16[192,1536]{1,0:T(8,128)(2,1)S(1)}, bf16[192,1536]{1,0:T(8,128)(2,1)S(1)}, u32[]{:S(2)}, u32[]{:S(2)}) collective-permute-start(bf16[192,1536]{1,0:T(8,128)(2,1)S(1)} %constant_dynamic-update-slice_fusion.a0), channel_id=1, source_target_pairs={{0,16},{8,72},{16,32},{24,88},{32,48},{40,104},{48,0},{56,120},{64... | collective-permute-start | bytes 1769480 | tf_op jit(solution)/shard_map/ppermute | solution.py:65
  16.3 16.7 %collective-permute-start.5 = (bf16[192,1536]{1,0:T(8,128)(2,1)S(1)}, bf16[192,1536]{1,0:T(8,128)(2,1)}, u32[]{:S(2)}, u32[]{:S(2)}) collective-permute-start(bf16[192,1536]{1,0:T(8,128)(2,1)S(1)} %constant_dynamic-update-slice_fusion.a0), channel_id=1, source_target_pairs={{0,48},{8,200},{16,0},{24,216},{32,16},{40,232},{48,32},{56,248},{... | collective-permute-start | bytes 1769480 | tf_op jit(solution)/shard_map/ppermute | solution.py:65
  19.0 14.0 %collective-permute-start.6 = (bf16[192,1536]{1,0:T(8,128)(2,1)S(1)}, bf16[192,1536]{1,0:T(8,128)(2,1)}, u32[]{:S(2)}, u32[]{:S(2)}) collective-permute-start(bf16[192,1536]{1,0:T(8,128)(2,1)S(1)} %constant_dynamic-update-slice_fusion.a0), channel_id=1, source_target_pairs={{0,32},{8,136},{16,48},{24,152},{32,0},{40,168},{48,16},{56,184},{... | collective-permute-start | bytes 1769480 | tf_op jit(solution)/shard_map/ppermute | solution.py:65
  46.7 10.4 %collective-permute-start.13 = (bf16[96,768]{1,0:T(8,128)(2,1)S(1)}, bf16[96,768]{1,0:T(8,128)(2,1)S(1)}, u32[]{:S(2)}, u32[]{:S(2)}) collective-permute-start(bf16[96,768]{1,0:T(8,128)(2,1)S(1)} %get-tuple-element.41), channel_id=1, source_target_pairs={{0,7},{1,0},{2,1},{3,2},{4,3},{5,4},{6,5},{7,6},{8,15},{9,8},{10,9... | collective-permute-start | bytes 442376 | tf_op jit(solution)/shard_map/ppermute | solution.py:69
  54.4 33.3 %collective-permute-start.17 = (bf16[768,1536]{1,0:T(8,128)(2,1)S(1)}, bf16[768,1536]{1,0:T(8,128)(2,1)S(1)}, u32[]{:S(2)}, u32[]{:S(2)}) collective-permute-start(bf16[768,1536]{1,0:T(8,128)(2,1)S(1)} %bitcast.57), channel_id=1, source_target_pairs={{0,8},{8,0},{16,24},{24,16},{32,40},{40,32},{48,56},{56,48},{64,72... | collective-permute-start | bytes 7077896 | tf_op jit(solution)/shard_map/ppermute | solution.py:45
  57.4 9.1 %collective-permute-start.14 = (bf16[96,1536]{1,0:T(8,128)(2,1)S(1)}, bf16[96,1536]{1,0:T(8,128)(2,1)S(1)}, u32[]{:S(2)}, u32[]{:S(2)}) collective-permute-start(bf16[96,1536]{1,0:T(8,128)(2,1)S(1)} %fusion.51), channel_id=1, source_target_pairs={{0,7},{1,0},{2,1},{3,2},{4,3},{5,4},{6,5},{7,6},{8,15},{9,8},{10,9... | collective-permute-start | bytes 884744 | tf_op jit(solution)/shard_map/ppermute | solution.py:69
  60.7 9.6 %collective-permute-start.10 = (bf16[96,1536]{1,0:T(8,128)(2,1)S(1)}, bf16[96,1536]{1,0:T(8,128)(2,1)S(1)}, u32[]{:S(2)}, u32[]{:S(2)}) collective-permute-start(bf16[96,1536]{1,0:T(8,128)(2,1)S(1)} %fusion.48), channel_id=1, source_target_pairs={{0,1},{1,2},{2,3},{3,4},{4,5},{5,6},{6,7},{7,0},{8,9},{9,10},{10,1... | collective-permute-start | bytes 884744 | tf_op jit(solution)/shard_map/ppermute | solution.py:69
  66.8 8.5 %collective-permute-start.15 = (bf16[96,1536]{1,0:T(8,128)(2,1)S(1)}, bf16[96,1536]{1,0:T(8,128)(2,1)S(1)}, u32[]{:S(2)}, u32[]{:S(2)}) collective-permute-start(bf16[96,1536]{1,0:T(8,128)(2,1)S(1)} %fusion.52), channel_id=1, source_target_pairs={{0,7},{1,0},{2,1},{3,2},{4,3},{5,4},{6,5},{7,6},{8,15},{9,8},{10,9... | collective-permute-start | bytes 884744 | tf_op jit(solution)/shard_map/ppermute | solution.py:69
  70.7 8.5 %collective-permute-start.11 = (bf16[96,1536]{1,0:T(8,128)(2,1)S(1)}, bf16[96,1536]{1,0:T(8,128)(2,1)S(1)}, u32[]{:S(2)}, u32[]{:S(2)}) collective-permute-start(bf16[96,1536]{1,0:T(8,128)(2,1)S(1)} %fusion.49), channel_id=1, source_target_pairs={{0,1},{1,2},{2,3},{3,4},{4,5},{5,6},{6,7},{7,0},{8,9},{9,10},{10,1... | collective-permute-start | bytes 884744 | tf_op jit(solution)/shard_map/ppermute | solution.py:69
  75.8 7.6 %collective-permute-start.16 = (bf16[96,1536]{1,0:T(8,128)(2,1)S(1)}, bf16[96,1536]{1,0:T(8,128)(2,1)S(1)}, u32[]{:S(2)}, u32[]{:S(2)}) collective-permute-start(bf16[96,1536]{1,0:T(8,128)(2,1)S(1)} %fusion.53), channel_id=1, source_target_pairs={{0,7},{1,0},{2,1},{3,2},{4,3},{5,4},{6,5},{7,6},{8,15},{9,8},{10,9... | collective-permute-start | bytes 884744 | tf_op jit(solution)/shard_map/ppermute | solution.py:69
  79.7 7.3 %collective-permute-start.12 = (bf16[96,1536]{1,0:T(8,128)(2,1)S(1)}, bf16[96,1536]{1,0:T(8,128)(2,1)S(1)}, u32[]{:S(2)}, u32[]{:S(2)}) collective-permute-start(bf16[96,1536]{1,0:T(8,128)(2,1)S(1)} %fusion.50), channel_id=1, source_target_pairs={{0,1},{1,2},{2,3},{3,4},{4,5},{5,6},{6,7},{7,0},{8,9},{9,10},{10,1... | collective-permute-start | bytes 884744 | tf_op jit(solution)/shard_map/ppermute | solution.py:69
  93.3 8.3 %collective-permute-start.19 = (bf16[96,1536]{1,0:T(8,128)(2,1)S(1)}, bf16[96,1536]{1,0:T(8,128)(2,1)S(1)}, u32[]{:S(2)}, u32[]{:S(2)}) collective-permute-start(bf16[96,1536]{1,0:T(8,128)(2,1)S(1)} %get-tuple-element.29.refs_0_), channel_id=1, source_target_pairs={{0,7},{1,0},{2,1},{3,2},{4,3},{5,4},{6,5},{7,6},{8,15},{9,8},{10,9... | collective-permute-start | bytes 884744 | tf_op jit(solution)/shard_map/ppermute | solution.py:69
  93.3 9.7 %collective-permute-start.22 = (bf16[96,1536]{1,0:T(8,128)(2,1)S(1)}, bf16[96,1536]{1,0:T(8,128)(2,1)S(1)}, u32[]{:S(2)}, u32[]{:S(2)}) collective-permute-start(bf16[96,1536]{1,0:T(8,128)(2,1)S(1)} %get-tuple-element.29.refs_0_), channel_id=1, source_target_pairs={{0,1},{1,2},{2,3},{3,4},{4,5},{5,6},{6,7},{7,0},{8,9},{9,10},{10,1... | collective-permute-start | bytes 884744 | tf_op jit(solution)/shard_map/ppermute | solution.py:69
  101.6 7.3 %collective-permute-start.20 = (bf16[96,1536]{1,0:T(8,128)(2,1)S(1)}, bf16[96,1536]{1,0:T(8,128)(2,1)S(1)}, u32[]{:S(2)}, u32[]{:S(2)}) collective-permute-start(bf16[96,1536]{1,0:T(8,128)(2,1)S(1)} %collective-permute-done.19.refs_1_), channel_id=1, source_target_pairs={{0,7},{1,0},{2,1},{3,2},{4,3},{5,4},{6,5},{7,6},{8,15},{9,8},{10,9... | collective-permute-start | bytes 884744 | tf_op jit(solution)/shard_map/ppermute | solution.py:69
  103.1 8.9 %collective-permute-start.23 = (bf16[96,1536]{1,0:T(8,128)(2,1)S(1)}, bf16[96,1536]{1,0:T(8,128)(2,1)S(1)}, u32[]{:S(2)}, u32[]{:S(2)}) collective-permute-start(bf16[96,1536]{1,0:T(8,128)(2,1)S(1)} %collective-permute-done.22.refs_7_), channel_id=1, source_target_pairs={{0,1},{1,2},{2,3},{3,4},{4,5},{5,6},{6,7},{7,0},{8,9},{9,10},{10,1... | collective-permute-start | bytes 884744 | tf_op jit(solution)/shard_map/ppermute | solution.py:69
  108.9 10.8 %collective-permute-start.21 = (bf16[96,1536]{1,0:T(8,128)(2,1)S(1)}, bf16[96,1536]{1,0:T(8,128)(2,1)S(1)}, u32[]{:S(2)}, u32[]{:S(2)}) collective-permute-start(bf16[96,1536]{1,0:T(8,128)(2,1)S(1)} %collective-permute-done.20.refs_2_), channel_id=1, source_target_pairs={{0,7},{1,0},{2,1},{3,2},{4,3},{5,4},{6,5},{7,6},{8,15},{9,8},{10,9... | collective-permute-start | bytes 884744 | tf_op jit(solution)/shard_map/ppermute | solution.py:69
  111.9 7.7 %collective-permute-start.24 = (bf16[96,1536]{1,0:T(8,128)(2,1)S(1)}, bf16[96,1536]{1,0:T(8,128)(2,1)S(1)}, u32[]{:S(2)}, u32[]{:S(2)}) collective-permute-start(bf16[96,1536]{1,0:T(8,128)(2,1)S(1)} %collective-permute-done.23.refs_6_), channel_id=1, source_target_pairs={{0,1},{1,2},{2,3},{3,4},{4,5},{5,6},{6,7},{7,0},{8,9},{9,10},{10,1... | collective-permute-start | bytes 884744 | tf_op jit(solution)/shard_map/ppermute | solution.py:69
  125.2 11.9 %collective-permute-start.27 = (bf16[768,768]{1,0:T(8,128)(2,1)S(1)}, bf16[768,768]{1,0:T(8,128)(2,1)S(1)}, u32[]{:S(2)}, u32[]{:S(2)}) collective-permute-start(bf16[768,768]{1,0:T(8,128)(2,1)S(1)} %get-tuple-element.44), channel_id=1, source_target_pairs={{0,8},{8,0},{16,24},{24,16},{32,40},{40,32},{48,56},{56,48},{64,72... | collective-permute-start | bytes 3538952 | tf_op jit(solution)/shard_map/ppermute | solution.py:45
  137.2 10.0 %collective-permute-start.28 = (bf16[4,48,1536]{2,1,0:T(8,128)(2,1)S(1)}, bf16[4,48,1536]{2,1,0:T(8,128)(2,1)S(1)}, u32[]{:S(2)}, u32[]{:S(2)}) collective-permute-start(bf16[4,48,1536]{2,1,0:T(8,128)(2,1)S(1)} %get-tuple-element.45), channel_id=1, source_target_pairs={{0,48},{8,200},{16,0},{24,216},{32,16},{40,232},{48,32},{56,248},{... | collective-permute-start | bytes 1769480 | tf_op jit(solution)/shard_map/ppermute | solution.py:65
  138.6 16.6 %collective-permute-start.29 = (bf16[4,48,1536]{2,1,0:T(8,128)(2,1)S(1)}, bf16[4,48,1536]{2,1,0:T(8,128)(2,1)S(1)}, u32[]{:S(2)}, u32[]{:S(2)}) collective-permute-start(bf16[4,48,1536]{2,1,0:T(8,128)(2,1)S(1)} %get-tuple-element.47), channel_id=1, source_target_pairs={{0,16},{8,72},{16,32},{24,88},{32,48},{40,104},{48,0},{56,120},{64... | collective-permute-start | bytes 1769480 | tf_op jit(solution)/shard_map/ppermute | solution.py:65
  138.8 16.4 %collective-permute-start.30 = (bf16[4,48,1536]{2,1,0:T(8,128)(2,1)S(1)}, bf16[4,48,1536]{2,1,0:T(8,128)(2,1)S(1)}, u32[]{:S(2)}, u32[]{:S(2)}) collective-permute-start(bf16[4,48,1536]{2,1,0:T(8,128)(2,1)S(1)} %get-tuple-element.46), channel_id=1, source_target_pairs={{0,32},{8,136},{16,48},{24,152},{32,0},{40,168},{48,16},{56,184},{... | collective-permute-start | bytes 1769480 | tf_op jit(solution)/shard_map/ppermute | solution.py:65
  157.3 6.8 %collective-permute-start.32 = (bf16[48,1536]{1,0:T(8,128)(2,1)S(1)}, bf16[48,1536]{1,0:T(8,128)(2,1)S(1)}, u32[]{:S(2)}, u32[]{:S(2)}) collective-permute-start(bf16[48,1536]{1,0:T(8,128)(2,1)S(1)} %get-tuple-element.50), channel_id=1, source_target_pairs={{0,64},{8,24},{16,80},{24,40},{32,96},{40,56},{48,112},{56,8},{64,... | collective-permute-start | bytes 442376 | tf_op jit(solution)/shard_map/ppermute | solution.py:56
  (15 other events, 72.3 us)

commit v2 on v0

v2 whole, which is shorter than its diff:
```python
import jax
import jax.numpy as jnp
from jax import lax
from jax.experimental import pallas as pl
from jax.experimental.pallas import tpu as pltpu
from jax.sharding import PartitionSpec as P

gelu_scale = 0.7978845608028654
gelu_cubic = 0.044715
f32 = jnp.float32
bf16 = jnp.bfloat16
side = 4
ring = 8
tile = 256
steps = (1, -1, 2)
barrier = lax.optimization_barrier


def gelu_parts(hidden):
    inner = gelu_scale * (hidden + gelu_cubic * hidden * hidden * hidden)
    tangent = jnp.tanh(inner)
    value = 0.5 * hidden * (1.0 + tangent)
    slopes = 0.5 * (1.0 + tangent) + 0.5 * hidden * (1.0 - tangent * tangent) * gelu_scale * (
        1.0 + 3.0 * gelu_cubic * hidden * hidden
    )
    return (value, slopes)


def coded(array):
    array = array * 2.0**30
    return (array * array * array).astype(bf16)


def decoded(array):
    array = array.astype(f32)
    return jnp.sign(array) * jnp.exp2(jnp.log2(jnp.abs(array)) * (1.0 / 3.0) - 30.0)


def place(x, y, core):
    return ((x % side) * side + y % side) * 2 + core


def swap_cores(array):
    return lax.ppermute(array, "row", [(r, r ^ 1) for r in range(32)])


def first_axis(array, by):
    pairs = []
    for x in range(side):
        for y in range(side):
            pairs.append((place(x, y, 0), place(x + by, y, 0)))
            pairs.append((place(x, y, 1), place(x, y + by, 1)))
    return lax.ppermute(array, "row", pairs)


def second_axis(array, by):
    pairs = []
    for x in range(side):
        for y in range(side):
            pairs.append((place(x, y, 0), place(x, y + by, 0)))
            pairs.append((place(x, y, 1), place(x + by, y, 1)))
    return lax.ppermute(array, "row", pairs)


def along_z(array, by):
    return lax.ppermute(array, "col", [(z, (z + by) % ring) for z in range(ring)])


def slot(at, outer, inner):
    core, me = at[0], at[1]
    spot = jnp.where(core == 0, inner * side + outer, outer * side + inner)
    return lax.rem(spot // 2 + ring - me, ring), lax.rem(spot, 2)


def call(kernel, at, args, in_specs, out_specs, out_shape, grid, macs, scratch=()):
    return pl.pallas_call(
        kernel,
        grid_spec=pltpu.PrefetchScalarGridSpec(
            num_scalar_prefetch=1,
            grid=grid,
            in_specs=in_specs,
            out_specs=out_specs,
            scratch_shapes=scratch,
        ),
        out_shape=out_shape,
        compiler_params=pltpu.CompilerParams(vmem_limit_bytes=32 << 20),
        cost_estimate=pl.CostEstimate(
            flops=2 * macs, bytes_accessed=8 << 20, transcendentals=0
        ),
    )(at, *args)


def shape(*dims, of=bf16):
    return jax.ShapeDtypeStruct(dims, of)


def fixed(*dims):
    return pl.BlockSpec(dims, lambda j, at: (0,) * len(dims))


def pair_kernel(at, mine, got, out):
    a, b = mine[...].astype(f32), got[...].astype(f32)
    core = at[0]

    @pl.when(core == 0)
    def _():
        out[...] = jnp.concatenate([a, b]).astype(bf16)

    @pl.when(core == 1)
    def _():
        out[...] = jnp.concatenate([b, a]).astype(bf16)


def make_pair(at, mine, got):
    return call(
        pair_kernel, at, (mine, got), [fixed(24, 1536)] * 2, fixed(48, 1536), shape(48, 1536), (1,), 0
    )


def turn_kernel(at, in_own, in_par, out_own, out_par, one_own, one_par, two_own, two_par):
    core = at[0]

    @pl.when(core == 0)
    def _():
        one_own[...] = in_own[...]
        one_par[...] = in_par[...]
        two_own[...] = out_own[...]
        two_par[...] = out_par[...]

    @pl.when(core == 1)
    def _():
        one_own[...] = out_own[...].T
        one_par[...] = out_par[...].T
        two_own[...] = in_own[...].T
        two_par[...] = in_par[...].T


def turned(at, in_own, in_par, out_own, out_par):
    tall = pl.BlockSpec((1536, tile), lambda j, at: (0, j))
    wide = pl.BlockSpec((tile, 1536), lambda j, at: (j, 0))
    return call(
        turn_kernel,
        at,
        (in_own, in_par, out_own, out_par),
        [tall, tall, wide, wide],
        [tall, tall, wide, wide],
        [shape(1536, 768)] * 2 + [shape(768, 1536)] * 2,
        (3,),
        0,
    )


halves = [
    pl.BlockSpec((1536, tile), lambda j, at: (0, jnp.minimum(j, 2))),
    pl.BlockSpec((1536, tile), lambda j, at: (0, jnp.maximum(j - 3, 0))),
]


def farthest_kernel(at, own, par, a0, a1, a2, a3, all_ref, up_ref, down_ref):
    step = pl.program_id(0)

    @pl.when(step == 0)
    def _():
        for outer, ref in enumerate((a0, a1, a2, a3)):
            for inner in range(side):
                chunk, half = slot(at, outer, inner)
                all_ref[chunk, half] = ref[pl.ds(inner * 48, 48), :]

    def product(w):
        a = all_ref[4].reshape(96, 1536)
        return jnp.dot(a, w[...], preferred_element_type=f32).astype(bf16)

    @pl.when(step < 3)
    def _():
        up_ref[...] = product(own)

    @pl.when(step >= 3)
    def _():
        down_ref[...] = product(par)


def farthest(at, own, par, blocks):
    return call(
        farthest_kernel,
        at,
        (own, par, *blocks),
        halves + [fixed(192, 1536)] * 4,
        [
            fixed(ring, 2, 48, 1536),
            pl.BlockSpec((96, tile), lambda j, at: (0, jnp.minimum(j, 2))),
            pl.BlockSpec((96, tile), lambda j, at: (0, jnp.maximum(j - 3, 0))),
        ],
        [shape(ring, 2, 48, 1536), shape(96, 768), shape(96, 768)],
        (6,),
        96 * 1536 * 1536,
    )


def first_product(at, own, par, gathered, picked):
    n = len(picked)

    def kernel(at, own, par, *refs):
        step = pl.program_id(0)

        def product(w):
            a = jnp.concatenate([ref[0].reshape(96, 1536) for ref in refs[:n]])
            h = jnp.dot(a, w[...], preferred_element_type=f32)
            for i, out in enumerate(refs[n:]):
                out[...] = h[i * 96 : (i + 1) * 96]

        pl.when(step < 3)(lambda: product(own))
        pl.when(step >= 3)(lambda: product(par))

    def chunk(i):
        return pl.BlockSpec((1, 2, 48, 1536), lambda j, at: (i, 0, 0, 0))

    return call(
        kernel,
        at,
        (own, par) + (gathered,) * n,
        halves + [chunk(i) for i in picked],
        [pl.BlockSpec((96, tile), lambda j, at: (0, j))] * n,
        [shape(96, 1536, of=f32)] * n,
        (6,),
        n * 96 * 1536 * 1536,
    )


columns = [pl.BlockSpec((768, tile), lambda j, at: (0, j))] * 2
wide_tile = pl.BlockSpec((96, tile), lambda j, at: (0, j))


def second_product(at, own, par, chunks):
    n = len(chunks)

    def kernel(at, own, par, *refs):
        b = jnp.concatenate([ref[...] for ref in refs[:n]])
        o = jnp.dot(b[:, :768], own[...], preferred_element_type=f32) + jnp.dot(
            b[:, 768:], par[...], preferred_element_type=f32
        )
        for i, out in enumerate(refs[n:]):
            out[...] = o[i * 96 : (i + 1) * 96].astype(bf16)

    return call(
        kernel,
        at,
        (own, par, *chunks),
        columns + [fixed(96, 1536)] * n,
        [wide_tile] * n,
        [shape(96, 1536)] * n,
        (6,),
        n * 96 * 1536 * 1536,
    )


def last_kernel(at, own, par, b_own, b_par, *refs):
    ready, (o_ref, made) = refs[: ring - 1], refs[ring - 1 :]
    o = jnp.dot(b_own[...], own[...], preferred_element_type=f32) + jnp.dot(
        b_par[...], par[...], preferred_element_type=f32
    )
    spare = iter(ready)
    for i in range(ring):
        part = o.astype(bf16) if i == 4 else next(spare)[...]
        made[i] = part.reshape(2, 48, tile)
    for outer in range(side):
        for inner in range(side):
            chunk, half = slot(at, outer, inner)
            o_ref[outer, inner] = made[chunk, half]


def last_product(at, own, par, b_own, b_par, ready):
    return call(
        last_kernel,
        at,
        (own, par, b_own, b_par, *ready),
        columns + [fixed(96, 768)] * 2 + [wide_tile] * (ring - 1),
        pl.BlockSpec((side, side, 48, tile), lambda j, at: (0, 0, 0, j)),
        shape(side, side, 48, 1536),
        (6,),
        96 * 1536 * 1536,
        scratch=[pltpu.VMEM((ring, 2, 48, tile), bf16)],
    )


def grad_kernel(at, a_own, a_oth, b_own, b_oth, gin_ref, gout_ref):
    core = at[0]
    first = (((0,), (0,)), ((), ()))

    def both(x, g, act, hid):
        gout_ref[...] = lax.dot_general(act[...], g[...], first, preferred_element_type=f32).astype(
            bf16
        )
        gin_ref[...] = lax.dot_general(x[...], hid[...], first, preferred_element_type=f32).astype(
            bf16
        )

    pl.when(core == 0)(lambda: both(a_own, a_oth, b_own, b_oth))
    pl.when(core == 1)(lambda: both(a_oth, a_own, b_oth, b_own))


def weight_grads(at, a_own, a_oth, b_own, b_oth):
    part = pl.BlockSpec((768, tile), lambda j, at: (0, j))
    return call(
        grad_kernel,
        at,
        (a_own, a_oth, b_own, b_oth),
        [part, part, fixed(768, 768), fixed(768, 768)],
        [pl.BlockSpec((tile, 768), lambda j, at: (j, 0)), part],
        [shape(1536, 768), shape(768, 1536)],
        (6,),
        2 * 768 * 768 * 1536,
    )


def local(inputs, w_in, w_out, out_grad):
    core = lax.axis_index("row") % 2
    me = lax.axis_index("col")
    at = jnp.stack([core, me]).astype(jnp.int32)
    fore = core == 0

    mine = jnp.where(fore, inputs, out_grad)
    got = swap_cores(jnp.where(fore, out_grad, inputs))
    got, send_in, send_out = barrier((got, w_in, w_out))
    in_par, out_par = swap_cores(send_in), swap_cores(send_out)
    pair = make_pair(at, mine, got)
    row = jnp.concatenate([pair] + [first_axis(pair, by) for by in steps])
    row, late = barrier((row, at))
    blocks = [row] + [second_axis(row, by) for by in steps]
    one, par_one, two, par_two = turned(late, w_in, in_par, w_out, out_par)
    *blocks, one, par_one = barrier((*blocks, one, par_one))

    gathered, up, down = farthest(at, one, par_one, blocks)
    for left in (3, 2, 1):
        came_up, came_down = along_z(up, 1), along_z(down, -1)
        picked = (left, ring - left) if left > 1 else (1, ring - 1, 0)
        parts = first_product(at, one, par_one, gathered, picked)
        came_up, came_down, *parts = barrier((came_up, came_down, *parts))
        if left < 2:
            came_up, came_down = decoded(came_up), decoded(came_down)
        came_up, came_down = came_up.astype(f32), came_down.astype(f32)
        if left == 3:
            came_up = jnp.pad(came_up, ((0, 0), (0, 768)))
            came_down = jnp.pad(came_down, ((0, 0), (768, 0)))
            gathered_oth = swap_cores(gathered)
        up, down = parts[0] + came_up, parts[1] + came_down
        up, down = (up.astype(bf16), down.astype(bf16)) if left > 2 else (coded(up), coded(down))
        up, down, gathered = barrier((up, down, gathered))
    total = parts[2] + decoded(along_z(up, 1)) + decoded(along_z(down, -1))
    total, gathered, gathered_oth = barrier((total, gathered, gathered_oth))

    other = swap_cores(total)
    other = jnp.concatenate([other[:, 768:], other[:, :768]], axis=1)
    value, slopes = gelu_parts(jnp.where(fore, total, other))
    hid = jnp.where(fore, other, total) * slopes
    here = jnp.where(fore, value, hid).astype(bf16)

    chunks, ready = {0: here}, {}
    up = down = here
    for far in (1, 2, 3, 4):
        came_up, came_down = (up, down) if far < 4 else (up[:, :768], down[:, 768:])
        came_up, came_down = along_z(came_up, 1), along_z(came_down, -1)
        names = [0] if far == 1 else [far - 1, ring + 1 - far]
        made = second_product(at, two, par_two, [chunks[i] for i in names])
        ready.update(zip(names, made))
        up, down, *made = barrier((came_up, came_down, *made))
        ready.update(zip(names, made))
        if far < 4:
            chunks[ring - far], chunks[far] = up, down
    order = [0, 1, 2, 3, 5, 6, 7]
    acts_own = [chunks[i][:, :768] for i in order]
    acts_own = jnp.concatenate(acts_own[:4] + [up] + acts_own[4:])
    acts_oth = [chunks[i][:, 768:] for i in order]
    acts_oth = swap_cores(jnp.concatenate(acts_oth[:4] + [down] + acts_oth[4:]))
    partial = last_product(at, two, par_two, up, down, [ready[i] for i in order])
    partial, acts_oth = barrier((partial, acts_oth))

    kept = partial[0].astype(f32)
    for k, by in enumerate(steps):
        kept = kept + second_axis(partial[k + 1], -by).astype(f32)
    gathered, gathered_oth = gathered.reshape(768, 1536), gathered_oth.reshape(768, 1536)
    grad_in, grad_out = weight_grads(at, gathered, gathered_oth, acts_own, acts_oth)
    kept, grad_in, grad_out = barrier((kept, grad_in, grad_out))
    last = kept[0]
    for k, by in enumerate(steps):
        last = last + first_axis(kept[k + 1].astype(bf16), -by).astype(f32)
    last = last.astype(bf16)
    keep = jnp.where(fore, last[:24], last[24:])
    came = swap_cores(jnp.where(fore, last[24:], last[:24]))
    output = jnp.where(fore, keep, came)
    input_grad = jnp.where(fore, came, keep)
    return (output, input_grad, grad_in, grad_out)


def solution(mesh):
    placed = (P("row", "col"), P("col", "row"), P("row", "col"), P("row", "col"))
    return jax.shard_map(
        local,
        mesh=mesh,
        in_specs=placed,
        out_specs=(P("row", "col"), P("row", "col"), P("col", "row"), P("row", "col")),
        check_vma=False,
    )
```

time: 438 us -> 146 us (0.33)
  waiting for transfers between devices: 379 us -> 38 us
  starting transfers between devices: 0.2 us -> 58.1 us
  Pallas kernels: 0 us -> 40.1 us
  matrix products: 32.3 us -> 0 us
  between operations: 13.8 us -> 1.02 us
    reduce_scatter x2 -> x0, waiting for transfers between devices: 158 us -> none  [the longest x1 93.5 us: local(): lax.psum_scatter(contract_last(picked, w_in), 'row', scatter_dimension=0,...]
    psum x1 -> x0, waiting for transfers between devices: 118 us -> none  [local(): hidden = lax.psum(hidden_part, 'col')]
    all_gather x2 -> x0, waiting for transfers between devices: 101 us -> none  [the longest x1 55.3 us: local(): lax.all_gather(out_grad, 'row', axis=0, tiled=True)]
    ppermute x0 -> x35, starting transfers between devices: none -> 58.1 us  [the longest x16 24.9 us: along_z(): lax.ppermute(array, 'col', [(z, (z + by) % ring) for z in range(ring)])]
    pallas_call x0 -> x12, Pallas kernels: none -> 40.1 us  [call(): pl.pallas_call(kernel, grid_spec=pltpu.PrefetchScalarGridSpec(num_scalar_...]
    ppermute x0 -> x35, waiting for transfers between devices: none -> 38 us  [the longest x16 15.1 us: along_z(): lax.ppermute(array, 'col', [(z, (z + by) % ring) for z in range(ring)])]
    dot_general x6 -> x0, matrix products: 32.3 us -> none  [the longest x2 11.2 us: contract_first(): lax.dot_general(left, right, (((0,), (0,)), ((), ())), preferred_element_...]
    convert_element_type x3 -> x7, other arithmetic: 7.11 us -> 1.67 us  [the longest x4 1.06 us: coded(): return (array * array * array).astype(bf16)]
  transfers between devices with their start and end apart: 5 -> 35, of which waited for: 5 -> 19; matrix products, arithmetic and copies ran while one was open for 7% -> 1% of each run, Pallas kernels for 0% -> 26%
where the time goes in v2:
time: 146 us; the launch traced here: 145 us
  starting transfers between devices  58.1 us (40%)
  Pallas kernels  40.1 us (27%)
  waiting for transfers between devices  38 us (26%)
  other arithmetic  4.43 us (3%)
  local copies, waits for them, and re-layouts  3.71 us (3%)
    pallas_call x12, Pallas kernels, call(): pl.pallas_call(kernel, grid_spec=pltpu.PrefetchScalarGridSpec(num_scalar_...  40.1 us
    ppermute x16, starting transfers between devices, along_z(): lax.ppermute(array, 'col', [(z, (z + by) % ring) for z in range(ring)])  24.9 us
    ppermute x7, starting transfers between devices, swap_cores(): return lax.ppermute(array, 'row', [(r, r ^ 1) for r in range(32)])  18.6 us
    ppermute x16, waiting for transfers between devices, along_z(): lax.ppermute(array, 'col', [(z, (z + by) % ring) for z in range(ring)])  15.1 us
    ppermute x6, waiting for transfers between devices, second_axis(): return lax.ppermute(array, 'row', pairs)  11.8 us
    ppermute x6, waiting for transfers between devices, first_axis(): return lax.ppermute(array, 'row', pairs)  7.73 us
    ppermute x6, starting transfers between devices, first_axis(): return lax.ppermute(array, 'row', pairs)  7.32 us
    ppermute x6, starting transfers between devices, second_axis(): return lax.ppermute(array, 'row', pairs)  7.18 us
  transfers between devices with their start and end apart: 35, of which 19 were waited for; matrix products, arithmetic and copies ran while one was open for 1% of the time, Pallas kernels for 26%

profile of v2, /device:TPU:1, one launch (start us, length us, event | category | flops | bytes accessed | tf_op | source)
XLA Modules:
  0.0 145.4 jit_solution(12954990894463489628)
XLA Ops:
  1.6 3.3 %collective-permute-start = (bf16[24,1536]{1,0:T(8,128)(2,1)S(1)}, bf16[24,1536]{1,0:T(8,128)(2,1)S(1)}, u32[]{:S(2)}, u32[]{:S(2)}) collective-permute-start(bf16[24,1536]{1,0:T(8,128)(2,1)S(1)} %get-tuple-element.185), channel_id=1, source_target_pairs={{0,8},{8,0},{16,24},{24,16},{32,40},{40,32},{48,56},{56,48},{64,72... | collective-permute-start | bytes 221192 | tf_op jit(solution)/shard_map/ppermute | solution.py:44
  9.7 3.1 %collective-permute-done.3 = bf16[48,1536]{1,0:T(8,128)(2,1)S(1)} collective-permute-done((bf16[48,1536]{1,0:T(8,128)(2,1)S(1)}, bf16[48,1536]{1,0:T(8,128)(2,1)S(1)}, u32[]{:S(2)}, u32[]{:S(2)}) %collective-permute-start.3) | collective-permute-done | bytes 147488 | tf_op jit(solution)/shard_map/ppermute | solution.py:53
  21.9 5.0 %shard_map.76 = (bf16[1536,768]{1,0:T(8,128)(2,1)S(1)}, bf16[1536,768]{1,0:T(8,128)(2,1)S(1)}, bf16[768,1536]{1,0:T(8,128)(2,1)S(1)}, bf16[768,1536]{1,0:T(8,128)(2,1)S(1)}) custom-call(s32[2]{0:T(128)S(1)} %pad_add_fusion.at, bf16[1536,768]{1,0:T(8,128)(2,1)S(1)} %copy-done, bf16[1536,768]{1,0:T(8,128)(2,1)S(1)} %collective-permute-done.4.in_par, ...), custom_call_target="tpu_custom_call" | custom-call | bytes 8388608 | tf_op jit(solution)/shard_map/pallas_call | solution.py:76
  26.9 3.6 %collective-permute-done.7.a2 = bf16[192,1536]{1,0:T(8,128)(2,1)S(1)} collective-permute-done((bf16[192,1536]{1,0:T(8,128)(2,1)S(1)}, bf16[192,1536]{1,0:T(8,128)(2,1)S(1)}, u32[]{:S(2)}, u32[]{:S(2)}) %collective-permute-start.7) | collective-permute-done | bytes 589856 | tf_op jit(solution)/shard_map/ppermute | solution.py:62
  31.9 3.0 %shard_map.77 = (bf16[8,2,48,1536]{3,2,1,0:T(8,128)(2,1)S(1)}, bf16[96,768]{1,0:T(8,128)(2,1)S(1)}, bf16[96,768]{1,0:T(8,128)(2,1)S(1)}) custom-call(s32[2]{0:T(128)S(1)} %pad_add_fusion.at, bf16[1536,768]{1,0:T(8,128)(2,1)S(1)} %get-tuple-element.91.own, bf16[1536,768]{1,0:T(8,128)(2,1)S(1)} %get-tuple-element.92.par, ...), custom_call_target="tpu_custom_call" | custom-call | flops 452984832 | bytes 8388608 | tf_op jit(solution)/shard_map/pallas_call | solution.py:76
  36.6 4.0 %collective-permute-start.10 = (bf16[96,768]{1,0:T(8,128)(2,1)S(1)}, bf16[96,768]{1,0:T(8,128)(2,1)S(1)}, u32[]{:S(2)}, u32[]{:S(2)}) collective-permute-start(bf16[96,768]{1,0:T(8,128)(2,1)S(1)} %get-tuple-element.98), channel_id=1, source_target_pairs={{0,7},{1,0},{2,1},{3,2},{4,3},{5,4},{6,5},{7,6},{8,15},{9,8},{10,9... | collective-permute-start | bytes 442376 | tf_op jit(solution)/shard_map/ppermute | solution.py:66
  40.6 3.1 %shard_map.78 = (f32[96,1536]{1,0:T(8,128)S(1)}, f32[96,1536]{1,0:T(8,128)S(1)}) custom-call(s32[2]{0:T(128)S(1)} %pad_add_fusion.at, bf16[1536,768]{1,0:T(8,128)(2,1)S(1)} %get-tuple-element.91.own, bf16[1536,768]{1,0:T(8,128)(2,1)S(1)} %get-tuple-element.92.par, bf16[8,2,48,1536]{3,2,1,0:T(8,128)(2,1)S(1)} %get-tuple-element.152.refs_0_.refs_1_.refs_2_, ...), custom_call_target="tpu_custom_call" | custom-call | flops 905969664 | bytes 8388608 | tf_op jit(solution)/shard_map/pallas_call | solution.py:76
  43.9 2.7 %collective-permute-start.12 = (bf16[96,1536]{1,0:T(8,128)(2,1)S(1)}, bf16[96,1536]{1,0:T(8,128)(2,1)S(1)}, u32[]{:S(2)}, u32[]{:S(2)}) collective-permute-start(bf16[96,1536]{1,0:T(8,128)(2,1)S(1)} %get-tuple-element.107), channel_id=1, source_target_pairs={{0,7},{1,0},{2,1},{3,2},{4,3},{5,4},{6,5},{7,6},{8,15},{9,8},{10,9... | collective-permute-start | bytes 884744 | tf_op jit(solution)/shard_map/ppermute | solution.py:66
  46.6 4.0 %collective-permute-start.17 = (bf16[8,2,48,1536]{3,2,1,0:T(8,128)(2,1)S(1)}, bf16[8,2,48,1536]{3,2,1,0:T(8,128)(2,1)S(1)}, u32[]{:S(2)}, u32[]{:S(2)}) collective-permute-start(bf16[8,2,48,1536]{3,2,1,0:T(8,128)(2,1)S(1)} %get-tuple-element.152.refs_0_.refs_1_.refs_2_), channel_id=1, source_target_pairs={{0,8},{8,0},{16,24},{24,16},{32,40},{40,32},{48,56},{56,48},{64,72... | collective-permute-start | bytes 7077896 | tf_op jit(solution)/shard_map/ppermute | solution.py:44
  50.6 3.1 %shard_map.79 = (f32[96,1536]{1,0:T(8,128)S(1)}, f32[96,1536]{1,0:T(8,128)S(1)}) custom-call(s32[2]{0:T(128)S(1)} %pad_add_fusion.at, bf16[1536,768]{1,0:T(8,128)(2,1)S(1)} %get-tuple-element.91.own, bf16[1536,768]{1,0:T(8,128)(2,1)S(1)} %get-tuple-element.92.par, bf16[8,2,48,1536]{3,2,1,0:T(8,128)(2,1)S(1)} %get-tuple-element.152.refs_0_.refs_1_.refs_2_, ...), custom_call_target="tpu_custom_call" | custom-call | flops 905969664 | bytes 8388608 | tf_op jit(solution)/shard_map/pallas_call | solution.py:76
  54.0 2.7 %collective-permute-start.14 = (bf16[96,1536]{1,0:T(8,128)(2,1)S(1)}, bf16[96,1536]{1,0:T(8,128)(2,1)S(1)}, u32[]{:S(2)}, u32[]{:S(2)}) collective-permute-start(bf16[96,1536]{1,0:T(8,128)(2,1)S(1)} %fusion.33), channel_id=1, source_target_pairs={{0,7},{1,0},{2,1},{3,2},{4,3},{5,4},{6,5},{7,6},{8,15},{9,8},{10,9... | collective-permute-start | bytes 884744 | tf_op jit(solution)/shard_map/ppermute | solution.py:66
  56.7 3.6 %shard_map.80 = (f32[96,1536]{1,0:T(8,128)S(1)}, f32[96,1536]{1,0:T(8,128)S(1)}, f32[96,1536]{1,0:T(8,128)S(1)}) custom-call(s32[2]{0:T(128)S(1)} %pad_add_fusion.at, bf16[1536,768]{1,0:T(8,128)(2,1)S(1)} %get-tuple-element.91.own, bf16[1536,768]{1,0:T(8,128)(2,1)S(1)} %get-tuple-element.92.par, ...), custom_call_target="tpu_custom_call" | custom-call | flops 1358954496 | bytes 8388608 | tf_op jit(solution)/shard_map/pallas_call | solution.py:76
  65.8 4.1 %collective-permute-done.15 = bf16[96,1536]{1,0:T(8,128)(2,1)S(1)} collective-permute-done((bf16[96,1536]{1,0:T(8,128)(2,1)S(1)}, bf16[96,1536]{1,0:T(8,128)(2,1)S(1)}, u32[]{:S(2)}, u32[]{:S(2)}) %collective-permute-start.15) | collective-permute-done | bytes 294944 | tf_op jit(solution)/shard_map/ppermute | solution.py:66
  70.6 5.0 %collective-permute-start.18 = (f32[96,1536]{1,0:T(8,128)S(1)}, f32[96,1536]{1,0:T(8,128)S(1)}, u32[]{:S(2)}, u32[]{:S(2)}) collective-permute-start(f32[96,1536]{1,0:T(8,128)S(1)} %fusion.20), channel_id=1, source_target_pairs={{0,8},{8,0},{16,24},{24,16},{32,40},{40,32},{48,56},{56,48},{64,72... | collective-permute-start | bytes 1769480 | tf_op jit(solution)/shard_map/ppermute | solution.py:44
  83.1 4.1 %collective-permute-done.19.refs_1_ = bf16[96,1536]{1,0:T(8,128)(2,1)S(1)} collective-permute-done((bf16[96,1536]{1,0:T(8,128)(2,1)S(1)}, bf16[96,1536]{1,0:T(8,128)(2,1)S(1)}, u32[]{:S(2)}, u32[]{:S(2)}) %collective-permute-start.19) | collective-permute-done | bytes 294944 | tf_op jit(solution)/shard_map/ppermute | solution.py:66
  90.1 3.0 %shard_map.82 = (bf16[96,1536]{1,0:T(8,128)(2,1)S(1)}, bf16[96,1536]{1,0:T(8,128)(2,1)S(1)}) custom-call(s32[2]{0:T(128)S(1)} %pad_add_fusion.at, bf16[768,1536]{1,0:T(8,128)(2,1)S(1)} %get-tuple-element.86.own, bf16[768,1536]{1,0:T(8,128)(2,1)S(1)} %get-tuple-element.87.par, bf16[96,1536]{1,0:T(8,128)(2,1)S(1)} %collective-permute-done.20.refs_0_, ...), custom_call_target="tpu_custom_call" | custom-call | flops 905969664 | bytes 8388608 | tf_op jit(solution)/shard_map/pallas_call | solution.py:76
  93.1 2.8 %collective-permute-done.21.refs_1_ = bf16[96,1536]{1,0:T(8,128)(2,1)S(1)} collective-permute-done((bf16[96,1536]{1,0:T(8,128)(2,1)S(1)}, bf16[96,1536]{1,0:T(8,128)(2,1)S(1)}, u32[]{:S(2)}, u32[]{:S(2)}) %collective-permute-start.21) | collective-permute-done | bytes 294944 | tf_op jit(solution)/shard_map/ppermute | solution.py:66
  98.6 3.0 %shard_map.83 = (bf16[96,1536]{1,0:T(8,128)(2,1)S(1)}, bf16[96,1536]{1,0:T(8,128)(2,1)S(1)}) custom-call(s32[2]{0:T(128)S(1)} %pad_add_fusion.at, bf16[768,1536]{1,0:T(8,128)(2,1)S(1)} %get-tuple-element.86.own, bf16[768,1536]{1,0:T(8,128)(2,1)S(1)} %get-tuple-element.87.par, bf16[96,1536]{1,0:T(8,128)(2,1)S(1)} %collective-permute-done.22.refs_0_, ...), custom_call_target="tpu_custom_call" | custom-call | flops 905969664 | bytes 8388608 | tf_op jit(solution)/shard_map/pallas_call | solution.py:76
  106.4 3.0 %shard_map.84 = (bf16[96,1536]{1,0:T(8,128)(2,1)S(1)}, bf16[96,1536]{1,0:T(8,128)(2,1)S(1)}) custom-call(s32[2]{0:T(128)S(1)} %pad_add_fusion.at, bf16[768,1536]{1,0:T(8,128)(2,1)S(1)} %get-tuple-element.86.own, bf16[768,1536]{1,0:T(8,128)(2,1)S(1)} %get-tuple-element.87.par, bf16[96,1536]{1,0:T(8,128)(2,1)S(1)} %collective-permute-done.24.refs_0_, ...), custom_call_target="tpu_custom_call" | custom-call | flops 905969664 | bytes 8388608 | tf_op jit(solution)/shard_map/pallas_call | solution.py:76
  109.5 4.0 %collective-permute-start.27 = (bf16[768,768]{1,0:T(8,128)(2,1)S(1)}, bf16[768,768]{1,0:T(8,128)(2,1)S(1)}, u32[]{:S(2)}, u32[]{:S(2)}) collective-permute-start(bf16[768,768]{1,0:T(8,128)(2,1)S(1)} %get-tuple-element.169), channel_id=1, source_target_pairs={{0,8},{8,0},{16,24},{24,16},{32,40},{40,32},{48,56},{56,48},{64,72... | collective-permute-start | bytes 3538952 | tf_op jit(solution)/shard_map/ppermute | solution.py:44
  113.5 3.4 %shard_map.85 = bf16[4,4,48,1536]{3,2,1,0:T(8,128)(2,1)S(1)} custom-call(s32[2]{0:T(128)S(1)} %pad_add_fusion.at, bf16[768,1536]{1,0:T(8,128)(2,1)S(1)} %get-tuple-element.86.own, bf16[768,1536]{1,0:T(8,128)(2,1)S(1)} %get-tuple-element.87.par, bf16[96,768]{1,0:T(8,128)(2,1)S(1)} %collective-permute-done.25.b_own, ...), custom_call_target="tpu_custom_call" | custom-call | flops 452984832 | bytes 8388608 | tf_op jit(solution)/shard_map/pallas_call | solution.py:76
  120.2 6.9 %shard_map.86 = (bf16[1536,768]{1,0:T(8,128)(2,1)}, bf16[768,1536]{1,0:T(8,128)(2,1)}) custom-call(s32[2]{0:T(128)S(1)} %pad_add_fusion.at, bf16[768,1536]{1,0:T(8,128)(2,1)S(1)} %bitcast.27, bf16[768,1536]{1,0:T(8,128)(2,1)S(1)} %bitcast.28, bf16[768,768]{1,0:T(8,128)(2,1)S(1)} %get-tuple-element.168.b_own, bf16[768,768]{1,0:T(8,128)(2,1)S(1)} %collective-permute-done.27.b_oth), custom_call_target="tpu_custom_call" | custom-call | flops 3623878656 | bytes 8388608 | tf_op jit(solution)/shard_map/pallas_call | solution.py:76
  127.7 6.3 %collective-permute-done.29 = bf16[4,48,1536]{2,1,0:T(8,128)(2,1)S(1)} collective-permute-done((bf16[4,48,1536]{2,1,0:T(8,128)(2,1)S(1)}, bf16[4,48,1536]{2,1,0:T(8,128)(2,1)S(1)}, u32[]{:S(2)}, u32[]{:S(2)}) %collective-permute-start.29) | collective-permute-done | bytes 589856 | tf_op jit(solution)/shard_map/ppermute | solution.py:62
  134.6 2.9 %collective-permute-start.32 = (bf16[48,1536]{1,0:T(8,128)(2,1)S(1)}, bf16[48,1536]{1,0:T(8,128)(2,1)S(1)}, u32[]{:S(2)}, u32[]{:S(2)}) collective-permute-start(bf16[48,1536]{1,0:T(8,128)(2,1)S(1)} %get-tuple-element.165), channel_id=1, source_target_pairs={{0,64},{8,24},{16,80},{24,40},{32,96},{40,56},{48,112},{56,8},{64,... | collective-permute-start | bytes 442376 | tf_op jit(solution)/shard_map/ppermute | solution.py:53
  (90 shorter events, 54.9 us)
Async XLA Ops:
  5.8 12.7 %collective-permute-start.4 = (bf16[1536,768]{1,0:T(8,128)(2,1)}, bf16[1536,768]{1,0:T(8,128)(2,1)S(1)}, u32[]{:S(2)}, u32[]{:S(2)}) collective-permute-start(bf16[1536,768]{1,0:T(8,128)(2,1)} %in_own.1), channel_id=1, source_target_pairs={{0,8},{8,0},{16,24},{24,16},{32,40},{40,32},{48,56},{56,48},{64,72... | collective-permute-start | bytes 7077896 | tf_op jit(solution)/shard_map/ppermute | solution.py:44
  6.2 12.4 %collective-permute-start.5 = (bf16[768,1536]{1,0:T(8,128)(2,1)}, bf16[768,1536]{1,0:T(8,128)(2,1)}, u32[]{:S(2)}, u32[]{:S(2)}) collective-permute-start(bf16[768,1536]{1,0:T(8,128)(2,1)} %out_own.1), channel_id=1, source_target_pairs={{0,8},{8,0},{16,24},{24,16},{32,40},{40,32},{48,56},{56,48},{64,72... | collective-permute-start | bytes 7077896 | tf_op jit(solution)/shard_map/ppermute | solution.py:44
  14.6 12.3 %collective-permute-start.6 = (bf16[192,1536]{1,0:T(8,128)(2,1)S(1)}, bf16[192,1536]{1,0:T(8,128)(2,1)S(1)}, u32[]{:S(2)}, u32[]{:S(2)}) collective-permute-start(bf16[192,1536]{1,0:T(8,128)(2,1)S(1)} %pad_maximum_fusion.a0), channel_id=1, source_target_pairs={{0,16},{8,72},{16,32},{24,88},{32,48},{40,104},{48,0},{56,120},{64... | collective-permute-start | bytes 1769480 | tf_op jit(solution)/shard_map/ppermute | solution.py:62
  15.6 14.9 %collective-permute-start.7 = (bf16[192,1536]{1,0:T(8,128)(2,1)S(1)}, bf16[192,1536]{1,0:T(8,128)(2,1)S(1)}, u32[]{:S(2)}, u32[]{:S(2)}) collective-permute-start(bf16[192,1536]{1,0:T(8,128)(2,1)S(1)} %pad_maximum_fusion.a0), channel_id=1, source_target_pairs={{0,48},{8,200},{16,0},{24,216},{32,16},{40,232},{48,32},{56,248},{... | collective-permute-start | bytes 1769480 | tf_op jit(solution)/shard_map/ppermute | solution.py:62
  17.3 14.6 %collective-permute-start.8 = (bf16[192,1536]{1,0:T(8,128)(2,1)S(1)}, bf16[192,1536]{1,0:T(8,128)(2,1)S(1)}, u32[]{:S(2)}, u32[]{:S(2)}) collective-permute-start(bf16[192,1536]{1,0:T(8,128)(2,1)S(1)} %pad_maximum_fusion.a0), channel_id=1, source_target_pairs={{0,32},{8,136},{16,48},{24,152},{32,0},{40,168},{48,16},{56,184},{... | collective-permute-start | bytes 1769480 | tf_op jit(solution)/shard_map/ppermute | solution.py:62
  34.8 8.9 %collective-permute-start.9 = (bf16[96,768]{1,0:T(8,128)(2,1)S(1)}, bf16[96,768]{1,0:T(8,128)(2,1)S(1)}, u32[]{:S(2)}, u32[]{:S(2)}) collective-permute-start(bf16[96,768]{1,0:T(8,128)(2,1)S(1)} %get-tuple-element.97), channel_id=1, source_target_pairs={{0,1},{1,2},{2,3},{3,4},{4,5},{5,6},{6,7},{7,0},{8,9},{9,10},{10,1... | collective-permute-start | bytes 442376 | tf_op jit(solution)/shard_map/ppermute | solution.py:66
  36.6 7.2 %collective-permute-start.10 = (bf16[96,768]{1,0:T(8,128)(2,1)S(1)}, bf16[96,768]{1,0:T(8,128)(2,1)S(1)}, u32[]{:S(2)}, u32[]{:S(2)}) collective-permute-start(bf16[96,768]{1,0:T(8,128)(2,1)S(1)} %get-tuple-element.98), channel_id=1, source_target_pairs={{0,7},{1,0},{2,1},{3,2},{4,3},{5,4},{6,5},{7,6},{8,15},{9,8},{10,9... | collective-permute-start | bytes 442376 | tf_op jit(solution)/shard_map/ppermute | solution.py:66
  43.8 9.9 %collective-permute-start.11 = (bf16[96,1536]{1,0:T(8,128)(2,1)S(1)}, bf16[96,1536]{1,0:T(8,128)(2,1)S(1)}, u32[]{:S(2)}, u32[]{:S(2)}) collective-permute-start(bf16[96,1536]{1,0:T(8,128)(2,1)S(1)} %get-tuple-element.106), channel_id=1, source_target_pairs={{0,1},{1,2},{2,3},{3,4},{4,5},{5,6},{6,7},{7,0},{8,9},{9,10},{10,1... | collective-permute-start | bytes 884744 | tf_op jit(solution)/shard_map/ppermute | solution.py:66
  43.9 9.8 %collective-permute-start.12 = (bf16[96,1536]{1,0:T(8,128)(2,1)S(1)}, bf16[96,1536]{1,0:T(8,128)(2,1)S(1)}, u32[]{:S(2)}, u32[]{:S(2)}) collective-permute-start(bf16[96,1536]{1,0:T(8,128)(2,1)S(1)} %get-tuple-element.107), channel_id=1, source_target_pairs={{0,7},{1,0},{2,1},{3,2},{4,3},{5,4},{6,5},{7,6},{8,15},{9,8},{10,9... | collective-permute-start | bytes 884744 | tf_op jit(solution)/shard_map/ppermute | solution.py:66
  46.6 24.0 %collective-permute-start.17 = (bf16[8,2,48,1536]{3,2,1,0:T(8,128)(2,1)S(1)}, bf16[8,2,48,1536]{3,2,1,0:T(8,128)(2,1)S(1)}, u32[]{:S(2)}, u32[]{:S(2)}) collective-permute-start(bf16[8,2,48,1536]{3,2,1,0:T(8,128)(2,1)S(1)} %get-tuple-element.152.refs_0_.refs_1_.refs_2_), channel_id=1, source_target_pairs={{0,8},{8,0},{16,24},{24,16},{32,40},{40,32},{48,56},{56,48},{64,72... | collective-permute-start | bytes 7077896 | tf_op jit(solution)/shard_map/ppermute | solution.py:44
  54.0 8.2 %collective-permute-start.13 = (bf16[96,1536]{1,0:T(8,128)(2,1)S(1)}, bf16[96,1536]{1,0:T(8,128)(2,1)S(1)}, u32[]{:S(2)}, u32[]{:S(2)}) collective-permute-start(bf16[96,1536]{1,0:T(8,128)(2,1)S(1)} %fusion.32), channel_id=1, source_target_pairs={{0,1},{1,2},{2,3},{3,4},{4,5},{5,6},{6,7},{7,0},{8,9},{9,10},{10,1... | collective-permute-start | bytes 884744 | tf_op jit(solution)/shard_map/ppermute | solution.py:66
  54.0 8.2 %collective-permute-start.14 = (bf16[96,1536]{1,0:T(8,128)(2,1)S(1)}, bf16[96,1536]{1,0:T(8,128)(2,1)S(1)}, u32[]{:S(2)}, u32[]{:S(2)}) collective-permute-start(bf16[96,1536]{1,0:T(8,128)(2,1)S(1)} %fusion.33), channel_id=1, source_target_pairs={{0,7},{1,0},{2,1},{3,2},{4,3},{5,4},{6,5},{7,6},{8,15},{9,8},{10,9... | collective-permute-start | bytes 884744 | tf_op jit(solution)/shard_map/ppermute | solution.py:66
  63.1 6.9 %collective-permute-start.15 = (bf16[96,1536]{1,0:T(8,128)(2,1)S(1)}, bf16[96,1536]{1,0:T(8,128)(2,1)S(1)}, u32[]{:S(2)}, u32[]{:S(2)}) collective-permute-start(bf16[96,1536]{1,0:T(8,128)(2,1)S(1)} %fusion.34), channel_id=1, source_target_pairs={{0,1},{1,2},{2,3},{3,4},{4,5},{5,6},{6,7},{7,0},{8,9},{9,10},{10,1... | collective-permute-start | bytes 884744 | tf_op jit(solution)/shard_map/ppermute | solution.py:66
  77.7 9.5 %collective-permute-start.19 = (bf16[96,1536]{1,0:T(8,128)(2,1)S(1)}, bf16[96,1536]{1,0:T(8,128)(2,1)S(1)}, u32[]{:S(2)}, u32[]{:S(2)}) collective-permute-start(bf16[96,1536]{1,0:T(8,128)(2,1)S(1)} %fusion.43.refs_0_), channel_id=1, source_target_pairs={{0,1},{1,2},{2,3},{3,4},{4,5},{5,6},{6,7},{7,0},{8,9},{9,10},{10,1... | collective-permute-start | bytes 884744 | tf_op jit(solution)/shard_map/ppermute | solution.py:66
  78.9 8.5 %collective-permute-start.20 = (bf16[96,1536]{1,0:T(8,128)(2,1)S(1)}, bf16[96,1536]{1,0:T(8,128)(2,1)S(1)}, u32[]{:S(2)}, u32[]{:S(2)}) collective-permute-start(bf16[96,1536]{1,0:T(8,128)(2,1)S(1)} %fusion.43.refs_0_), channel_id=1, source_target_pairs={{0,7},{1,0},{2,1},{3,2},{4,3},{5,4},{6,5},{7,6},{8,15},{9,8},{10,9... | collective-permute-start | bytes 884744 | tf_op jit(solution)/shard_map/ppermute | solution.py:66
  87.4 8.5 %collective-permute-start.21 = (bf16[96,1536]{1,0:T(8,128)(2,1)S(1)}, bf16[96,1536]{1,0:T(8,128)(2,1)S(1)}, u32[]{:S(2)}, u32[]{:S(2)}) collective-permute-start(bf16[96,1536]{1,0:T(8,128)(2,1)S(1)} %collective-permute-done.19.refs_1_), channel_id=1, source_target_pairs={{0,1},{1,2},{2,3},{3,4},{4,5},{5,6},{6,7},{7,0},{8,9},{9,10},{10,1... | collective-permute-start | bytes 884744 | tf_op jit(solution)/shard_map/ppermute | solution.py:66
  88.6 7.4 %collective-permute-start.22 = (bf16[96,1536]{1,0:T(8,128)(2,1)S(1)}, bf16[96,1536]{1,0:T(8,128)(2,1)S(1)}, u32[]{:S(2)}, u32[]{:S(2)}) collective-permute-start(bf16[96,1536]{1,0:T(8,128)(2,1)S(1)} %collective-permute-done.20.refs_0_), channel_id=1, source_target_pairs={{0,7},{1,0},{2,1},{3,2},{4,3},{5,4},{6,5},{7,6},{8,15},{9,8},{10,9... | collective-permute-start | bytes 884744 | tf_op jit(solution)/shard_map/ppermute | solution.py:66
  95.9 7.6 %collective-permute-start.23 = (bf16[96,1536]{1,0:T(8,128)(2,1)S(1)}, bf16[96,1536]{1,0:T(8,128)(2,1)S(1)}, u32[]{:S(2)}, u32[]{:S(2)}) collective-permute-start(bf16[96,1536]{1,0:T(8,128)(2,1)S(1)} %collective-permute-done.21.refs_1_), channel_id=1, source_target_pairs={{0,1},{1,2},{2,3},{3,4},{4,5},{5,6},{6,7},{7,0},{8,9},{9,10},{10,1... | collective-permute-start | bytes 884744 | tf_op jit(solution)/shard_map/ppermute | solution.py:66
  96.5 7.0 %collective-permute-start.24 = (bf16[96,1536]{1,0:T(8,128)(2,1)S(1)}, bf16[96,1536]{1,0:T(8,128)(2,1)S(1)}, u32[]{:S(2)}, u32[]{:S(2)}) collective-permute-start(bf16[96,1536]{1,0:T(8,128)(2,1)S(1)} %collective-permute-done.22.refs_0_), channel_id=1, source_target_pairs={{0,7},{1,0},{2,1},{3,2},{4,3},{5,4},{6,5},{7,6},{8,15},{9,8},{10,9... | collective-permute-start | bytes 884744 | tf_op jit(solution)/shard_map/ppermute | solution.py:66
  109.5 7.4 %collective-permute-start.27 = (bf16[768,768]{1,0:T(8,128)(2,1)S(1)}, bf16[768,768]{1,0:T(8,128)(2,1)S(1)}, u32[]{:S(2)}, u32[]{:S(2)}) collective-permute-start(bf16[768,768]{1,0:T(8,128)(2,1)S(1)} %get-tuple-element.169), channel_id=1, source_target_pairs={{0,8},{8,0},{16,24},{24,16},{32,40},{40,32},{48,56},{56,48},{64,72... | collective-permute-start | bytes 3538952 | tf_op jit(solution)/shard_map/ppermute | solution.py:44
  117.0 10.7 %collective-permute-start.30 = (bf16[4,48,1536]{2,1,0:T(8,128)(2,1)S(1)}, bf16[4,48,1536]{2,1,0:T(8,128)(2,1)S(1)}, u32[]{:S(2)}, u32[]{:S(2)}) collective-permute-start(bf16[4,48,1536]{2,1,0:T(8,128)(2,1)S(1)} %get-tuple-element.161), channel_id=1, source_target_pairs={{0,32},{8,136},{16,48},{24,152},{32,0},{40,168},{48,16},{56,184},{... | collective-permute-start | bytes 1769480 | tf_op jit(solution)/shard_map/ppermute | solution.py:62
  117.5 16.4 %collective-permute-start.29 = (bf16[4,48,1536]{2,1,0:T(8,128)(2,1)S(1)}, bf16[4,48,1536]{2,1,0:T(8,128)(2,1)S(1)}, u32[]{:S(2)}, u32[]{:S(2)}) collective-permute-start(bf16[4,48,1536]{2,1,0:T(8,128)(2,1)S(1)} %get-tuple-element.162), channel_id=1, source_target_pairs={{0,16},{8,72},{16,32},{24,88},{32,48},{40,104},{48,0},{56,120},{64... | collective-permute-start | bytes 1769480 | tf_op jit(solution)/shard_map/ppermute | solution.py:62
  118.3 15.6 %collective-permute-start.28 = (bf16[4,48,1536]{2,1,0:T(8,128)(2,1)S(1)}, bf16[4,48,1536]{2,1,0:T(8,128)(2,1)S(1)}, u32[]{:S(2)}, u32[]{:S(2)}) collective-permute-start(bf16[4,48,1536]{2,1,0:T(8,128)(2,1)S(1)} %get-tuple-element.160), channel_id=1, source_target_pairs={{0,48},{8,200},{16,0},{24,216},{32,16},{40,232},{48,32},{56,248},{... | collective-permute-start | bytes 1769480 | tf_op jit(solution)/shard_map/ppermute | solution.py:62
  134.6 7.2 %collective-permute-start.32 = (bf16[48,1536]{1,0:T(8,128)(2,1)S(1)}, bf16[48,1536]{1,0:T(8,128)(2,1)S(1)}, u32[]{:S(2)}, u32[]{:S(2)}) collective-permute-start(bf16[48,1536]{1,0:T(8,128)(2,1)S(1)} %get-tuple-element.165), channel_id=1, source_target_pairs={{0,64},{8,24},{16,80},{24,40},{32,96},{40,56},{48,112},{56,8},{64,... | collective-permute-start | bytes 442376 | tf_op jit(solution)/shard_map/ppermute | solution.py:53
  (13 other events, 60.9 us)

commit v3 on v2

--- a/solution.py
+++ b/solution.py
@@ -12,7 +12,7 @@
 side = 4
 ring = 8
 tile = 256
-steps = (1, -1, 2)
+steps = (2, 1, -1)
 barrier = lax.optimization_barrier
 
 

time: 146 us -> 148 us (1.014)
    ppermute x6, waiting for transfers between devices: 7.73 us -> 10 us  [first_axis(): return lax.ppermute(array, 'row', pairs)]
  transfers between devices with their start and end apart: 35 -> 35, of which waited for: 19 -> 18; matrix products, arithmetic and copies ran while one was open for 1% -> 1% of each run, Pallas kernels for 26% -> 25%
where the time goes in v3:
time: 148 us
  starting transfers between devices  59.4 us (40%)
  Pallas kernels  40.1 us (27%)
  waiting for transfers between devices  38.9 us (26%)
  other arithmetic  4.43 us (3%)
  local copies, waits for them, and re-layouts  3.71 us (3%)
    pallas_call x12, Pallas kernels, call(): pl.pallas_call(kernel, grid_spec=pltpu.PrefetchScalarGridSpec(num_scalar_...  40.1 us
    ppermute x16, starting transfers between devices, along_z(): lax.ppermute(array, 'col', [(z, (z + by) % ring) for z in range(ring)])  24.9 us
    ppermute x7, starting transfers between devices, swap_cores(): return lax.ppermute(array, 'row', [(r, r ^ 1) for r in range(32)])  19.4 us
    ppermute x16, waiting for transfers between devices, along_z(): lax.ppermute(array, 'col', [(z, (z + by) % ring) for z in range(ring)])  15 us
    ppermute x6, waiting for transfers between devices, second_axis(): return lax.ppermute(array, 'row', pairs)  10.4 us
    ppermute x6, waiting for transfers between devices, first_axis(): return lax.ppermute(array, 'row', pairs)  10 us
    ppermute x6, starting transfers between devices, second_axis(): return lax.ppermute(array, 'row', pairs)  8.63 us
    ppermute x6, starting transfers between devices, first_axis(): return lax.ppermute(array, 'row', pairs)  6.4 us
  transfers between devices with their start and end apart: 35, of which 18 were waited for; matrix products, arithmetic and copies ran while one was open for 1% of the time, Pallas kernels for 25%

profile of v3, /device:TPU:1, one launch (start us, length us, event | category | flops | bytes accessed | tf_op | source)
XLA Modules:
  0.0 147.6 jit_solution(15240649100881827912)
XLA Ops:
  1.6 3.3 %collective-permute-start = (bf16[24,1536]{1,0:T(8,128)(2,1)S(1)}, bf16[24,1536]{1,0:T(8,128)(2,1)S(1)}, u32[]{:S(2)}, u32[]{:S(2)}) collective-permute-start(bf16[24,1536]{1,0:T(8,128)(2,1)S(1)} %get-tuple-element.185), channel_id=1, source_target_pairs={{0,8},{8,0},{16,24},{24,16},{32,40},{40,32},{48,56},{56,48},{64,72... | collective-permute-start | bytes 221192 | tf_op jit(solution)/shard_map/ppermute | solution.py:44
  11.3 3.8 %collective-permute-done.2 = bf16[48,1536]{1,0:T(8,128)(2,1)S(1)} collective-permute-done((bf16[48,1536]{1,0:T(8,128)(2,1)S(1)}, bf16[48,1536]{1,0:T(8,128)(2,1)S(1)}, u32[]{:S(2)}, u32[]{:S(2)}) %collective-permute-start.2) | collective-permute-done | bytes 147488 | tf_op jit(solution)/shard_map/ppermute | solution.py:53
  23.7 5.0 %shard_map.76 = (bf16[1536,768]{1,0:T(8,128)(2,1)S(1)}, bf16[1536,768]{1,0:T(8,128)(2,1)S(1)}, bf16[768,1536]{1,0:T(8,128)(2,1)S(1)}, bf16[768,1536]{1,0:T(8,128)(2,1)S(1)}) custom-call(s32[2]{0:T(128)S(1)} %pad_add_fusion.at, bf16[1536,768]{1,0:T(8,128)(2,1)S(1)} %copy-done, bf16[1536,768]{1,0:T(8,128)(2,1)S(1)} %collective-permute-done.4.in_par, ...), custom_call_target="tpu_custom_call" | custom-call | bytes 8388608 | tf_op jit(solution)/shard_map/pallas_call | solution.py:76
  28.7 3.4 %collective-permute-done.7.a2 = bf16[192,1536]{1,0:T(8,128)(2,1)S(1)} collective-permute-done((bf16[192,1536]{1,0:T(8,128)(2,1)S(1)}, bf16[192,1536]{1,0:T(8,128)(2,1)S(1)}, u32[]{:S(2)}, u32[]{:S(2)}) %collective-permute-start.7) | collective-permute-done | bytes 589856 | tf_op jit(solution)/shard_map/ppermute | solution.py:62
  32.2 3.0 %shard_map.77 = (bf16[8,2,48,1536]{3,2,1,0:T(8,128)(2,1)S(1)}, bf16[96,768]{1,0:T(8,128)(2,1)S(1)}, bf16[96,768]{1,0:T(8,128)(2,1)S(1)}) custom-call(s32[2]{0:T(128)S(1)} %pad_add_fusion.at, bf16[1536,768]{1,0:T(8,128)(2,1)S(1)} %get-tuple-element.91.own, bf16[1536,768]{1,0:T(8,128)(2,1)S(1)} %get-tuple-element.92.par, ...), custom_call_target="tpu_custom_call" | custom-call | flops 452984832 | bytes 8388608 | tf_op jit(solution)/shard_map/pallas_call | solution.py:76
  36.9 4.0 %collective-permute-start.10 = (bf16[96,768]{1,0:T(8,128)(2,1)S(1)}, bf16[96,768]{1,0:T(8,128)(2,1)S(1)}, u32[]{:S(2)}, u32[]{:S(2)}) collective-permute-start(bf16[96,768]{1,0:T(8,128)(2,1)S(1)} %get-tuple-element.98), channel_id=1, source_target_pairs={{0,7},{1,0},{2,1},{3,2},{4,3},{5,4},{6,5},{7,6},{8,15},{9,8},{10,9... | collective-permute-start | bytes 442376 | tf_op jit(solution)/shard_map/ppermute | solution.py:66
  41.0 3.1 %shard_map.78 = (f32[96,1536]{1,0:T(8,128)S(1)}, f32[96,1536]{1,0:T(8,128)S(1)}) custom-call(s32[2]{0:T(128)S(1)} %pad_add_fusion.at, bf16[1536,768]{1,0:T(8,128)(2,1)S(1)} %get-tuple-element.91.own, bf16[1536,768]{1,0:T(8,128)(2,1)S(1)} %get-tuple-element.92.par, bf16[8,2,48,1536]{3,2,1,0:T(8,128)(2,1)S(1)} %get-tuple-element.152.refs_0_.refs_1_.refs_2_, ...), custom_call_target="tpu_custom_call" | custom-call | flops 905969664 | bytes 8388608 | tf_op jit(solution)/shard_map/pallas_call | solution.py:76
  44.3 2.7 %collective-permute-start.12 = (bf16[96,1536]{1,0:T(8,128)(2,1)S(1)}, bf16[96,1536]{1,0:T(8,128)(2,1)S(1)}, u32[]{:S(2)}, u32[]{:S(2)}) collective-permute-start(bf16[96,1536]{1,0:T(8,128)(2,1)S(1)} %get-tuple-element.107), channel_id=1, source_target_pairs={{0,7},{1,0},{2,1},{3,2},{4,3},{5,4},{6,5},{7,6},{8,15},{9,8},{10,9... | collective-permute-start | bytes 884744 | tf_op jit(solution)/shard_map/ppermute | solution.py:66
  47.0 3.2 %collective-permute-start.17 = (bf16[8,2,48,1536]{3,2,1,0:T(8,128)(2,1)S(1)}, bf16[8,2,48,1536]{3,2,1,0:T(8,128)(2,1)S(1)}, u32[]{:S(2)}, u32[]{:S(2)}) collective-permute-start(bf16[8,2,48,1536]{3,2,1,0:T(8,128)(2,1)S(1)} %get-tuple-element.152.refs_0_.refs_1_.refs_2_), channel_id=1, source_target_pairs={{0,8},{8,0},{16,24},{24,16},{32,40},{40,32},{48,56},{56,48},{64,72... | collective-permute-start | bytes 7077896 | tf_op jit(solution)/shard_map/ppermute | solution.py:44
  50.2 3.1 %shard_map.79 = (f32[96,1536]{1,0:T(8,128)S(1)}, f32[96,1536]{1,0:T(8,128)S(1)}) custom-call(s32[2]{0:T(128)S(1)} %pad_add_fusion.at, bf16[1536,768]{1,0:T(8,128)(2,1)S(1)} %get-tuple-element.91.own, bf16[1536,768]{1,0:T(8,128)(2,1)S(1)} %get-tuple-element.92.par, bf16[8,2,48,1536]{3,2,1,0:T(8,128)(2,1)S(1)} %get-tuple-element.152.refs_0_.refs_1_.refs_2_, ...), custom_call_target="tpu_custom_call" | custom-call | flops 905969664 | bytes 8388608 | tf_op jit(solution)/shard_map/pallas_call | solution.py:76
  53.7 2.7 %collective-permute-start.14 = (bf16[96,1536]{1,0:T(8,128)(2,1)S(1)}, bf16[96,1536]{1,0:T(8,128)(2,1)S(1)}, u32[]{:S(2)}, u32[]{:S(2)}) collective-permute-start(bf16[96,1536]{1,0:T(8,128)(2,1)S(1)} %fusion.33), channel_id=1, source_target_pairs={{0,7},{1,0},{2,1},{3,2},{4,3},{5,4},{6,5},{7,6},{8,15},{9,8},{10,9... | collective-permute-start | bytes 884744 | tf_op jit(solution)/shard_map/ppermute | solution.py:66
  56.3 3.6 %shard_map.80 = (f32[96,1536]{1,0:T(8,128)S(1)}, f32[96,1536]{1,0:T(8,128)S(1)}, f32[96,1536]{1,0:T(8,128)S(1)}) custom-call(s32[2]{0:T(128)S(1)} %pad_add_fusion.at, bf16[1536,768]{1,0:T(8,128)(2,1)S(1)} %get-tuple-element.91.own, bf16[1536,768]{1,0:T(8,128)(2,1)S(1)} %get-tuple-element.92.par, ...), custom_call_target="tpu_custom_call" | custom-call | flops 1358954496 | bytes 8388608 | tf_op jit(solution)/shard_map/pallas_call | solution.py:76
  65.4 4.1 %collective-permute-done.15 = bf16[96,1536]{1,0:T(8,128)(2,1)S(1)} collective-permute-done((bf16[96,1536]{1,0:T(8,128)(2,1)S(1)}, bf16[96,1536]{1,0:T(8,128)(2,1)S(1)}, u32[]{:S(2)}, u32[]{:S(2)}) %collective-permute-start.15) | collective-permute-done | bytes 294944 | tf_op jit(solution)/shard_map/ppermute | solution.py:66
  70.2 5.0 %collective-permute-start.18 = (f32[96,1536]{1,0:T(8,128)S(1)}, f32[96,1536]{1,0:T(8,128)S(1)}, u32[]{:S(2)}, u32[]{:S(2)}) collective-permute-start(f32[96,1536]{1,0:T(8,128)S(1)} %fusion.20), channel_id=1, source_target_pairs={{0,8},{8,0},{16,24},{24,16},{32,40},{40,32},{48,56},{56,48},{64,72... | collective-permute-start | bytes 1769480 | tf_op jit(solution)/shard_map/ppermute | solution.py:44
  82.7 4.1 %collective-permute-done.19.refs_1_ = bf16[96,1536]{1,0:T(8,128)(2,1)S(1)} collective-permute-done((bf16[96,1536]{1,0:T(8,128)(2,1)S(1)}, bf16[96,1536]{1,0:T(8,128)(2,1)S(1)}, u32[]{:S(2)}, u32[]{:S(2)}) %collective-permute-start.19) | collective-permute-done | bytes 294944 | tf_op jit(solution)/shard_map/ppermute | solution.py:66
  89.7 3.0 %shard_map.82 = (bf16[96,1536]{1,0:T(8,128)(2,1)S(1)}, bf16[96,1536]{1,0:T(8,128)(2,1)S(1)}) custom-call(s32[2]{0:T(128)S(1)} %pad_add_fusion.at, bf16[768,1536]{1,0:T(8,128)(2,1)S(1)} %get-tuple-element.86.own, bf16[768,1536]{1,0:T(8,128)(2,1)S(1)} %get-tuple-element.87.par, bf16[96,1536]{1,0:T(8,128)(2,1)S(1)} %collective-permute-done.20.refs_0_, ...), custom_call_target="tpu_custom_call" | custom-call | flops 905969664 | bytes 8388608 | tf_op jit(solution)/shard_map/pallas_call | solution.py:76
  92.7 2.8 %collective-permute-done.21.refs_1_ = bf16[96,1536]{1,0:T(8,128)(2,1)S(1)} collective-permute-done((bf16[96,1536]{1,0:T(8,128)(2,1)S(1)}, bf16[96,1536]{1,0:T(8,128)(2,1)S(1)}, u32[]{:S(2)}, u32[]{:S(2)}) %collective-permute-start.21) | collective-permute-done | bytes 294944 | tf_op jit(solution)/shard_map/ppermute | solution.py:66
  98.2 3.0 %shard_map.83 = (bf16[96,1536]{1,0:T(8,128)(2,1)S(1)}, bf16[96,1536]{1,0:T(8,128)(2,1)S(1)}) custom-call(s32[2]{0:T(128)S(1)} %pad_add_fusion.at, bf16[768,1536]{1,0:T(8,128)(2,1)S(1)} %get-tuple-element.86.own, bf16[768,1536]{1,0:T(8,128)(2,1)S(1)} %get-tuple-element.87.par, bf16[96,1536]{1,0:T(8,128)(2,1)S(1)} %collective-permute-done.22.refs_0_, ...), custom_call_target="tpu_custom_call" | custom-call | flops 905969664 | bytes 8388608 | tf_op jit(solution)/shard_map/pallas_call | solution.py:76
  106.0 3.0 %shard_map.84 = (bf16[96,1536]{1,0:T(8,128)(2,1)S(1)}, bf16[96,1536]{1,0:T(8,128)(2,1)S(1)}) custom-call(s32[2]{0:T(128)S(1)} %pad_add_fusion.at, bf16[768,1536]{1,0:T(8,128)(2,1)S(1)} %get-tuple-element.86.own, bf16[768,1536]{1,0:T(8,128)(2,1)S(1)} %get-tuple-element.87.par, bf16[96,1536]{1,0:T(8,128)(2,1)S(1)} %collective-permute-done.24.refs_0_, ...), custom_call_target="tpu_custom_call" | custom-call | flops 905969664 | bytes 8388608 | tf_op jit(solution)/shard_map/pallas_call | solution.py:76
  109.1 4.0 %collective-permute-start.27 = (bf16[768,768]{1,0:T(8,128)(2,1)S(1)}, bf16[768,768]{1,0:T(8,128)(2,1)S(1)}, u32[]{:S(2)}, u32[]{:S(2)}) collective-permute-start(bf16[768,768]{1,0:T(8,128)(2,1)S(1)} %get-tuple-element.169), channel_id=1, source_target_pairs={{0,8},{8,0},{16,24},{24,16},{32,40},{40,32},{48,56},{56,48},{64,72... | collective-permute-start | bytes 3538952 | tf_op jit(solution)/shard_map/ppermute | solution.py:44
  113.1 3.4 %shard_map.85 = bf16[4,4,48,1536]{3,2,1,0:T(8,128)(2,1)S(1)} custom-call(s32[2]{0:T(128)S(1)} %pad_add_fusion.at, bf16[768,1536]{1,0:T(8,128)(2,1)S(1)} %get-tuple-element.86.own, bf16[768,1536]{1,0:T(8,128)(2,1)S(1)} %get-tuple-element.87.par, bf16[96,768]{1,0:T(8,128)(2,1)S(1)} %collective-permute-done.25.b_own, ...), custom_call_target="tpu_custom_call" | custom-call | flops 452984832 | bytes 8388608 | tf_op jit(solution)/shard_map/pallas_call | solution.py:76
  120.0 7.0 %shard_map.86 = (bf16[1536,768]{1,0:T(8,128)(2,1)}, bf16[768,1536]{1,0:T(8,128)(2,1)}) custom-call(s32[2]{0:T(128)S(1)} %pad_add_fusion.at, bf16[768,1536]{1,0:T(8,128)(2,1)S(1)} %bitcast.27, bf16[768,1536]{1,0:T(8,128)(2,1)S(1)} %bitcast.28, bf16[768,768]{1,0:T(8,128)(2,1)S(1)} %get-tuple-element.168.b_own, bf16[768,768]{1,0:T(8,128)(2,1)S(1)} %collective-permute-done.27.b_oth), custom_call_target="tpu_custom_call" | custom-call | flops 3623878656 | bytes 8388608 | tf_op jit(solution)/shard_map/pallas_call | solution.py:76
  127.0 5.5 %collective-permute-done.29 = bf16[4,48,1536]{2,1,0:T(8,128)(2,1)S(1)} collective-permute-done((bf16[4,48,1536]{2,1,0:T(8,128)(2,1)S(1)}, bf16[4,48,1536]{2,1,0:T(8,128)(2,1)S(1)}, u32[]{:S(2)}, u32[]{:S(2)}) %collective-permute-start.29) | collective-permute-done | bytes 589856 | tf_op jit(solution)/shard_map/ppermute | solution.py:62
  142.6 3.4 %collective-permute-start.34 = (bf16[24,1536]{1,0:T(8,128)(2,1)S(1)}, bf16[24,1536]{1,0:T(8,128)(2,1)S(1)}, u32[]{:S(2)}, u32[]{:S(2)}) collective-permute-start(bf16[24,1536]{1,0:T(8,128)(2,1)S(1)} %broadcast_select_fusion.2), channel_id=1, source_target_pairs={{0,8},{8,0},{16,24},{24,16},{32,40},{40,32},{48,56},{56,48},{64,72... | collective-permute-start | bytes 221192 | tf_op jit(solution)/shard_map/ppermute | solution.py:44
  (90 shorter events, 57.6 us)
Async XLA Ops:
  5.8 14.6 %collective-permute-start.4 = (bf16[1536,768]{1,0:T(8,128)(2,1)}, bf16[1536,768]{1,0:T(8,128)(2,1)S(1)}, u32[]{:S(2)}, u32[]{:S(2)}) collective-permute-start(bf16[1536,768]{1,0:T(8,128)(2,1)} %in_own.1), channel_id=1, source_target_pairs={{0,8},{8,0},{16,24},{24,16},{32,40},{40,32},{48,56},{56,48},{64,72... | collective-permute-start | bytes 7077896 | tf_op jit(solution)/shard_map/ppermute | solution.py:44
  6.2 14.2 %collective-permute-start.5 = (bf16[768,1536]{1,0:T(8,128)(2,1)}, bf16[768,1536]{1,0:T(8,128)(2,1)}, u32[]{:S(2)}, u32[]{:S(2)}) collective-permute-start(bf16[768,1536]{1,0:T(8,128)(2,1)} %out_own.1), channel_id=1, source_target_pairs={{0,8},{8,0},{16,24},{24,16},{32,40},{40,32},{48,56},{56,48},{64,72... | collective-permute-start | bytes 7077896 | tf_op jit(solution)/shard_map/ppermute | solution.py:44
  8.1 7.1 %collective-permute-start.2 = (bf16[48,1536]{1,0:T(8,128)(2,1)S(1)}, bf16[48,1536]{1,0:T(8,128)(2,1)S(1)}, u32[]{:S(2)}, u32[]{:S(2)}) collective-permute-start(bf16[48,1536]{1,0:T(8,128)(2,1)S(1)} %shard_map.75), channel_id=1, source_target_pairs={{0,64},{8,24},{16,80},{24,40},{32,96},{40,56},{48,112},{56,8},{64,... | collective-permute-start | bytes 442376 | tf_op jit(solution)/shard_map/ppermute | solution.py:53
  15.2 13.6 %collective-permute-start.6 = (bf16[192,1536]{1,0:T(8,128)(2,1)S(1)}, bf16[192,1536]{1,0:T(8,128)(2,1)S(1)}, u32[]{:S(2)}, u32[]{:S(2)}) collective-permute-start(bf16[192,1536]{1,0:T(8,128)(2,1)S(1)} %pad_maximum_fusion.a0), channel_id=1, source_target_pairs={{0,32},{8,136},{16,48},{24,152},{32,0},{40,168},{48,16},{56,184},{... | collective-permute-start | bytes 1769480 | tf_op jit(solution)/shard_map/ppermute | solution.py:62
  17.7 14.4 %collective-permute-start.7 = (bf16[192,1536]{1,0:T(8,128)(2,1)S(1)}, bf16[192,1536]{1,0:T(8,128)(2,1)S(1)}, u32[]{:S(2)}, u32[]{:S(2)}) collective-permute-start(bf16[192,1536]{1,0:T(8,128)(2,1)S(1)} %pad_maximum_fusion.a0), channel_id=1, source_target_pairs={{0,16},{8,72},{16,32},{24,88},{32,48},{40,104},{48,0},{56,120},{64... | collective-permute-start | bytes 1769480 | tf_op jit(solution)/shard_map/ppermute | solution.py:62
  18.3 13.9 %collective-permute-start.8 = (bf16[192,1536]{1,0:T(8,128)(2,1)S(1)}, bf16[192,1536]{1,0:T(8,128)(2,1)S(1)}, u32[]{:S(2)}, u32[]{:S(2)}) collective-permute-start(bf16[192,1536]{1,0:T(8,128)(2,1)S(1)} %pad_maximum_fusion.a0), channel_id=1, source_target_pairs={{0,48},{8,200},{16,0},{24,216},{32,16},{40,232},{48,32},{56,248},{... | collective-permute-start | bytes 1769480 | tf_op jit(solution)/shard_map/ppermute | solution.py:62
  35.2 8.9 %collective-permute-start.9 = (bf16[96,768]{1,0:T(8,128)(2,1)S(1)}, bf16[96,768]{1,0:T(8,128)(2,1)S(1)}, u32[]{:S(2)}, u32[]{:S(2)}) collective-permute-start(bf16[96,768]{1,0:T(8,128)(2,1)S(1)} %get-tuple-element.97), channel_id=1, source_target_pairs={{0,1},{1,2},{2,3},{3,4},{4,5},{5,6},{6,7},{7,0},{8,9},{9,10},{10,1... | collective-permute-start | bytes 442376 | tf_op jit(solution)/shard_map/ppermute | solution.py:66
  36.9 7.2 %collective-permute-start.10 = (bf16[96,768]{1,0:T(8,128)(2,1)S(1)}, bf16[96,768]{1,0:T(8,128)(2,1)S(1)}, u32[]{:S(2)}, u32[]{:S(2)}) collective-permute-start(bf16[96,768]{1,0:T(8,128)(2,1)S(1)} %get-tuple-element.98), channel_id=1, source_target_pairs={{0,7},{1,0},{2,1},{3,2},{4,3},{5,4},{6,5},{7,6},{8,15},{9,8},{10,9... | collective-permute-start | bytes 442376 | tf_op jit(solution)/shard_map/ppermute | solution.py:66
  44.2 9.1 %collective-permute-start.11 = (bf16[96,1536]{1,0:T(8,128)(2,1)S(1)}, bf16[96,1536]{1,0:T(8,128)(2,1)S(1)}, u32[]{:S(2)}, u32[]{:S(2)}) collective-permute-start(bf16[96,1536]{1,0:T(8,128)(2,1)S(1)} %get-tuple-element.106), channel_id=1, source_target_pairs={{0,1},{1,2},{2,3},{3,4},{4,5},{5,6},{6,7},{7,0},{8,9},{9,10},{10,1... | collective-permute-start | bytes 884744 | tf_op jit(solution)/shard_map/ppermute | solution.py:66
  44.3 9.0 %collective-permute-start.12 = (bf16[96,1536]{1,0:T(8,128)(2,1)S(1)}, bf16[96,1536]{1,0:T(8,128)(2,1)S(1)}, u32[]{:S(2)}, u32[]{:S(2)}) collective-permute-start(bf16[96,1536]{1,0:T(8,128)(2,1)S(1)} %get-tuple-element.107), channel_id=1, source_target_pairs={{0,7},{1,0},{2,1},{3,2},{4,3},{5,4},{6,5},{7,6},{8,15},{9,8},{10,9... | collective-permute-start | bytes 884744 | tf_op jit(solution)/shard_map/ppermute | solution.py:66
  47.0 23.2 %collective-permute-start.17 = (bf16[8,2,48,1536]{3,2,1,0:T(8,128)(2,1)S(1)}, bf16[8,2,48,1536]{3,2,1,0:T(8,128)(2,1)S(1)}, u32[]{:S(2)}, u32[]{:S(2)}) collective-permute-start(bf16[8,2,48,1536]{3,2,1,0:T(8,128)(2,1)S(1)} %get-tuple-element.152.refs_0_.refs_1_.refs_2_), channel_id=1, source_target_pairs={{0,8},{8,0},{16,24},{24,16},{32,40},{40,32},{48,56},{56,48},{64,72... | collective-permute-start | bytes 7077896 | tf_op jit(solution)/shard_map/ppermute | solution.py:44
  53.6 8.2 %collective-permute-start.13 = (bf16[96,1536]{1,0:T(8,128)(2,1)S(1)}, bf16[96,1536]{1,0:T(8,128)(2,1)S(1)}, u32[]{:S(2)}, u32[]{:S(2)}) collective-permute-start(bf16[96,1536]{1,0:T(8,128)(2,1)S(1)} %fusion.32), channel_id=1, source_target_pairs={{0,1},{1,2},{2,3},{3,4},{4,5},{5,6},{6,7},{7,0},{8,9},{9,10},{10,1... | collective-permute-start | bytes 884744 | tf_op jit(solution)/shard_map/ppermute | solution.py:66
  53.7 8.1 %collective-permute-start.14 = (bf16[96,1536]{1,0:T(8,128)(2,1)S(1)}, bf16[96,1536]{1,0:T(8,128)(2,1)S(1)}, u32[]{:S(2)}, u32[]{:S(2)}) collective-permute-start(bf16[96,1536]{1,0:T(8,128)(2,1)S(1)} %fusion.33), channel_id=1, source_target_pairs={{0,7},{1,0},{2,1},{3,2},{4,3},{5,4},{6,5},{7,6},{8,15},{9,8},{10,9... | collective-permute-start | bytes 884744 | tf_op jit(solution)/shard_map/ppermute | solution.py:66
  62.6 6.9 %collective-permute-start.15 = (bf16[96,1536]{1,0:T(8,128)(2,1)S(1)}, bf16[96,1536]{1,0:T(8,128)(2,1)S(1)}, u32[]{:S(2)}, u32[]{:S(2)}) collective-permute-start(bf16[96,1536]{1,0:T(8,128)(2,1)S(1)} %fusion.34), channel_id=1, source_target_pairs={{0,1},{1,2},{2,3},{3,4},{4,5},{5,6},{6,7},{7,0},{8,9},{9,10},{10,1... | collective-permute-start | bytes 884744 | tf_op jit(solution)/shard_map/ppermute | solution.py:66
  77.4 9.5 %collective-permute-start.19 = (bf16[96,1536]{1,0:T(8,128)(2,1)S(1)}, bf16[96,1536]{1,0:T(8,128)(2,1)S(1)}, u32[]{:S(2)}, u32[]{:S(2)}) collective-permute-start(bf16[96,1536]{1,0:T(8,128)(2,1)S(1)} %fusion.43.refs_0_), channel_id=1, source_target_pairs={{0,1},{1,2},{2,3},{3,4},{4,5},{5,6},{6,7},{7,0},{8,9},{9,10},{10,1... | collective-permute-start | bytes 884744 | tf_op jit(solution)/shard_map/ppermute | solution.py:66
  78.5 8.5 %collective-permute-start.20 = (bf16[96,1536]{1,0:T(8,128)(2,1)S(1)}, bf16[96,1536]{1,0:T(8,128)(2,1)S(1)}, u32[]{:S(2)}, u32[]{:S(2)}) collective-permute-start(bf16[96,1536]{1,0:T(8,128)(2,1)S(1)} %fusion.43.refs_0_), channel_id=1, source_target_pairs={{0,7},{1,0},{2,1},{3,2},{4,3},{5,4},{6,5},{7,6},{8,15},{9,8},{10,9... | collective-permute-start | bytes 884744 | tf_op jit(solution)/shard_map/ppermute | solution.py:66
  87.0 8.5 %collective-permute-start.21 = (bf16[96,1536]{1,0:T(8,128)(2,1)S(1)}, bf16[96,1536]{1,0:T(8,128)(2,1)S(1)}, u32[]{:S(2)}, u32[]{:S(2)}) collective-permute-start(bf16[96,1536]{1,0:T(8,128)(2,1)S(1)} %collective-permute-done.19.refs_1_), channel_id=1, source_target_pairs={{0,1},{1,2},{2,3},{3,4},{4,5},{5,6},{6,7},{7,0},{8,9},{9,10},{10,1... | collective-permute-start | bytes 884744 | tf_op jit(solution)/shard_map/ppermute | solution.py:66
  88.2 7.4 %collective-permute-start.22 = (bf16[96,1536]{1,0:T(8,128)(2,1)S(1)}, bf16[96,1536]{1,0:T(8,128)(2,1)S(1)}, u32[]{:S(2)}, u32[]{:S(2)}) collective-permute-start(bf16[96,1536]{1,0:T(8,128)(2,1)S(1)} %collective-permute-done.20.refs_0_), channel_id=1, source_target_pairs={{0,7},{1,0},{2,1},{3,2},{4,3},{5,4},{6,5},{7,6},{8,15},{9,8},{10,9... | collective-permute-start | bytes 884744 | tf_op jit(solution)/shard_map/ppermute | solution.py:66
  95.6 7.6 %collective-permute-start.23 = (bf16[96,1536]{1,0:T(8,128)(2,1)S(1)}, bf16[96,1536]{1,0:T(8,128)(2,1)S(1)}, u32[]{:S(2)}, u32[]{:S(2)}) collective-permute-start(bf16[96,1536]{1,0:T(8,128)(2,1)S(1)} %collective-permute-done.21.refs_1_), channel_id=1, source_target_pairs={{0,1},{1,2},{2,3},{3,4},{4,5},{5,6},{6,7},{7,0},{8,9},{9,10},{10,1... | collective-permute-start | bytes 884744 | tf_op jit(solution)/shard_map/ppermute | solution.py:66
  96.1 7.1 %collective-permute-start.24 = (bf16[96,1536]{1,0:T(8,128)(2,1)S(1)}, bf16[96,1536]{1,0:T(8,128)(2,1)S(1)}, u32[]{:S(2)}, u32[]{:S(2)}) collective-permute-start(bf16[96,1536]{1,0:T(8,128)(2,1)S(1)} %collective-permute-done.22.refs_0_), channel_id=1, source_target_pairs={{0,7},{1,0},{2,1},{3,2},{4,3},{5,4},{6,5},{7,6},{8,15},{9,8},{10,9... | collective-permute-start | bytes 884744 | tf_op jit(solution)/shard_map/ppermute | solution.py:66
  109.1 7.3 %collective-permute-start.27 = (bf16[768,768]{1,0:T(8,128)(2,1)S(1)}, bf16[768,768]{1,0:T(8,128)(2,1)S(1)}, u32[]{:S(2)}, u32[]{:S(2)}) collective-permute-start(bf16[768,768]{1,0:T(8,128)(2,1)S(1)} %get-tuple-element.169), channel_id=1, source_target_pairs={{0,8},{8,0},{16,24},{24,16},{32,40},{40,32},{48,56},{56,48},{64,72... | collective-permute-start | bytes 3538952 | tf_op jit(solution)/shard_map/ppermute | solution.py:44
  116.6 10.4 %collective-permute-start.30 = (bf16[4,48,1536]{2,1,0:T(8,128)(2,1)S(1)}, bf16[4,48,1536]{2,1,0:T(8,128)(2,1)S(1)}, u32[]{:S(2)}, u32[]{:S(2)}) collective-permute-start(bf16[4,48,1536]{2,1,0:T(8,128)(2,1)S(1)} %get-tuple-element.161), channel_id=1, source_target_pairs={{0,16},{8,72},{16,32},{24,88},{32,48},{40,104},{48,0},{56,120},{64... | collective-permute-start | bytes 1769480 | tf_op jit(solution)/shard_map/ppermute | solution.py:62
  117.0 15.5 %collective-permute-start.29 = (bf16[4,48,1536]{2,1,0:T(8,128)(2,1)S(1)}, bf16[4,48,1536]{2,1,0:T(8,128)(2,1)S(1)}, u32[]{:S(2)}, u32[]{:S(2)}) collective-permute-start(bf16[4,48,1536]{2,1,0:T(8,128)(2,1)S(1)} %get-tuple-element.162), channel_id=1, source_target_pairs={{0,48},{8,200},{16,0},{24,216},{32,16},{40,232},{48,32},{56,248},{... | collective-permute-start | bytes 1769480 | tf_op jit(solution)/shard_map/ppermute | solution.py:62
  119.4 14.5 %collective-permute-start.28 = (bf16[4,48,1536]{2,1,0:T(8,128)(2,1)S(1)}, bf16[4,48,1536]{2,1,0:T(8,128)(2,1)S(1)}, u32[]{:S(2)}, u32[]{:S(2)}) collective-permute-start(bf16[4,48,1536]{2,1,0:T(8,128)(2,1)S(1)} %get-tuple-element.160), channel_id=1, source_target_pairs={{0,32},{8,136},{16,48},{24,152},{32,0},{40,168},{48,16},{56,184},{... | collective-permute-start | bytes 1769480 | tf_op jit(solution)/shard_map/ppermute | solution.py:62
  (13 other events, 62.1 us)

commit v4 on v2

--- a/solution.py
+++ b/solution.py
@@ -325,7 +325,8 @@
     pair = make_pair(at, mine, got)
     row = jnp.concatenate([pair] + [first_axis(pair, by) for by in steps])
     row, late = barrier((row, at))
-    blocks = [row] + [second_axis(row, by) for by in steps]
+    far = second_axis(row, steps[2])
+    blocks = [row] + [second_axis(row, by) for by in steps[:2]] + [far]
     one, par_one, two, par_two = turned(late, w_in, in_par, w_out, out_par)
     *blocks, one, par_one = barrier((*blocks, one, par_one))
 

time: 146 us -> 146 us (level)
  no operation moved by 1% of the time
where the time goes in v4:
time: 146 us; the launch traced here: 145 us
  starting transfers between devices  58.1 us (40%)
  Pallas kernels  40.1 us (27%)
  waiting for transfers between devices  38 us (26%)
  other arithmetic  4.43 us (3%)
  local copies, waits for them, and re-layouts  3.71 us (3%)
    pallas_call x12, Pallas kernels, call(): pl.pallas_call(kernel, grid_spec=pltpu.PrefetchScalarGridSpec(num_scalar_...  40.1 us
    ppermute x16, starting transfers between devices, along_z(): lax.ppermute(array, 'col', [(z, (z + by) % ring) for z in range(ring)])  24.9 us
    ppermute x7, starting transfers between devices, swap_cores(): return lax.ppermute(array, 'row', [(r, r ^ 1) for r in range(32)])  18.6 us
    ppermute x16, waiting for transfers between devices, along_z(): lax.ppermute(array, 'col', [(z, (z + by) % ring) for z in range(ring)])  15.1 us
    ppermute x6, waiting for transfers between devices, second_axis(): return lax.ppermute(array, 'row', pairs)  11.8 us
    ppermute x6, waiting for transfers between devices, first_axis(): return lax.ppermute(array, 'row', pairs)  7.73 us
    ppermute x6, starting transfers between devices, first_axis(): return lax.ppermute(array, 'row', pairs)  7.32 us
    ppermute x6, starting transfers between devices, second_axis(): return lax.ppermute(array, 'row', pairs)  7.18 us
  transfers between devices with their start and end apart: 35, of which 19 were waited for; matrix products, arithmetic and copies ran while one was open for 1% of the time, Pallas kernels for 26%

profile of v4, /device:TPU:1, one launch (start us, length us, event | category | flops | bytes accessed | tf_op | source)
XLA Modules:
  0.0 145.4 jit_solution(12954990894463489628)
XLA Ops:
  1.6 3.3 %collective-permute-start = (bf16[24,1536]{1,0:T(8,128)(2,1)S(1)}, bf16[24,1536]{1,0:T(8,128)(2,1)S(1)}, u32[]{:S(2)}, u32[]{:S(2)}) collective-permute-start(bf16[24,1536]{1,0:T(8,128)(2,1)S(1)} %get-tuple-element.185), channel_id=1, source_target_pairs={{0,8},{8,0},{16,24},{24,16},{32,40},{40,32},{48,56},{56,48},{64,72... | collective-permute-start | bytes 221192 | tf_op jit(solution)/shard_map/ppermute | solution.py:44
  9.7 3.1 %collective-permute-done.3 = bf16[48,1536]{1,0:T(8,128)(2,1)S(1)} collective-permute-done((bf16[48,1536]{1,0:T(8,128)(2,1)S(1)}, bf16[48,1536]{1,0:T(8,128)(2,1)S(1)}, u32[]{:S(2)}, u32[]{:S(2)}) %collective-permute-start.3) | collective-permute-done | bytes 147488 | tf_op jit(solution)/shard_map/ppermute | solution.py:53
  21.9 5.0 %shard_map.76 = (bf16[1536,768]{1,0:T(8,128)(2,1)S(1)}, bf16[1536,768]{1,0:T(8,128)(2,1)S(1)}, bf16[768,1536]{1,0:T(8,128)(2,1)S(1)}, bf16[768,1536]{1,0:T(8,128)(2,1)S(1)}) custom-call(s32[2]{0:T(128)S(1)} %pad_add_fusion.at, bf16[1536,768]{1,0:T(8,128)(2,1)S(1)} %copy-done, bf16[1536,768]{1,0:T(8,128)(2,1)S(1)} %collective-permute-done.4.in_par, ...), custom_call_target="tpu_custom_call" | custom-call | bytes 8388608 | tf_op jit(solution)/shard_map/pallas_call | solution.py:76
  26.9 3.6 %collective-permute-done.7.a2 = bf16[192,1536]{1,0:T(8,128)(2,1)S(1)} collective-permute-done((bf16[192,1536]{1,0:T(8,128)(2,1)S(1)}, bf16[192,1536]{1,0:T(8,128)(2,1)S(1)}, u32[]{:S(2)}, u32[]{:S(2)}) %collective-permute-start.7) | collective-permute-done | bytes 589856 | tf_op jit(solution)/shard_map/ppermute | solution.py:62
  31.9 3.0 %shard_map.77 = (bf16[8,2,48,1536]{3,2,1,0:T(8,128)(2,1)S(1)}, bf16[96,768]{1,0:T(8,128)(2,1)S(1)}, bf16[96,768]{1,0:T(8,128)(2,1)S(1)}) custom-call(s32[2]{0:T(128)S(1)} %pad_add_fusion.at, bf16[1536,768]{1,0:T(8,128)(2,1)S(1)} %get-tuple-element.91.own, bf16[1536,768]{1,0:T(8,128)(2,1)S(1)} %get-tuple-element.92.par, ...), custom_call_target="tpu_custom_call" | custom-call | flops 452984832 | bytes 8388608 | tf_op jit(solution)/shard_map/pallas_call | solution.py:76
  36.6 4.0 %collective-permute-start.10 = (bf16[96,768]{1,0:T(8,128)(2,1)S(1)}, bf16[96,768]{1,0:T(8,128)(2,1)S(1)}, u32[]{:S(2)}, u32[]{:S(2)}) collective-permute-start(bf16[96,768]{1,0:T(8,128)(2,1)S(1)} %get-tuple-element.98), channel_id=1, source_target_pairs={{0,7},{1,0},{2,1},{3,2},{4,3},{5,4},{6,5},{7,6},{8,15},{9,8},{10,9... | collective-permute-start | bytes 442376 | tf_op jit(solution)/shard_map/ppermute | solution.py:66
  40.6 3.1 %shard_map.78 = (f32[96,1536]{1,0:T(8,128)S(1)}, f32[96,1536]{1,0:T(8,128)S(1)}) custom-call(s32[2]{0:T(128)S(1)} %pad_add_fusion.at, bf16[1536,768]{1,0:T(8,128)(2,1)S(1)} %get-tuple-element.91.own, bf16[1536,768]{1,0:T(8,128)(2,1)S(1)} %get-tuple-element.92.par, bf16[8,2,48,1536]{3,2,1,0:T(8,128)(2,1)S(1)} %get-tuple-element.152.refs_0_.refs_1_.refs_2_, ...), custom_call_target="tpu_custom_call" | custom-call | flops 905969664 | bytes 8388608 | tf_op jit(solution)/shard_map/pallas_call | solution.py:76
  43.9 2.7 %collective-permute-start.12 = (bf16[96,1536]{1,0:T(8,128)(2,1)S(1)}, bf16[96,1536]{1,0:T(8,128)(2,1)S(1)}, u32[]{:S(2)}, u32[]{:S(2)}) collective-permute-start(bf16[96,1536]{1,0:T(8,128)(2,1)S(1)} %get-tuple-element.107), channel_id=1, source_target_pairs={{0,7},{1,0},{2,1},{3,2},{4,3},{5,4},{6,5},{7,6},{8,15},{9,8},{10,9... | collective-permute-start | bytes 884744 | tf_op jit(solution)/shard_map/ppermute | solution.py:66
  46.6 4.0 %collective-permute-start.17 = (bf16[8,2,48,1536]{3,2,1,0:T(8,128)(2,1)S(1)}, bf16[8,2,48,1536]{3,2,1,0:T(8,128)(2,1)S(1)}, u32[]{:S(2)}, u32[]{:S(2)}) collective-permute-start(bf16[8,2,48,1536]{3,2,1,0:T(8,128)(2,1)S(1)} %get-tuple-element.152.refs_0_.refs_1_.refs_2_), channel_id=1, source_target_pairs={{0,8},{8,0},{16,24},{24,16},{32,40},{40,32},{48,56},{56,48},{64,72... | collective-permute-start | bytes 7077896 | tf_op jit(solution)/shard_map/ppermute | solution.py:44
  50.6 3.1 %shard_map.79 = (f32[96,1536]{1,0:T(8,128)S(1)}, f32[96,1536]{1,0:T(8,128)S(1)}) custom-call(s32[2]{0:T(128)S(1)} %pad_add_fusion.at, bf16[1536,768]{1,0:T(8,128)(2,1)S(1)} %get-tuple-element.91.own, bf16[1536,768]{1,0:T(8,128)(2,1)S(1)} %get-tuple-element.92.par, bf16[8,2,48,1536]{3,2,1,0:T(8,128)(2,1)S(1)} %get-tuple-element.152.refs_0_.refs_1_.refs_2_, ...), custom_call_target="tpu_custom_call" | custom-call | flops 905969664 | bytes 8388608 | tf_op jit(solution)/shard_map/pallas_call | solution.py:76
  54.0 2.7 %collective-permute-start.14 = (bf16[96,1536]{1,0:T(8,128)(2,1)S(1)}, bf16[96,1536]{1,0:T(8,128)(2,1)S(1)}, u32[]{:S(2)}, u32[]{:S(2)}) collective-permute-start(bf16[96,1536]{1,0:T(8,128)(2,1)S(1)} %fusion.33), channel_id=1, source_target_pairs={{0,7},{1,0},{2,1},{3,2},{4,3},{5,4},{6,5},{7,6},{8,15},{9,8},{10,9... | collective-permute-start | bytes 884744 | tf_op jit(solution)/shard_map/ppermute | solution.py:66
  56.7 3.6 %shard_map.80 = (f32[96,1536]{1,0:T(8,128)S(1)}, f32[96,1536]{1,0:T(8,128)S(1)}, f32[96,1536]{1,0:T(8,128)S(1)}) custom-call(s32[2]{0:T(128)S(1)} %pad_add_fusion.at, bf16[1536,768]{1,0:T(8,128)(2,1)S(1)} %get-tuple-element.91.own, bf16[1536,768]{1,0:T(8,128)(2,1)S(1)} %get-tuple-element.92.par, ...), custom_call_target="tpu_custom_call" | custom-call | flops 1358954496 | bytes 8388608 | tf_op jit(solution)/shard_map/pallas_call | solution.py:76
  65.8 4.1 %collective-permute-done.15 = bf16[96,1536]{1,0:T(8,128)(2,1)S(1)} collective-permute-done((bf16[96,1536]{1,0:T(8,128)(2,1)S(1)}, bf16[96,1536]{1,0:T(8,128)(2,1)S(1)}, u32[]{:S(2)}, u32[]{:S(2)}) %collective-permute-start.15) | collective-permute-done | bytes 294944 | tf_op jit(solution)/shard_map/ppermute | solution.py:66
  70.6 5.0 %collective-permute-start.18 = (f32[96,1536]{1,0:T(8,128)S(1)}, f32[96,1536]{1,0:T(8,128)S(1)}, u32[]{:S(2)}, u32[]{:S(2)}) collective-permute-start(f32[96,1536]{1,0:T(8,128)S(1)} %fusion.20), channel_id=1, source_target_pairs={{0,8},{8,0},{16,24},{24,16},{32,40},{40,32},{48,56},{56,48},{64,72... | collective-permute-start | bytes 1769480 | tf_op jit(solution)/shard_map/ppermute | solution.py:44
  83.1 4.1 %collective-permute-done.19.refs_1_ = bf16[96,1536]{1,0:T(8,128)(2,1)S(1)} collective-permute-done((bf16[96,1536]{1,0:T(8,128)(2,1)S(1)}, bf16[96,1536]{1,0:T(8,128)(2,1)S(1)}, u32[]{:S(2)}, u32[]{:S(2)}) %collective-permute-start.19) | collective-permute-done | bytes 294944 | tf_op jit(solution)/shard_map/ppermute | solution.py:66
  90.1 3.0 %shard_map.82 = (bf16[96,1536]{1,0:T(8,128)(2,1)S(1)}, bf16[96,1536]{1,0:T(8,128)(2,1)S(1)}) custom-call(s32[2]{0:T(128)S(1)} %pad_add_fusion.at, bf16[768,1536]{1,0:T(8,128)(2,1)S(1)} %get-tuple-element.86.own, bf16[768,1536]{1,0:T(8,128)(2,1)S(1)} %get-tuple-element.87.par, bf16[96,1536]{1,0:T(8,128)(2,1)S(1)} %collective-permute-done.20.refs_0_, ...), custom_call_target="tpu_custom_call" | custom-call | flops 905969664 | bytes 8388608 | tf_op jit(solution)/shard_map/pallas_call | solution.py:76
  93.1 2.8 %collective-permute-done.21.refs_1_ = bf16[96,1536]{1,0:T(8,128)(2,1)S(1)} collective-permute-done((bf16[96,1536]{1,0:T(8,128)(2,1)S(1)}, bf16[96,1536]{1,0:T(8,128)(2,1)S(1)}, u32[]{:S(2)}, u32[]{:S(2)}) %collective-permute-start.21) | collective-permute-done | bytes 294944 | tf_op jit(solution)/shard_map/ppermute | solution.py:66
  98.6 3.0 %shard_map.83 = (bf16[96,1536]{1,0:T(8,128)(2,1)S(1)}, bf16[96,1536]{1,0:T(8,128)(2,1)S(1)}) custom-call(s32[2]{0:T(128)S(1)} %pad_add_fusion.at, bf16[768,1536]{1,0:T(8,128)(2,1)S(1)} %get-tuple-element.86.own, bf16[768,1536]{1,0:T(8,128)(2,1)S(1)} %get-tuple-element.87.par, bf16[96,1536]{1,0:T(8,128)(2,1)S(1)} %collective-permute-done.22.refs_0_, ...), custom_call_target="tpu_custom_call" | custom-call | flops 905969664 | bytes 8388608 | tf_op jit(solution)/shard_map/pallas_call | solution.py:76
  106.4 3.0 %shard_map.84 = (bf16[96,1536]{1,0:T(8,128)(2,1)S(1)}, bf16[96,1536]{1,0:T(8,128)(2,1)S(1)}) custom-call(s32[2]{0:T(128)S(1)} %pad_add_fusion.at, bf16[768,1536]{1,0:T(8,128)(2,1)S(1)} %get-tuple-element.86.own, bf16[768,1536]{1,0:T(8,128)(2,1)S(1)} %get-tuple-element.87.par, bf16[96,1536]{1,0:T(8,128)(2,1)S(1)} %collective-permute-done.24.refs_0_, ...), custom_call_target="tpu_custom_call" | custom-call | flops 905969664 | bytes 8388608 | tf_op jit(solution)/shard_map/pallas_call | solution.py:76
  109.5 4.0 %collective-permute-start.27 = (bf16[768,768]{1,0:T(8,128)(2,1)S(1)}, bf16[768,768]{1,0:T(8,128)(2,1)S(1)}, u32[]{:S(2)}, u32[]{:S(2)}) collective-permute-start(bf16[768,768]{1,0:T(8,128)(2,1)S(1)} %get-tuple-element.169), channel_id=1, source_target_pairs={{0,8},{8,0},{16,24},{24,16},{32,40},{40,32},{48,56},{56,48},{64,72... | collective-permute-start | bytes 3538952 | tf_op jit(solution)/shard_map/ppermute | solution.py:44
  113.5 3.4 %shard_map.85 = bf16[4,4,48,1536]{3,2,1,0:T(8,128)(2,1)S(1)} custom-call(s32[2]{0:T(128)S(1)} %pad_add_fusion.at, bf16[768,1536]{1,0:T(8,128)(2,1)S(1)} %get-tuple-element.86.own, bf16[768,1536]{1,0:T(8,128)(2,1)S(1)} %get-tuple-element.87.par, bf16[96,768]{1,0:T(8,128)(2,1)S(1)} %collective-permute-done.25.b_own, ...), custom_call_target="tpu_custom_call" | custom-call | flops 452984832 | bytes 8388608 | tf_op jit(solution)/shard_map/pallas_call | solution.py:76
  120.2 6.9 %shard_map.86 = (bf16[1536,768]{1,0:T(8,128)(2,1)}, bf16[768,1536]{1,0:T(8,128)(2,1)}) custom-call(s32[2]{0:T(128)S(1)} %pad_add_fusion.at, bf16[768,1536]{1,0:T(8,128)(2,1)S(1)} %bitcast.27, bf16[768,1536]{1,0:T(8,128)(2,1)S(1)} %bitcast.28, bf16[768,768]{1,0:T(8,128)(2,1)S(1)} %get-tuple-element.168.b_own, bf16[768,768]{1,0:T(8,128)(2,1)S(1)} %collective-permute-done.27.b_oth), custom_call_target="tpu_custom_call" | custom-call | flops 3623878656 | bytes 8388608 | tf_op jit(solution)/shard_map/pallas_call | solution.py:76
  127.7 6.3 %collective-permute-done.29 = bf16[4,48,1536]{2,1,0:T(8,128)(2,1)S(1)} collective-permute-done((bf16[4,48,1536]{2,1,0:T(8,128)(2,1)S(1)}, bf16[4,48,1536]{2,1,0:T(8,128)(2,1)S(1)}, u32[]{:S(2)}, u32[]{:S(2)}) %collective-permute-start.29) | collective-permute-done | bytes 589856 | tf_op jit(solution)/shard_map/ppermute | solution.py:62
  134.6 2.9 %collective-permute-start.32 = (bf16[48,1536]{1,0:T(8,128)(2,1)S(1)}, bf16[48,1536]{1,0:T(8,128)(2,1)S(1)}, u32[]{:S(2)}, u32[]{:S(2)}) collective-permute-start(bf16[48,1536]{1,0:T(8,128)(2,1)S(1)} %get-tuple-element.165), channel_id=1, source_target_pairs={{0,64},{8,24},{16,80},{24,40},{32,96},{40,56},{48,112},{56,8},{64,... | collective-permute-start | bytes 442376 | tf_op jit(solution)/shard_map/ppermute | solution.py:53
  (90 shorter events, 54.9 us)
Async XLA Ops:
  5.8 12.7 %collective-permute-start.4 = (bf16[1536,768]{1,0:T(8,128)(2,1)}, bf16[1536,768]{1,0:T(8,128)(2,1)S(1)}, u32[]{:S(2)}, u32[]{:S(2)}) collective-permute-start(bf16[1536,768]{1,0:T(8,128)(2,1)} %in_own.1), channel_id=1, source_target_pairs={{0,8},{8,0},{16,24},{24,16},{32,40},{40,32},{48,56},{56,48},{64,72... | collective-permute-start | bytes 7077896 | tf_op jit(solution)/shard_map/ppermute | solution.py:44
  6.2 12.4 %collective-permute-start.5 = (bf16[768,1536]{1,0:T(8,128)(2,1)}, bf16[768,1536]{1,0:T(8,128)(2,1)}, u32[]{:S(2)}, u32[]{:S(2)}) collective-permute-start(bf16[768,1536]{1,0:T(8,128)(2,1)} %out_own.1), channel_id=1, source_target_pairs={{0,8},{8,0},{16,24},{24,16},{32,40},{40,32},{48,56},{56,48},{64,72... | collective-permute-start | bytes 7077896 | tf_op jit(solution)/shard_map/ppermute | solution.py:44
  14.6 12.3 %collective-permute-start.6 = (bf16[192,1536]{1,0:T(8,128)(2,1)S(1)}, bf16[192,1536]{1,0:T(8,128)(2,1)S(1)}, u32[]{:S(2)}, u32[]{:S(2)}) collective-permute-start(bf16[192,1536]{1,0:T(8,128)(2,1)S(1)} %pad_maximum_fusion.a0), channel_id=1, source_target_pairs={{0,16},{8,72},{16,32},{24,88},{32,48},{40,104},{48,0},{56,120},{64... | collective-permute-start | bytes 1769480 | tf_op jit(solution)/shard_map/ppermute | solution.py:62
  15.6 14.9 %collective-permute-start.7 = (bf16[192,1536]{1,0:T(8,128)(2,1)S(1)}, bf16[192,1536]{1,0:T(8,128)(2,1)S(1)}, u32[]{:S(2)}, u32[]{:S(2)}) collective-permute-start(bf16[192,1536]{1,0:T(8,128)(2,1)S(1)} %pad_maximum_fusion.a0), channel_id=1, source_target_pairs={{0,48},{8,200},{16,0},{24,216},{32,16},{40,232},{48,32},{56,248},{... | collective-permute-start | bytes 1769480 | tf_op jit(solution)/shard_map/ppermute | solution.py:62
  17.3 14.6 %collective-permute-start.8 = (bf16[192,1536]{1,0:T(8,128)(2,1)S(1)}, bf16[192,1536]{1,0:T(8,128)(2,1)S(1)}, u32[]{:S(2)}, u32[]{:S(2)}) collective-permute-start(bf16[192,1536]{1,0:T(8,128)(2,1)S(1)} %pad_maximum_fusion.a0), channel_id=1, source_target_pairs={{0,32},{8,136},{16,48},{24,152},{32,0},{40,168},{48,16},{56,184},{... | collective-permute-start | bytes 1769480 | tf_op jit(solution)/shard_map/ppermute | solution.py:62
  34.8 8.9 %collective-permute-start.9 = (bf16[96,768]{1,0:T(8,128)(2,1)S(1)}, bf16[96,768]{1,0:T(8,128)(2,1)S(1)}, u32[]{:S(2)}, u32[]{:S(2)}) collective-permute-start(bf16[96,768]{1,0:T(8,128)(2,1)S(1)} %get-tuple-element.97), channel_id=1, source_target_pairs={{0,1},{1,2},{2,3},{3,4},{4,5},{5,6},{6,7},{7,0},{8,9},{9,10},{10,1... | collective-permute-start | bytes 442376 | tf_op jit(solution)/shard_map/ppermute | solution.py:66
  36.6 7.2 %collective-permute-start.10 = (bf16[96,768]{1,0:T(8,128)(2,1)S(1)}, bf16[96,768]{1,0:T(8,128)(2,1)S(1)}, u32[]{:S(2)}, u32[]{:S(2)}) collective-permute-start(bf16[96,768]{1,0:T(8,128)(2,1)S(1)} %get-tuple-element.98), channel_id=1, source_target_pairs={{0,7},{1,0},{2,1},{3,2},{4,3},{5,4},{6,5},{7,6},{8,15},{9,8},{10,9... | collective-permute-start | bytes 442376 | tf_op jit(solution)/shard_map/ppermute | solution.py:66
  43.8 9.9 %collective-permute-start.11 = (bf16[96,1536]{1,0:T(8,128)(2,1)S(1)}, bf16[96,1536]{1,0:T(8,128)(2,1)S(1)}, u32[]{:S(2)}, u32[]{:S(2)}) collective-permute-start(bf16[96,1536]{1,0:T(8,128)(2,1)S(1)} %get-tuple-element.106), channel_id=1, source_target_pairs={{0,1},{1,2},{2,3},{3,4},{4,5},{5,6},{6,7},{7,0},{8,9},{9,10},{10,1... | collective-permute-start | bytes 884744 | tf_op jit(solution)/shard_map/ppermute | solution.py:66
  43.9 9.8 %collective-permute-start.12 = (bf16[96,1536]{1,0:T(8,128)(2,1)S(1)}, bf16[96,1536]{1,0:T(8,128)(2,1)S(1)}, u32[]{:S(2)}, u32[]{:S(2)}) collective-permute-start(bf16[96,1536]{1,0:T(8,128)(2,1)S(1)} %get-tuple-element.107), channel_id=1, source_target_pairs={{0,7},{1,0},{2,1},{3,2},{4,3},{5,4},{6,5},{7,6},{8,15},{9,8},{10,9... | collective-permute-start | bytes 884744 | tf_op jit(solution)/shard_map/ppermute | solution.py:66
  46.6 24.0 %collective-permute-start.17 = (bf16[8,2,48,1536]{3,2,1,0:T(8,128)(2,1)S(1)}, bf16[8,2,48,1536]{3,2,1,0:T(8,128)(2,1)S(1)}, u32[]{:S(2)}, u32[]{:S(2)}) collective-permute-start(bf16[8,2,48,1536]{3,2,1,0:T(8,128)(2,1)S(1)} %get-tuple-element.152.refs_0_.refs_1_.refs_2_), channel_id=1, source_target_pairs={{0,8},{8,0},{16,24},{24,16},{32,40},{40,32},{48,56},{56,48},{64,72... | collective-permute-start | bytes 7077896 | tf_op jit(solution)/shard_map/ppermute | solution.py:44
  54.0 8.2 %collective-permute-start.13 = (bf16[96,1536]{1,0:T(8,128)(2,1)S(1)}, bf16[96,1536]{1,0:T(8,128)(2,1)S(1)}, u32[]{:S(2)}, u32[]{:S(2)}) collective-permute-start(bf16[96,1536]{1,0:T(8,128)(2,1)S(1)} %fusion.32), channel_id=1, source_target_pairs={{0,1},{1,2},{2,3},{3,4},{4,5},{5,6},{6,7},{7,0},{8,9},{9,10},{10,1... | collective-permute-start | bytes 884744 | tf_op jit(solution)/shard_map/ppermute | solution.py:66
  54.0 8.2 %collective-permute-start.14 = (bf16[96,1536]{1,0:T(8,128)(2,1)S(1)}, bf16[96,1536]{1,0:T(8,128)(2,1)S(1)}, u32[]{:S(2)}, u32[]{:S(2)}) collective-permute-start(bf16[96,1536]{1,0:T(8,128)(2,1)S(1)} %fusion.33), channel_id=1, source_target_pairs={{0,7},{1,0},{2,1},{3,2},{4,3},{5,4},{6,5},{7,6},{8,15},{9,8},{10,9... | collective-permute-start | bytes 884744 | tf_op jit(solution)/shard_map/ppermute | solution.py:66
  63.1 6.9 %collective-permute-start.15 = (bf16[96,1536]{1,0:T(8,128)(2,1)S(1)}, bf16[96,1536]{1,0:T(8,128)(2,1)S(1)}, u32[]{:S(2)}, u32[]{:S(2)}) collective-permute-start(bf16[96,1536]{1,0:T(8,128)(2,1)S(1)} %fusion.34), channel_id=1, source_target_pairs={{0,1},{1,2},{2,3},{3,4},{4,5},{5,6},{6,7},{7,0},{8,9},{9,10},{10,1... | collective-permute-start | bytes 884744 | tf_op jit(solution)/shard_map/ppermute | solution.py:66
  77.7 9.5 %collective-permute-start.19 = (bf16[96,1536]{1,0:T(8,128)(2,1)S(1)}, bf16[96,1536]{1,0:T(8,128)(2,1)S(1)}, u32[]{:S(2)}, u32[]{:S(2)}) collective-permute-start(bf16[96,1536]{1,0:T(8,128)(2,1)S(1)} %fusion.43.refs_0_), channel_id=1, source_target_pairs={{0,1},{1,2},{2,3},{3,4},{4,5},{5,6},{6,7},{7,0},{8,9},{9,10},{10,1... | collective-permute-start | bytes 884744 | tf_op jit(solution)/shard_map/ppermute | solution.py:66
  78.9 8.5 %collective-permute-start.20 = (bf16[96,1536]{1,0:T(8,128)(2,1)S(1)}, bf16[96,1536]{1,0:T(8,128)(2,1)S(1)}, u32[]{:S(2)}, u32[]{:S(2)}) collective-permute-start(bf16[96,1536]{1,0:T(8,128)(2,1)S(1)} %fusion.43.refs_0_), channel_id=1, source_target_pairs={{0,7},{1,0},{2,1},{3,2},{4,3},{5,4},{6,5},{7,6},{8,15},{9,8},{10,9... | collective-permute-start | bytes 884744 | tf_op jit(solution)/shard_map/ppermute | solution.py:66
  87.4 8.5 %collective-permute-start.21 = (bf16[96,1536]{1,0:T(8,128)(2,1)S(1)}, bf16[96,1536]{1,0:T(8,128)(2,1)S(1)}, u32[]{:S(2)}, u32[]{:S(2)}) collective-permute-start(bf16[96,1536]{1,0:T(8,128)(2,1)S(1)} %collective-permute-done.19.refs_1_), channel_id=1, source_target_pairs={{0,1},{1,2},{2,3},{3,4},{4,5},{5,6},{6,7},{7,0},{8,9},{9,10},{10,1... | collective-permute-start | bytes 884744 | tf_op jit(solution)/shard_map/ppermute | solution.py:66
  88.6 7.4 %collective-permute-start.22 = (bf16[96,1536]{1,0:T(8,128)(2,1)S(1)}, bf16[96,1536]{1,0:T(8,128)(2,1)S(1)}, u32[]{:S(2)}, u32[]{:S(2)}) collective-permute-start(bf16[96,1536]{1,0:T(8,128)(2,1)S(1)} %collective-permute-done.20.refs_0_), channel_id=1, source_target_pairs={{0,7},{1,0},{2,1},{3,2},{4,3},{5,4},{6,5},{7,6},{8,15},{9,8},{10,9... | collective-permute-start | bytes 884744 | tf_op jit(solution)/shard_map/ppermute | solution.py:66
  95.9 7.6 %collective-permute-start.23 = (bf16[96,1536]{1,0:T(8,128)(2,1)S(1)}, bf16[96,1536]{1,0:T(8,128)(2,1)S(1)}, u32[]{:S(2)}, u32[]{:S(2)}) collective-permute-start(bf16[96,1536]{1,0:T(8,128)(2,1)S(1)} %collective-permute-done.21.refs_1_), channel_id=1, source_target_pairs={{0,1},{1,2},{2,3},{3,4},{4,5},{5,6},{6,7},{7,0},{8,9},{9,10},{10,1... | collective-permute-start | bytes 884744 | tf_op jit(solution)/shard_map/ppermute | solution.py:66
  96.5 7.0 %collective-permute-start.24 = (bf16[96,1536]{1,0:T(8,128)(2,1)S(1)}, bf16[96,1536]{1,0:T(8,128)(2,1)S(1)}, u32[]{:S(2)}, u32[]{:S(2)}) collective-permute-start(bf16[96,1536]{1,0:T(8,128)(2,1)S(1)} %collective-permute-done.22.refs_0_), channel_id=1, source_target_pairs={{0,7},{1,0},{2,1},{3,2},{4,3},{5,4},{6,5},{7,6},{8,15},{9,8},{10,9... | collective-permute-start | bytes 884744 | tf_op jit(solution)/shard_map/ppermute | solution.py:66
  109.5 7.4 %collective-permute-start.27 = (bf16[768,768]{1,0:T(8,128)(2,1)S(1)}, bf16[768,768]{1,0:T(8,128)(2,1)S(1)}, u32[]{:S(2)}, u32[]{:S(2)}) collective-permute-start(bf16[768,768]{1,0:T(8,128)(2,1)S(1)} %get-tuple-element.169), channel_id=1, source_target_pairs={{0,8},{8,0},{16,24},{24,16},{32,40},{40,32},{48,56},{56,48},{64,72... | collective-permute-start | bytes 3538952 | tf_op jit(solution)/shard_map/ppermute | solution.py:44
  117.0 10.7 %collective-permute-start.30 = (bf16[4,48,1536]{2,1,0:T(8,128)(2,1)S(1)}, bf16[4,48,1536]{2,1,0:T(8,128)(2,1)S(1)}, u32[]{:S(2)}, u32[]{:S(2)}) collective-permute-start(bf16[4,48,1536]{2,1,0:T(8,128)(2,1)S(1)} %get-tuple-element.161), channel_id=1, source_target_pairs={{0,32},{8,136},{16,48},{24,152},{32,0},{40,168},{48,16},{56,184},{... | collective-permute-start | bytes 1769480 | tf_op jit(solution)/shard_map/ppermute | solution.py:62
  117.5 16.4 %collective-permute-start.29 = (bf16[4,48,1536]{2,1,0:T(8,128)(2,1)S(1)}, bf16[4,48,1536]{2,1,0:T(8,128)(2,1)S(1)}, u32[]{:S(2)}, u32[]{:S(2)}) collective-permute-start(bf16[4,48,1536]{2,1,0:T(8,128)(2,1)S(1)} %get-tuple-element.162), channel_id=1, source_target_pairs={{0,16},{8,72},{16,32},{24,88},{32,48},{40,104},{48,0},{56,120},{64... | collective-permute-start | bytes 1769480 | tf_op jit(solution)/shard_map/ppermute | solution.py:62
  118.3 15.6 %collective-permute-start.28 = (bf16[4,48,1536]{2,1,0:T(8,128)(2,1)S(1)}, bf16[4,48,1536]{2,1,0:T(8,128)(2,1)S(1)}, u32[]{:S(2)}, u32[]{:S(2)}) collective-permute-start(bf16[4,48,1536]{2,1,0:T(8,128)(2,1)S(1)} %get-tuple-element.160), channel_id=1, source_target_pairs={{0,48},{8,200},{16,0},{24,216},{32,16},{40,232},{48,32},{56,248},{... | collective-permute-start | bytes 1769480 | tf_op jit(solution)/shard_map/ppermute | solution.py:62
  134.6 7.2 %collective-permute-start.32 = (bf16[48,1536]{1,0:T(8,128)(2,1)S(1)}, bf16[48,1536]{1,0:T(8,128)(2,1)S(1)}, u32[]{:S(2)}, u32[]{:S(2)}) collective-permute-start(bf16[48,1536]{1,0:T(8,128)(2,1)S(1)} %get-tuple-element.165), channel_id=1, source_target_pairs={{0,64},{8,24},{16,80},{24,40},{32,96},{40,56},{48,112},{56,8},{64,... | collective-permute-start | bytes 442376 | tf_op jit(solution)/shard_map/ppermute | solution.py:53
  (13 other events, 60.9 us)

commit v5 on v2

--- a/solution.py
+++ b/solution.py
@@ -98,22 +98,19 @@
     return pl.BlockSpec(dims, lambda j, at: (0,) * len(dims))
 
 
-def pair_kernel(at, mine, got, out):
-    a, b = mine[...].astype(f32), got[...].astype(f32)
+def pair_kernel(at, inputs, out_grad, got_in, got_grad, out):
     core = at[0]
 
-    @pl.when(core == 0)
-    def _():
-        out[...] = jnp.concatenate([a, b]).astype(bf16)
-
-    @pl.when(core == 1)
-    def _():
-        out[...] = jnp.concatenate([b, a]).astype(bf16)
-
-
-def make_pair(at, mine, got):
-    return call(
-        pair_kernel, at, (mine, got), [fixed(24, 1536)] * 2, fixed(48, 1536), shape(48, 1536), (1,), 0
+    def join(a, b):
+        out[...] = jnp.concatenate([a[...].astype(f32), b[...].astype(f32)]).astype(bf16)
+
+    pl.when(core == 0)(lambda: join(inputs, got_in))
+    pl.when(core == 1)(lambda: join(got_grad, out_grad))
+
+
+def make_pair(at, *parts):
+    return call(
+        pair_kernel, at, parts, [fixed(24, 1536)] * 4, fixed(48, 1536), shape(48, 1536), (1,), 0
     )
 
 
@@ -318,11 +315,10 @@
     at = jnp.stack([core, me]).astype(jnp.int32)
     fore = core == 0
 
-    mine = jnp.where(fore, inputs, out_grad)
-    got = swap_cores(jnp.where(fore, out_grad, inputs))
-    got, send_in, send_out = barrier((got, w_in, w_out))
+    got_in, got_grad = swap_cores(inputs), swap_cores(out_grad)
+    got_in, got_grad, send_in, send_out = barrier((got_in, got_grad, w_in, w_out))
     in_par, out_par = swap_cores(send_in), swap_cores(send_out)
-    pair = make_pair(at, mine, got)
+    pair = make_pair(at, inputs, out_grad, got_in, got_grad)
     row = jnp.concatenate([pair] + [first_axis(pair, by) for by in steps])
     row, late = barrier((row, at))
     blocks = [row] + [second_axis(row, by) for by in steps]

time: 146 us -> 150 us (1.027)
  local copies, waits for them, and re-layouts: 3.71 us -> 9.62 us
    unnamed x12 -> x30, local copies, waits for them, and re-layouts: 3.49 us -> 8.35 us
    ppermute x16, waiting for transfers between devices: 15.1 us -> 13.4 us  [along_z(): lax.ppermute(array, 'col', [(z, (z + by) % ring) for z in range(ring)])]
    ppermute x7 -> x8, waiting for transfers between devices: 3.47 us -> 4.06 us  [swap_cores(): return lax.ppermute(array, 'row', [(r, r ^ 1) for r in range(32)])]
    ppermute x7 -> x8, starting transfers between devices: 18.6 us -> 18.4 us  [swap_cores(): return lax.ppermute(array, 'row', [(r, r ^ 1) for r in range(32)])]
  transfers between devices with their start and end apart: 35 -> 36, of which waited for: 19 -> 19; matrix products, arithmetic and copies ran while one was open for 1% -> 1% of each run, Pallas kernels for 26% -> 25%
where the time goes in v5:
time: 150 us; the launch traced here: 149 us
  starting transfers between devices  57.7 us (38%)
  Pallas kernels  40.1 us (27%)
  waiting for transfers between devices  37 us (25%)
  local copies, waits for them, and re-layouts  9.62 us (6%)
  other arithmetic  3.51 us (2%)
    pallas_call x12, Pallas kernels, call(): pl.pallas_call(kernel, grid_spec=pltpu.PrefetchScalarGridSpec(num_scalar_...  40.1 us
    ppermute x16, starting transfers between devices, along_z(): lax.ppermute(array, 'col', [(z, (z + by) % ring) for z in range(ring)])  24.9 us
    ppermute x8, starting transfers between devices, swap_cores(): return lax.ppermute(array, 'row', [(r, r ^ 1) for r in range(32)])  18.4 us
    ppermute x16, waiting for transfers between devices, along_z(): lax.ppermute(array, 'col', [(z, (z + by) % ring) for z in range(ring)])  13.4 us
    ppermute x6, waiting for transfers between devices, second_axis(): return lax.ppermute(array, 'row', pairs)  11.7 us
    unnamed x30, local copies, waits for them, and re-layouts  8.35 us
    ppermute x6, waiting for transfers between devices, first_axis(): return lax.ppermute(array, 'row', pairs)  7.81 us
    ppermute x6, starting transfers between devices, second_axis(): return lax.ppermute(array, 'row', pairs)  7.21 us
  transfers between devices with their start and end apart: 36, of which 19 were waited for; matrix products, arithmetic and copies ran while one was open for 1% of the time, Pallas kernels for 25%

profile of v5, /device:TPU:1, one launch (start us, length us, event | category | flops | bytes accessed | tf_op | source)
XLA Modules:
  0.0 149.0 jit_solution(1197955315015119336)
XLA Ops:
  0.6 3.3 %collective-permute-start = (bf16[24,1536]{1,0:T(8,128)(2,1)}, bf16[24,1536]{1,0:T(8,128)(2,1)S(1)}, u32[]{:S(2)}, u32[]{:S(2)}) collective-permute-start(bf16[24,1536]{1,0:T(8,128)(2,1)} %inputs.1), channel_id=1, source_target_pairs={{0,8},{8,0},{16,24},{24,16},{32,40},{40,32},{48,56},{56,48},{64,72... | collective-permute-start | bytes 221192 | tf_op jit(solution)/shard_map/ppermute | solution.py:44
  11.1 3.1 %collective-permute-done.4 = bf16[48,1536]{1,0:T(8,128)(2,1)S(1)} collective-permute-done((bf16[48,1536]{1,0:T(8,128)(2,1)S(1)}, bf16[48,1536]{1,0:T(8,128)(2,1)S(1)}, u32[]{:S(2)}, u32[]{:S(2)}) %collective-permute-start.4) | collective-permute-done | bytes 147488 | tf_op jit(solution)/shard_map/ppermute | solution.py:53
  23.3 5.0 %shard_map.76 = (bf16[1536,768]{1,0:T(8,128)(2,1)S(1)}, bf16[1536,768]{1,0:T(8,128)(2,1)S(1)}, bf16[768,1536]{1,0:T(8,128)(2,1)S(1)}, bf16[768,1536]{1,0:T(8,128)(2,1)S(1)}) custom-call(s32[2]{0:T(128)S(1)} %pad_add_fusion.at, bf16[1536,768]{1,0:T(8,128)(2,1)S(1)} %copy-done.5, bf16[1536,768]{1,0:T(8,128)(2,1)S(1)} %collective-permute-done.5.in_par, ...), custom_call_target="tpu_custom_call" | custom-call | bytes 8388608 | tf_op jit(solution)/shard_map/pallas_call | solution.py:76
  28.3 3.5 %collective-permute-done.8.a2 = bf16[192,1536]{1,0:T(8,128)(2,1)S(1)} collective-permute-done((bf16[192,1536]{1,0:T(8,128)(2,1)S(1)}, bf16[192,1536]{1,0:T(8,128)(2,1)S(1)}, u32[]{:S(2)}, u32[]{:S(2)}) %collective-permute-start.8) | collective-permute-done | bytes 589856 | tf_op jit(solution)/shard_map/ppermute | solution.py:62
  33.3 3.0 %shard_map.77 = (bf16[8,2,48,1536]{3,2,1,0:T(8,128)(2,1)S(1)}, bf16[96,768]{1,0:T(8,128)(2,1)S(1)}, bf16[96,768]{1,0:T(8,128)(2,1)S(1)}) custom-call(s32[2]{0:T(128)S(1)} %pad_add_fusion.at, bf16[1536,768]{1,0:T(8,128)(2,1)S(1)} %get-tuple-element.93.own, bf16[1536,768]{1,0:T(8,128)(2,1)S(1)} %get-tuple-element.94.par, ...), custom_call_target="tpu_custom_call" | custom-call | flops 452984832 | bytes 8388608 | tf_op jit(solution)/shard_map/pallas_call | solution.py:76
  38.0 4.0 %collective-permute-start.11 = (bf16[96,768]{1,0:T(8,128)(2,1)S(1)}, bf16[96,768]{1,0:T(8,128)(2,1)S(1)}, u32[]{:S(2)}, u32[]{:S(2)}) collective-permute-start(bf16[96,768]{1,0:T(8,128)(2,1)S(1)} %get-tuple-element.100), channel_id=1, source_target_pairs={{0,7},{1,0},{2,1},{3,2},{4,3},{5,4},{6,5},{7,6},{8,15},{9,8},{10,9... | collective-permute-start | bytes 442376 | tf_op jit(solution)/shard_map/ppermute | solution.py:66
  42.0 3.1 %shard_map.78 = (f32[96,1536]{1,0:T(8,128)S(1)}, f32[96,1536]{1,0:T(8,128)S(1)}) custom-call(s32[2]{0:T(128)S(1)} %pad_add_fusion.at, bf16[1536,768]{1,0:T(8,128)(2,1)S(1)} %get-tuple-element.93.own, bf16[1536,768]{1,0:T(8,128)(2,1)S(1)} %get-tuple-element.94.par, bf16[8,2,48,1536]{3,2,1,0:T(8,128)(2,1)S(1)} %get-tuple-element.154.refs_0_.refs_1_.refs_2_, ...), custom_call_target="tpu_custom_call" | custom-call | flops 905969664 | bytes 8388608 | tf_op jit(solution)/shard_map/pallas_call | solution.py:76
  45.3 2.7 %collective-permute-start.13 = (bf16[96,1536]{1,0:T(8,128)(2,1)S(1)}, bf16[96,1536]{1,0:T(8,128)(2,1)S(1)}, u32[]{:S(2)}, u32[]{:S(2)}) collective-permute-start(bf16[96,1536]{1,0:T(8,128)(2,1)S(1)} %get-tuple-element.109), channel_id=1, source_target_pairs={{0,7},{1,0},{2,1},{3,2},{4,3},{5,4},{6,5},{7,6},{8,15},{9,8},{10,9... | collective-permute-start | bytes 884744 | tf_op jit(solution)/shard_map/ppermute | solution.py:66
  48.0 3.8 %collective-permute-start.18 = (bf16[8,2,48,1536]{3,2,1,0:T(8,128)(2,1)S(1)}, bf16[8,2,48,1536]{3,2,1,0:T(8,128)(2,1)S(1)}, u32[]{:S(2)}, u32[]{:S(2)}) collective-permute-start(bf16[8,2,48,1536]{3,2,1,0:T(8,128)(2,1)S(1)} %get-tuple-element.154.refs_0_.refs_1_.refs_2_), channel_id=1, source_target_pairs={{0,8},{8,0},{16,24},{24,16},{32,40},{40,32},{48,56},{56,48},{64,72... | collective-permute-start | bytes 7077896 | tf_op jit(solution)/shard_map/ppermute | solution.py:44
  51.8 3.1 %shard_map.79 = (f32[96,1536]{1,0:T(8,128)S(1)}, f32[96,1536]{1,0:T(8,128)S(1)}) custom-call(s32[2]{0:T(128)S(1)} %pad_add_fusion.at, bf16[1536,768]{1,0:T(8,128)(2,1)S(1)} %get-tuple-element.93.own, bf16[1536,768]{1,0:T(8,128)(2,1)S(1)} %get-tuple-element.94.par, bf16[8,2,48,1536]{3,2,1,0:T(8,128)(2,1)S(1)} %get-tuple-element.154.refs_0_.refs_1_.refs_2_, ...), custom_call_target="tpu_custom_call" | custom-call | flops 905969664 | bytes 8388608 | tf_op jit(solution)/shard_map/pallas_call | solution.py:76
  55.3 2.7 %collective-permute-start.15 = (bf16[96,1536]{1,0:T(8,128)(2,1)S(1)}, bf16[96,1536]{1,0:T(8,128)(2,1)S(1)}, u32[]{:S(2)}, u32[]{:S(2)}) collective-permute-start(bf16[96,1536]{1,0:T(8,128)(2,1)S(1)} %fusion.33), channel_id=1, source_target_pairs={{0,7},{1,0},{2,1},{3,2},{4,3},{5,4},{6,5},{7,6},{8,15},{9,8},{10,9... | collective-permute-start | bytes 884744 | tf_op jit(solution)/shard_map/ppermute | solution.py:66
  57.9 3.6 %shard_map.80 = (f32[96,1536]{1,0:T(8,128)S(1)}, f32[96,1536]{1,0:T(8,128)S(1)}, f32[96,1536]{1,0:T(8,128)S(1)}) custom-call(s32[2]{0:T(128)S(1)} %pad_add_fusion.at, bf16[1536,768]{1,0:T(8,128)(2,1)S(1)} %get-tuple-element.93.own, bf16[1536,768]{1,0:T(8,128)(2,1)S(1)} %get-tuple-element.94.par, ...), custom_call_target="tpu_custom_call" | custom-call | flops 1358954496 | bytes 8388608 | tf_op jit(solution)/shard_map/pallas_call | solution.py:76
  67.0 4.1 %collective-permute-done.16 = bf16[96,1536]{1,0:T(8,128)(2,1)S(1)} collective-permute-done((bf16[96,1536]{1,0:T(8,128)(2,1)S(1)}, bf16[96,1536]{1,0:T(8,128)(2,1)S(1)}, u32[]{:S(2)}, u32[]{:S(2)}) %collective-permute-start.16) | collective-permute-done | bytes 294944 | tf_op jit(solution)/shard_map/ppermute | solution.py:66
  73.3 4.9 %collective-permute-start.19 = (f32[96,1536]{1,0:T(8,128)S(1)}, f32[96,1536]{1,0:T(8,128)}, u32[]{:S(2)}, u32[]{:S(2)}) collective-permute-start(f32[96,1536]{1,0:T(8,128)S(1)} %fusion.20), channel_id=1, source_target_pairs={{0,8},{8,0},{16,24},{24,16},{32,40},{40,32},{48,56},{56,48},{64,72... | collective-permute-start | bytes 1769480 | tf_op jit(solution)/shard_map/ppermute | solution.py:44
  85.9 2.6 %shard_map.81.refs_0_ = bf16[96,1536]{1,0:T(8,128)(2,1)S(1)} custom-call(s32[2]{0:T(128)S(1)} %pad_add_fusion.at, bf16[768,1536]{1,0:T(8,128)(2,1)S(1)} %copy-done.1, bf16[768,1536]{1,0:T(8,128)(2,1)S(1)} %copy-done.3, bf16[96,1536]{1,0:T(8,128)(2,1)S(1)} %fusion.43.refs_0_), custom_call_target="tpu_custom_call" | custom-call | flops 452984832 | bytes 8388608 | tf_op jit(solution)/shard_map/pallas_call | solution.py:76
  93.8 3.0 %shard_map.82 = (bf16[96,1536]{1,0:T(8,128)(2,1)S(1)}, bf16[96,1536]{1,0:T(8,128)(2,1)S(1)}) custom-call(s32[2]{0:T(128)S(1)} %pad_add_fusion.at, bf16[768,1536]{1,0:T(8,128)(2,1)S(1)} %copy-done.1, bf16[768,1536]{1,0:T(8,128)(2,1)S(1)} %copy-done.4, bf16[96,1536]{1,0:T(8,128)(2,1)S(1)} %collective-permute-done.21.refs_0_, ...), custom_call_target="tpu_custom_call" | custom-call | flops 905969664 | bytes 8388608 | tf_op jit(solution)/shard_map/pallas_call | solution.py:76
  96.8 2.8 %collective-permute-done.22.refs_1_ = bf16[96,1536]{1,0:T(8,128)(2,1)S(1)} collective-permute-done((bf16[96,1536]{1,0:T(8,128)(2,1)S(1)}, bf16[96,1536]{1,0:T(8,128)(2,1)S(1)}, u32[]{:S(2)}, u32[]{:S(2)}) %collective-permute-start.22) | collective-permute-done | bytes 294944 | tf_op jit(solution)/shard_map/ppermute | solution.py:66
  102.3 3.0 %shard_map.83 = (bf16[96,1536]{1,0:T(8,128)(2,1)S(1)}, bf16[96,1536]{1,0:T(8,128)(2,1)S(1)}) custom-call(s32[2]{0:T(128)S(1)} %pad_add_fusion.at, bf16[768,1536]{1,0:T(8,128)(2,1)S(1)} %copy-done.1, bf16[768,1536]{1,0:T(8,128)(2,1)S(1)} %copy-done.4, bf16[96,1536]{1,0:T(8,128)(2,1)S(1)} %collective-permute-done.23.refs_0_, ...), custom_call_target="tpu_custom_call" | custom-call | flops 905969664 | bytes 8388608 | tf_op jit(solution)/shard_map/pallas_call | solution.py:76
  110.1 3.0 %shard_map.84 = (bf16[96,1536]{1,0:T(8,128)(2,1)S(1)}, bf16[96,1536]{1,0:T(8,128)(2,1)S(1)}) custom-call(s32[2]{0:T(128)S(1)} %pad_add_fusion.at, bf16[768,1536]{1,0:T(8,128)(2,1)S(1)} %copy-done.1, bf16[768,1536]{1,0:T(8,128)(2,1)S(1)} %copy-done.4, bf16[96,1536]{1,0:T(8,128)(2,1)S(1)} %collective-permute-done.25.refs_0_, ...), custom_call_target="tpu_custom_call" | custom-call | flops 905969664 | bytes 8388608 | tf_op jit(solution)/shard_map/pallas_call | solution.py:76
  113.2 4.0 %collective-permute-start.28 = (bf16[768,768]{1,0:T(8,128)(2,1)S(1)}, bf16[768,768]{1,0:T(8,128)(2,1)S(1)}, u32[]{:S(2)}, u32[]{:S(2)}) collective-permute-start(bf16[768,768]{1,0:T(8,128)(2,1)S(1)} %get-tuple-element.171), channel_id=1, source_target_pairs={{0,8},{8,0},{16,24},{24,16},{32,40},{40,32},{48,56},{56,48},{64,72... | collective-permute-start | bytes 3538952 | tf_op jit(solution)/shard_map/ppermute | solution.py:44
  117.2 3.4 %shard_map.85 = bf16[4,4,48,1536]{3,2,1,0:T(8,128)(2,1)S(1)} custom-call(s32[2]{0:T(128)S(1)} %pad_add_fusion.at, bf16[768,1536]{1,0:T(8,128)(2,1)S(1)} %copy-done.1, bf16[768,1536]{1,0:T(8,128)(2,1)S(1)} %copy-done.4, bf16[96,768]{1,0:T(8,128)(2,1)S(1)} %collective-permute-done.26.b_own, bf16[96,768]{1,0:T(8,128)(2,1)S(1)} %collective-permute-done.27.b_par, ...), custom_call_target="tpu_custom_call" | custom-call | flops 452984832 | bytes 8388608 | tf_op jit(solution)/shard_map/pallas_call | solution.py:76
  123.9 6.9 %shard_map.86 = (bf16[1536,768]{1,0:T(8,128)(2,1)}, bf16[768,1536]{1,0:T(8,128)(2,1)}) custom-call(s32[2]{0:T(128)S(1)} %pad_add_fusion.at, bf16[768,1536]{1,0:T(8,128)(2,1)S(1)} %bitcast.27, bf16[768,1536]{1,0:T(8,128)(2,1)S(1)} %bitcast.28, bf16[768,768]{1,0:T(8,128)(2,1)S(1)} %get-tuple-element.170.b_own, bf16[768,768]{1,0:T(8,128)(2,1)S(1)} %collective-permute-done.28.b_oth), custom_call_target="tpu_custom_call" | custom-call | flops 3623878656 | bytes 8388608 | tf_op jit(solution)/shard_map/pallas_call | solution.py:76
  131.4 6.3 %collective-permute-done.30 = bf16[4,48,1536]{2,1,0:T(8,128)(2,1)S(1)} collective-permute-done((bf16[4,48,1536]{2,1,0:T(8,128)(2,1)S(1)}, bf16[4,48,1536]{2,1,0:T(8,128)(2,1)S(1)}, u32[]{:S(2)}, u32[]{:S(2)}) %collective-permute-start.30) | collective-permute-done | bytes 589856 | tf_op jit(solution)/shard_map/ppermute | solution.py:62
  138.3 2.7 %collective-permute-start.33 = (bf16[48,1536]{1,0:T(8,128)(2,1)S(1)}, bf16[48,1536]{1,0:T(8,128)(2,1)S(1)}, u32[]{:S(2)}, u32[]{:S(2)}) collective-permute-start(bf16[48,1536]{1,0:T(8,128)(2,1)S(1)} %get-tuple-element.167), channel_id=1, source_target_pairs={{0,64},{8,24},{16,80},{24,40},{32,96},{40,56},{48,112},{56,8},{64,... | collective-permute-start | bytes 442376 | tf_op jit(solution)/shard_map/ppermute | solution.py:53
  (109 shorter events, 60.5 us)
Async XLA Ops:
  5.4 14.5 %collective-permute-start.5 = (bf16[1536,768]{1,0:T(8,128)(2,1)}, bf16[1536,768]{1,0:T(8,128)(2,1)S(1)}, u32[]{:S(2)}, u32[]{:S(2)}) collective-permute-start(bf16[1536,768]{1,0:T(8,128)(2,1)} %in_own.1), channel_id=1, source_target_pairs={{0,8},{8,0},{16,24},{24,16},{32,40},{40,32},{48,56},{56,48},{64,72... | collective-permute-start | bytes 7077896 | tf_op jit(solution)/shard_map/ppermute | solution.py:44
  5.6 14.3 %collective-permute-start.6 = (bf16[768,1536]{1,0:T(8,128)(2,1)}, bf16[768,1536]{1,0:T(8,128)(2,1)}, u32[]{:S(2)}, u32[]{:S(2)}) collective-permute-start(bf16[768,1536]{1,0:T(8,128)(2,1)} %out_own.1), channel_id=1, source_target_pairs={{0,8},{8,0},{16,24},{24,16},{32,40},{40,32},{48,56},{56,48},{64,72... | collective-permute-start | bytes 7077896 | tf_op jit(solution)/shard_map/ppermute | solution.py:44
  15.9 12.4 %collective-permute-start.7 = (bf16[192,1536]{1,0:T(8,128)(2,1)S(1)}, bf16[192,1536]{1,0:T(8,128)(2,1)S(1)}, u32[]{:S(2)}, u32[]{:S(2)}) collective-permute-start(bf16[192,1536]{1,0:T(8,128)(2,1)S(1)} %pad_maximum_fusion.a0), channel_id=1, source_target_pairs={{0,16},{8,72},{16,32},{24,88},{32,48},{40,104},{48,0},{56,120},{64... | collective-permute-start | bytes 1769480 | tf_op jit(solution)/shard_map/ppermute | solution.py:62
  16.9 14.9 %collective-permute-start.8 = (bf16[192,1536]{1,0:T(8,128)(2,1)S(1)}, bf16[192,1536]{1,0:T(8,128)(2,1)S(1)}, u32[]{:S(2)}, u32[]{:S(2)}) collective-permute-start(bf16[192,1536]{1,0:T(8,128)(2,1)S(1)} %pad_maximum_fusion.a0), channel_id=1, source_target_pairs={{0,48},{8,200},{16,0},{24,216},{32,16},{40,232},{48,32},{56,248},{... | collective-permute-start | bytes 1769480 | tf_op jit(solution)/shard_map/ppermute | solution.py:62
  18.7 14.6 %collective-permute-start.9 = (bf16[192,1536]{1,0:T(8,128)(2,1)S(1)}, bf16[192,1536]{1,0:T(8,128)(2,1)S(1)}, u32[]{:S(2)}, u32[]{:S(2)}) collective-permute-start(bf16[192,1536]{1,0:T(8,128)(2,1)S(1)} %pad_maximum_fusion.a0), channel_id=1, source_target_pairs={{0,32},{8,136},{16,48},{24,152},{32,0},{40,168},{48,16},{56,184},{... | collective-permute-start | bytes 1769480 | tf_op jit(solution)/shard_map/ppermute | solution.py:62
  36.2 8.9 %collective-permute-start.10 = (bf16[96,768]{1,0:T(8,128)(2,1)S(1)}, bf16[96,768]{1,0:T(8,128)(2,1)S(1)}, u32[]{:S(2)}, u32[]{:S(2)}) collective-permute-start(bf16[96,768]{1,0:T(8,128)(2,1)S(1)} %get-tuple-element.99), channel_id=1, source_target_pairs={{0,1},{1,2},{2,3},{3,4},{4,5},{5,6},{6,7},{7,0},{8,9},{9,10},{10,1... | collective-permute-start | bytes 442376 | tf_op jit(solution)/shard_map/ppermute | solution.py:66
  38.0 7.2 %collective-permute-start.11 = (bf16[96,768]{1,0:T(8,128)(2,1)S(1)}, bf16[96,768]{1,0:T(8,128)(2,1)S(1)}, u32[]{:S(2)}, u32[]{:S(2)}) collective-permute-start(bf16[96,768]{1,0:T(8,128)(2,1)S(1)} %get-tuple-element.100), channel_id=1, source_target_pairs={{0,7},{1,0},{2,1},{3,2},{4,3},{5,4},{6,5},{7,6},{8,15},{9,8},{10,9... | collective-permute-start | bytes 442376 | tf_op jit(solution)/shard_map/ppermute | solution.py:66
  45.2 9.7 %collective-permute-start.12 = (bf16[96,1536]{1,0:T(8,128)(2,1)S(1)}, bf16[96,1536]{1,0:T(8,128)(2,1)S(1)}, u32[]{:S(2)}, u32[]{:S(2)}) collective-permute-start(bf16[96,1536]{1,0:T(8,128)(2,1)S(1)} %get-tuple-element.108), channel_id=1, source_target_pairs={{0,1},{1,2},{2,3},{3,4},{4,5},{5,6},{6,7},{7,0},{8,9},{9,10},{10,1... | collective-permute-start | bytes 884744 | tf_op jit(solution)/shard_map/ppermute | solution.py:66
  45.3 9.6 %collective-permute-start.13 = (bf16[96,1536]{1,0:T(8,128)(2,1)S(1)}, bf16[96,1536]{1,0:T(8,128)(2,1)S(1)}, u32[]{:S(2)}, u32[]{:S(2)}) collective-permute-start(bf16[96,1536]{1,0:T(8,128)(2,1)S(1)} %get-tuple-element.109), channel_id=1, source_target_pairs={{0,7},{1,0},{2,1},{3,2},{4,3},{5,4},{6,5},{7,6},{8,15},{9,8},{10,9... | collective-permute-start | bytes 884744 | tf_op jit(solution)/shard_map/ppermute | solution.py:66
  48.0 23.8 %collective-permute-start.18 = (bf16[8,2,48,1536]{3,2,1,0:T(8,128)(2,1)S(1)}, bf16[8,2,48,1536]{3,2,1,0:T(8,128)(2,1)S(1)}, u32[]{:S(2)}, u32[]{:S(2)}) collective-permute-start(bf16[8,2,48,1536]{3,2,1,0:T(8,128)(2,1)S(1)} %get-tuple-element.154.refs_0_.refs_1_.refs_2_), channel_id=1, source_target_pairs={{0,8},{8,0},{16,24},{24,16},{32,40},{40,32},{48,56},{56,48},{64,72... | collective-permute-start | bytes 7077896 | tf_op jit(solution)/shard_map/ppermute | solution.py:44
  55.2 8.3 %collective-permute-start.14 = (bf16[96,1536]{1,0:T(8,128)(2,1)S(1)}, bf16[96,1536]{1,0:T(8,128)(2,1)S(1)}, u32[]{:S(2)}, u32[]{:S(2)}) collective-permute-start(bf16[96,1536]{1,0:T(8,128)(2,1)S(1)} %fusion.32), channel_id=1, source_target_pairs={{0,1},{1,2},{2,3},{3,4},{4,5},{5,6},{6,7},{7,0},{8,9},{9,10},{10,1... | collective-permute-start | bytes 884744 | tf_op jit(solution)/shard_map/ppermute | solution.py:66
  55.3 8.2 %collective-permute-start.15 = (bf16[96,1536]{1,0:T(8,128)(2,1)S(1)}, bf16[96,1536]{1,0:T(8,128)(2,1)S(1)}, u32[]{:S(2)}, u32[]{:S(2)}) collective-permute-start(bf16[96,1536]{1,0:T(8,128)(2,1)S(1)} %fusion.33), channel_id=1, source_target_pairs={{0,7},{1,0},{2,1},{3,2},{4,3},{5,4},{6,5},{7,6},{8,15},{9,8},{10,9... | collective-permute-start | bytes 884744 | tf_op jit(solution)/shard_map/ppermute | solution.py:66
  64.3 6.9 %collective-permute-start.16 = (bf16[96,1536]{1,0:T(8,128)(2,1)S(1)}, bf16[96,1536]{1,0:T(8,128)(2,1)S(1)}, u32[]{:S(2)}, u32[]{:S(2)}) collective-permute-start(bf16[96,1536]{1,0:T(8,128)(2,1)S(1)} %fusion.34), channel_id=1, source_target_pairs={{0,1},{1,2},{2,3},{3,4},{4,5},{5,6},{6,7},{7,0},{8,9},{9,10},{10,1... | collective-permute-start | bytes 884744 | tf_op jit(solution)/shard_map/ppermute | solution.py:66
  81.5 9.5 %collective-permute-start.20 = (bf16[96,1536]{1,0:T(8,128)(2,1)S(1)}, bf16[96,1536]{1,0:T(8,128)(2,1)S(1)}, u32[]{:S(2)}, u32[]{:S(2)}) collective-permute-start(bf16[96,1536]{1,0:T(8,128)(2,1)S(1)} %fusion.43.refs_0_), channel_id=1, source_target_pairs={{0,1},{1,2},{2,3},{3,4},{4,5},{5,6},{6,7},{7,0},{8,9},{9,10},{10,1... | collective-permute-start | bytes 884744 | tf_op jit(solution)/shard_map/ppermute | solution.py:66
  82.6 8.5 %collective-permute-start.21 = (bf16[96,1536]{1,0:T(8,128)(2,1)S(1)}, bf16[96,1536]{1,0:T(8,128)(2,1)S(1)}, u32[]{:S(2)}, u32[]{:S(2)}) collective-permute-start(bf16[96,1536]{1,0:T(8,128)(2,1)S(1)} %fusion.43.refs_0_), channel_id=1, source_target_pairs={{0,7},{1,0},{2,1},{3,2},{4,3},{5,4},{6,5},{7,6},{8,15},{9,8},{10,9... | collective-permute-start | bytes 884744 | tf_op jit(solution)/shard_map/ppermute | solution.py:66
  91.1 8.5 %collective-permute-start.22 = (bf16[96,1536]{1,0:T(8,128)(2,1)S(1)}, bf16[96,1536]{1,0:T(8,128)(2,1)S(1)}, u32[]{:S(2)}, u32[]{:S(2)}) collective-permute-start(bf16[96,1536]{1,0:T(8,128)(2,1)S(1)} %collective-permute-done.20.refs_1_), channel_id=1, source_target_pairs={{0,1},{1,2},{2,3},{3,4},{4,5},{5,6},{6,7},{7,0},{8,9},{9,10},{10,1... | collective-permute-start | bytes 884744 | tf_op jit(solution)/shard_map/ppermute | solution.py:66
  92.3 7.4 %collective-permute-start.23 = (bf16[96,1536]{1,0:T(8,128)(2,1)S(1)}, bf16[96,1536]{1,0:T(8,128)(2,1)S(1)}, u32[]{:S(2)}, u32[]{:S(2)}) collective-permute-start(bf16[96,1536]{1,0:T(8,128)(2,1)S(1)} %collective-permute-done.21.refs_0_), channel_id=1, source_target_pairs={{0,7},{1,0},{2,1},{3,2},{4,3},{5,4},{6,5},{7,6},{8,15},{9,8},{10,9... | collective-permute-start | bytes 884744 | tf_op jit(solution)/shard_map/ppermute | solution.py:66
  99.6 7.6 %collective-permute-start.24 = (bf16[96,1536]{1,0:T(8,128)(2,1)S(1)}, bf16[96,1536]{1,0:T(8,128)(2,1)S(1)}, u32[]{:S(2)}, u32[]{:S(2)}) collective-permute-start(bf16[96,1536]{1,0:T(8,128)(2,1)S(1)} %collective-permute-done.22.refs_1_), channel_id=1, source_target_pairs={{0,1},{1,2},{2,3},{3,4},{4,5},{5,6},{6,7},{7,0},{8,9},{9,10},{10,1... | collective-permute-start | bytes 884744 | tf_op jit(solution)/shard_map/ppermute | solution.py:66
  100.2 7.1 %collective-permute-start.25 = (bf16[96,1536]{1,0:T(8,128)(2,1)S(1)}, bf16[96,1536]{1,0:T(8,128)(2,1)S(1)}, u32[]{:S(2)}, u32[]{:S(2)}) collective-permute-start(bf16[96,1536]{1,0:T(8,128)(2,1)S(1)} %collective-permute-done.23.refs_0_), channel_id=1, source_target_pairs={{0,7},{1,0},{2,1},{3,2},{4,3},{5,4},{6,5},{7,6},{8,15},{9,8},{10,9... | collective-permute-start | bytes 884744 | tf_op jit(solution)/shard_map/ppermute | solution.py:66
  113.2 7.3 %collective-permute-start.28 = (bf16[768,768]{1,0:T(8,128)(2,1)S(1)}, bf16[768,768]{1,0:T(8,128)(2,1)S(1)}, u32[]{:S(2)}, u32[]{:S(2)}) collective-permute-start(bf16[768,768]{1,0:T(8,128)(2,1)S(1)} %get-tuple-element.171), channel_id=1, source_target_pairs={{0,8},{8,0},{16,24},{24,16},{32,40},{40,32},{48,56},{56,48},{64,72... | collective-permute-start | bytes 3538952 | tf_op jit(solution)/shard_map/ppermute | solution.py:44
  120.7 10.7 %collective-permute-start.31 = (bf16[4,48,1536]{2,1,0:T(8,128)(2,1)S(1)}, bf16[4,48,1536]{2,1,0:T(8,128)(2,1)S(1)}, u32[]{:S(2)}, u32[]{:S(2)}) collective-permute-start(bf16[4,48,1536]{2,1,0:T(8,128)(2,1)S(1)} %get-tuple-element.163), channel_id=1, source_target_pairs={{0,32},{8,136},{16,48},{24,152},{32,0},{40,168},{48,16},{56,184},{... | collective-permute-start | bytes 1769480 | tf_op jit(solution)/shard_map/ppermute | solution.py:62
  121.2 16.4 %collective-permute-start.30 = (bf16[4,48,1536]{2,1,0:T(8,128)(2,1)S(1)}, bf16[4,48,1536]{2,1,0:T(8,128)(2,1)S(1)}, u32[]{:S(2)}, u32[]{:S(2)}) collective-permute-start(bf16[4,48,1536]{2,1,0:T(8,128)(2,1)S(1)} %get-tuple-element.164), channel_id=1, source_target_pairs={{0,16},{8,72},{16,32},{24,88},{32,48},{40,104},{48,0},{56,120},{64... | collective-permute-start | bytes 1769480 | tf_op jit(solution)/shard_map/ppermute | solution.py:62
  122.1 15.6 %collective-permute-start.29 = (bf16[4,48,1536]{2,1,0:T(8,128)(2,1)S(1)}, bf16[4,48,1536]{2,1,0:T(8,128)(2,1)S(1)}, u32[]{:S(2)}, u32[]{:S(2)}) collective-permute-start(bf16[4,48,1536]{2,1,0:T(8,128)(2,1)S(1)} %get-tuple-element.162), channel_id=1, source_target_pairs={{0,48},{8,200},{16,0},{24,216},{32,16},{40,232},{48,32},{56,248},{... | collective-permute-start | bytes 1769480 | tf_op jit(solution)/shard_map/ppermute | solution.py:62
  138.3 7.2 %collective-permute-start.33 = (bf16[48,1536]{1,0:T(8,128)(2,1)S(1)}, bf16[48,1536]{1,0:T(8,128)(2,1)S(1)}, u32[]{:S(2)}, u32[]{:S(2)}) collective-permute-start(bf16[48,1536]{1,0:T(8,128)(2,1)S(1)} %get-tuple-element.167), channel_id=1, source_target_pairs={{0,64},{8,24},{16,80},{24,40},{32,96},{40,56},{48,112},{56,8},{64,... | collective-permute-start | bytes 442376 | tf_op jit(solution)/shard_map/ppermute | solution.py:53
  (23 other events, 100.9 us)
